TPU v7x, 512 devices: a whole 4x8x8 slice. The times are simulated.
512 devices in a mesh: tile: 64 (over z, x, core), lev: 8 (over y).
Axes of the slice: x: 4, y: 8, z: 8, core: 2. Of those that a mesh axis runs over, the one named last changes fastest.
Arguments:
- adj_in: bfloat16 [4, 32, 524288], P(None, 'lev', 'tile'), may hold values from -6 to 6
- helm_coef: float32 [32, 524288], P('lev', 'tile'), may hold values from 0.25 to 4
- geo_coef: float32 [32], P('lev'), may hold values from 0.03 to 0.3
- dest_tile: int32 [4096, 1], P('tile'), may hold values from 0 to 63, as said below
- src_window: int32 [4096], P('tile'), may hold values from 0 to 31
- src_cell: int32 [12, 524288], P(None, 'tile'), may hold values from 0 to 255
- interp_w: bfloat16 [12, 524288], P(None, 'tile'), may hold values from 0.019897461 to 0.5
Outputs:
- adj_out: float32 [4, 32, 524288], P(None, 'lev', 'tile')
Inputs may be any that keep to these rules, and one draw needn't show every extreme that they name: `dest_tile`: block b of tile t names t or a tile at most 3 away on either side. Exactly 32 of the 64 blocks of every tile name the tile itself; of the others, at most 16 name any one tile, and in every tile exactly 16 name some one other tile.
All inputs are finite; a program needn't handle non-finite values.
Results may differ from a plain program's by a relative error of at most 0.002.
Values may be sent and summed in bfloat16 or wider, within the bound.
No kernel may reach another device: no remote copies, remote signals or barrier semaphores. Data moves between devices by JAX's collectives and lax.ppermute only.
A program may use at most 64 MiB of HBM per device.

v0:
```python
import jax
import jax.numpy as jnp
from jax import lax
from jax.sharding import PartitionSpec as P

NLON = 4096
BLK = 128
WIN = 256
SWEEPS = 4
REACH = 3
HOME = 32
OFFCAP = 16


def shortened(shard):

    def short(part):
        return part.astype(jnp.bfloat16) if part.dtype == jnp.float32 else part

    return jax.tree.map(short, shard)


def extended(shard, sides, width):
    for axis, dim in sides:
        peers, length = (lax.axis_size(axis), shard.shape[dim])
        up = [(i, (i + 1) % peers) for i in range(peers - 1)]
        down = [(j, i) for i, j in up]
        last = lax.slice_in_dim(shard, length - width, length, axis=dim)
        first = lax.slice_in_dim(shard, 0, width, axis=dim)
        before = lax.ppermute(last, axis, up)
        after = lax.ppermute(first, axis, down)
        shard = jnp.concatenate([before, shard, after], axis=dim)
    return shard


def prefix(shard, axis, join, neutral):
    place = lax.axis_index(axis)
    gathered = lax.all_gather(
        shard.astype(jnp.bfloat16 if shard.dtype == jnp.float32 else shard.dtype), axis
    )
    state = jnp.zeros_like(shard) + jnp.asarray(neutral, shard.dtype)

    def one(lap, state):
        return join(state, lax.dynamic_index_in_dim(gathered, lap, 0, False).astype(shard.dtype))

    return lax.fori_loop(0, place, one, state)


def shifted_2(shard, axis, by):
    peers = lax.axis_size(axis)
    pairs = [(i, i + by) for i in range(peers) if 0 <= i + by < peers]
    return lax.ppermute(shard, axis, pairs)


def neighbours(padded, level_count, row_count, row_len):
    layout = padded.reshape(level_count, row_count + 2, row_len)
    centre_rows = layout[:, 1:-1]
    summed = (
        layout[:, :-2]
        + layout[:, 2:]
        + jnp.roll(centre_rows, 1, axis=2)
        + jnp.roll(centre_rows, -1, axis=2)
    )
    return summed.reshape(level_count, row_count * row_len)


def add_pair(earlier, later):
    return earlier + later


def select_blocks(stacked, routes, group, count):
    block_count = stacked.shape[1]
    hits = (routes == group).astype(jnp.float32)
    earlier_blocks = (
        lax.broadcasted_iota(jnp.int32, (block_count, block_count), 1)
        < lax.broadcasted_iota(jnp.int32, (block_count, block_count), 0)
    ).astype(jnp.float32)
    ranking = jnp.dot(earlier_blocks, hits).astype(jnp.int32)
    chosen = (lax.iota(jnp.int32, count)[:, None] == ranking[None, :]) & (routes[None, :] == group)
    selection = chosen.astype(jnp.bfloat16)
    packed = jnp.einsum("sb,xbc->sxc", selection, stacked, preferred_element_type=jnp.float32)
    return packed.astype(jnp.bfloat16)


def spread_slots(slots, row_width, stencil, window_len, windows):

    def spread_one(item):
        value_rows = item[:row_width]
        weight_item = item[row_width : row_width + stencil]
        indices = item[row_width + stencil : row_width + 2 * stencil].astype(jnp.int32)
        matches = indices[:, :, None] == lax.broadcasted_iota(jnp.int32, (1, 1, window_len), 2)
        spread_matrix = jnp.sum(
            jnp.where(matches, weight_item.astype(jnp.float32)[:, :, None], 0.0), axis=0
        )
        contribution = jnp.dot(
            value_rows.astype(jnp.float32), spread_matrix, precision=lax.Precision.HIGHEST
        )
        window = item[row_width + 2 * stencil, 0].astype(jnp.int32)
        placement = (lax.iota(jnp.int32, windows) == window).astype(jnp.float32)
        return (contribution, placement)

    contribution, placement = lax.map(spread_one, slots, batch_size=16)
    return jnp.einsum("sw,srj->rwj", placement, contribution, precision=lax.Precision.HIGHEST)


def body(adj_in, helm_coef, geo_coef, dest_tile, src_window, src_cell, interp_w):
    field_count, levels_here, cells_here = adj_in.shape
    stencil = src_cell.shape[0]
    row_len = NLON
    row_count = cells_here // row_len
    block_len = BLK
    window_len = WIN
    windows = cells_here // window_len
    block_count = cells_here // block_len
    row_width = field_count * levels_here
    right_side = adj_in[0].astype(jnp.float32)
    diagonal = 1.0 + 4.0 * helm_coef
    solved = right_side / diagonal
    for sweep in range(SWEEPS):
        shifted = extended(shortened(helm_coef * solved), (("tile", 1),), row_len)
        solved = (right_side + neighbours(shifted, levels_here, row_count, row_len)) / diagonal
    triangle = (
        lax.broadcasted_iota(jnp.int32, (levels_here, levels_here), 0)
        >= lax.broadcasted_iota(jnp.int32, (levels_here, levels_here), 1)
    ).astype(jnp.float32)
    local_sums = jnp.dot(triangle, solved, precision=lax.Precision.HIGHEST)
    column_totals = local_sums[-1]
    above = prefix(column_totals, "lev", add_pair, jnp.zeros_like(column_totals))
    geo_term = geo_coef[:, None] * (local_sums + above[None, :])
    tile_here = lax.axis_index("tile")
    routes = dest_tile[:, 0] - tile_here + REACH
    outgoing = jnp.concatenate([solved.astype(jnp.bfloat16)[None], adj_in[1:]], axis=0)
    outgoing = outgoing.reshape(row_width, block_count, block_len)
    weight_rows = interp_w.reshape(stencil, block_count, block_len)
    cell_rows = src_cell.astype(jnp.bfloat16).reshape(stencil, block_count, block_len)
    window_row = jnp.broadcast_to(
        src_window.astype(jnp.bfloat16)[None, :, None], (1, block_count, block_len)
    )
    route_row = jnp.broadcast_to(
        routes.astype(jnp.bfloat16)[None, :, None], (1, block_count, block_len)
    )
    stacked = jnp.concatenate([outgoing, weight_rows, cell_rows, window_row, route_row], axis=0)
    route_position = row_width + 2 * stencil + 1
    home_slots = select_blocks(stacked, routes, REACH, HOME)
    transported = spread_slots(home_slots, row_width, stencil, window_len, windows)
    for step_by in list(range(-REACH, 0)) + list(range(1, REACH + 1)):
        group = REACH + step_by
        arrived_band = shifted_2(stacked, "tile", step_by)
        arrived_routes = arrived_band[route_position, :, 0].astype(jnp.int32)
        arrived = select_blocks(arrived_band, arrived_routes, group, OFFCAP)
        transported = transported + spread_slots(arrived, row_width, stencil, window_len, windows)
    transported = transported.reshape(field_count, levels_here, cells_here)
    return transported.at[2].add(geo_term)


def solution(mesh):
    placed = (
        P(None, "lev", "tile"),
        P("lev", "tile"),
        P("lev"),
        P("tile", None),
        P("tile"),
        P(None, "tile"),
        P(None, "tile"),
    )
    return jax.shard_map(
        body, mesh=mesh, in_specs=placed, out_specs=P(None, "lev", "tile"), check_vma=False
    )
```

profile of v0, /device:TPU:256, one launch (start us, length us, event | category | flops | bytes accessed | tf_op | source)
XLA Modules:
  0.0 197.0 jit_solution(5729699392194219045)
XLA Ops:
  1.1 3.2 %collective-permute-start.1 = (bf16[4,4096]{1,0:T(4,128)(2,1)S(1)}, bf16[4,4096]{1,0:T(4,128)(2,1)S(1)}, u32[]{:S(2)}, u32[]{:S(2)}) collective-permute-start(bf16[4,4096]{1,0:T(4,128)(2,1)S(1)} %get-tuple-element.213), channel_id=1, source_target_pairs={{8,0},{16,8},{24,16},{32,24},{40,32},{48,40},{56,48},{64,56},{72,6... | collective-permute-start | bytes 98312 | tf_op jit(solution)/shard_map/ppermute | solution.py:31
  6.2 6.6 %collective-permute-done = bf16[4,4096]{1,0:T(4,128)(2,1)S(1)} collective-permute-done((bf16[4,4096]{1,0:T(4,128)(2,1)S(1)}, bf16[4,4096]{1,0:T(4,128)(2,1)S(1)}, u32[]{:S(2)}, u32[]{:S(2)}) %collective-permute-start) | collective-permute-done | bytes 32800 | tf_op jit(solution)/shard_map/ppermute | solution.py:30
  16.5 2.4 %collective-permute-start.2 = (bf16[4,4096]{1,0:T(4,128)(2,1)S(1)}, bf16[4,4096]{1,0:T(4,128)(2,1)S(1)}, u32[]{:S(2)}, u32[]{:S(2)}) collective-permute-start(bf16[4,4096]{1,0:T(4,128)(2,1)S(1)} %get-tuple-element.210), channel_id=1, source_target_pairs={{0,8},{8,16},{16,24},{24,32},{32,40},{40,48},{48,56},{56,64},{64,7... | collective-permute-start | bytes 98312 | tf_op jit(solution)/shard_map/ppermute | solution.py:30
  19.0 6.1 %collective-permute-done.2 = bf16[4,4096]{1,0:T(4,128)(2,1)S(1)} collective-permute-done((bf16[4,4096]{1,0:T(4,128)(2,1)S(1)}, bf16[4,4096]{1,0:T(4,128)(2,1)S(1)}, u32[]{:S(2)}, u32[]{:S(2)}) %collective-permute-start.2) | collective-permute-done | bytes 32800 | tf_op jit(solution)/shard_map/ppermute | solution.py:30
  26.0 1.9 collective-permute-start.5
  27.9 2.4 %collective-permute-start.4 = (bf16[4,4096]{1,0:T(4,128)(2,1)S(1)}, bf16[4,4096]{1,0:T(4,128)(2,1)S(1)}, u32[]{:S(2)}, u32[]{:S(2)}) collective-permute-start(bf16[4,4096]{1,0:T(4,128)(2,1)S(1)} %get-tuple-element.208), channel_id=1, source_target_pairs={{0,8},{8,16},{16,24},{24,32},{32,40},{40,48},{48,56},{56,64},{64,7... | collective-permute-start | bytes 98312 | tf_op jit(solution)/shard_map/ppermute | solution.py:30
  30.5 6.0 %collective-permute-done.4 = bf16[4,4096]{1,0:T(4,128)(2,1)S(1)} collective-permute-done((bf16[4,4096]{1,0:T(4,128)(2,1)S(1)}, bf16[4,4096]{1,0:T(4,128)(2,1)S(1)}, u32[]{:S(2)}, u32[]{:S(2)}) %collective-permute-start.4) | collective-permute-done | bytes 32800 | tf_op jit(solution)/shard_map/ppermute | solution.py:30
  39.3 2.4 %collective-permute-start.6 = (bf16[4,4096]{1,0:T(4,128)(2,1)S(1)}, bf16[4,4096]{1,0:T(4,128)(2,1)S(1)}, u32[]{:S(2)}, u32[]{:S(2)}) collective-permute-start(bf16[4,4096]{1,0:T(4,128)(2,1)S(1)} %get-tuple-element.206), channel_id=1, source_target_pairs={{0,8},{8,16},{16,24},{24,32},{32,40},{40,48},{48,56},{56,64},{64,7... | collective-permute-start | bytes 98312 | tf_op jit(solution)/shard_map/ppermute | solution.py:30
  41.9 5.9 %collective-permute-done.6 = bf16[4,4096]{1,0:T(4,128)(2,1)S(1)} collective-permute-done((bf16[4,4096]{1,0:T(4,128)(2,1)S(1)}, bf16[4,4096]{1,0:T(4,128)(2,1)S(1)}, u32[]{:S(2)}, u32[]{:S(2)}) %collective-permute-start.6) | collective-permute-done | bytes 32800 | tf_op jit(solution)/shard_map/ppermute | solution.py:30
  50.0 1.9 collective-permute-start.8
  55.8 2.4 %collective-permute-start.11 = (bf16[42,64,128]{2,1,0:T(8,128)(2,1)S(1)}, bf16[42,64,128]{2,1,0:T(8,128)(2,1)}, u32[]{:S(2)}, u32[]{:S(2)}) collective-permute-start(bf16[42,64,128]{2,1,0:T(8,128)(2,1)S(1)} %constant_dynamic-update-slice_fusion), channel_id=1, source_target_pairs={{0,8},{8,16},{16,24},{24,32},{32,40},{40,48},{48,56},{56,64},{64,7... | collective-permute-start | bytes 2064392 | tf_op jit(solution)/shard_map/ppermute | solution.py:52
  58.2 3.9 %collective-permute-start.12 = (bf16[42,64,128]{2,1,0:T(8,128)(2,1)S(1)}, bf16[42,64,128]{2,1,0:T(8,128)(2,1)S(1)}, u32[]{:S(2)}, u32[]{:S(2)}) collective-permute-start(bf16[42,64,128]{2,1,0:T(8,128)(2,1)S(1)} %constant_dynamic-update-slice_fusion), channel_id=1, source_target_pairs={{0,16},{8,24},{16,32},{24,40},{32,48},{40,56},{48,64},{56,72},{64,... | collective-permute-start | bytes 2064392 | tf_op jit(solution)/shard_map/ppermute | solution.py:52
  62.4 21.1 %while.5 = (s32[]{:T(128)}, f32[2,16,16,256]{3,1,0,2:T(8,128)}, f32[2,16,32]{2,1,0:T(8,128)S(1)}, bf16[2,16,42,128]{3,1,0,2:T(8,128)(2,1)S(1)}, s32[]{:T(128)}) while((s32[]{:T(128)}, f32[2,16,16,256]{3,1,0,2:T(8,128)}, f32[2,16,32]{2,1,0:T(8,128)S(1)}, bf16[2,16,42,128]{3,1,0,2:T(8,128)(2,1)S(1)}, s32[]{:T(128)}) %tuple.80), condition=%wide.region_2.3_spmd, body=%wide.region_0.2_spmd.sunk | while | flops 119063568 | bytes 10429161 | solution.py:102
  62.6 8.6 %select_reduce_fusion.8 = f32[16,128,256]{2,1,0:T(8,128)S(1)} fusion(f32[16,12,128]{2,1,0:T(8,128)S(1)} %get-tuple-element.263, s32[16,12,128]{2,1,0:T(8,128)S(1)} %get-tuple-element.264), kind=kLoop, calls=%fused_computation.1.clone.1 | loop fusion | flops 18350080 | bytes 2293760 | tf_op jit(solution)/shard_map/while/body/eval_jaxpr/vmap()/reduce_sum | solution.py:92
  73.1 8.6 %select_reduce_fusion.8 = f32[16,128,256]{2,1,0:T(8,128)S(1)} fusion(f32[16,12,128]{2,1,0:T(8,128)S(1)} %get-tuple-element.263, s32[16,12,128]{2,1,0:T(8,128)S(1)} %get-tuple-element.264), kind=kLoop, calls=%fused_computation.1.clone.1 | loop fusion | flops 18350080 | bytes 2293760 | tf_op jit(solution)/shard_map/while/body/eval_jaxpr/vmap()/reduce_sum | solution.py:92
  83.8 26.4 %all-gather = bf16[8,1,8192]{2,1,0:T(2,128)(2,1)S(1)} all-gather(bf16[1,1,8192]{2,1,0:T(2,128)(2,1)S(1)} %fusion.48), channel_id=1, replica_groups=mesh['tile'=64,'lev'=8] {'lev'}, dimensions={0}, use_global_device_ids=true | all-gather | bytes 147456 | tf_op jit(solution)/shard_map/all_gather | solution.py:38
  112.1 1.9 collective-permute-start.13
  120.9 12.6 %collective-permute-done.13 = bf16[42,64,128]{2,1,0:T(8,128)(2,1)S(1)} collective-permute-done((bf16[42,64,128]{2,1,0:T(8,128)(2,1)S(1)}, bf16[42,64,128]{2,1,0:T(8,128)(2,1)S(1)}, u32[]{:S(2)}, u32[]{:S(2)}) %collective-permute-start.13) | collective-permute-done | bytes 688160 | tf_op jit(solution)/shard_map/ppermute | solution.py:52
  134.8 8.8 %select_reduce_fusion.6 = f32[16,128,256]{2,1,0:T(8,128)S(1)} fusion(f32[16,12,128]{2,1,0:T(8,128)S(1)} %copy.91, s32[16,12,128]{2,1,0:T(8,128)S(1)} %copy.90), kind=kLoop, calls=%fused_computation.24 | loop fusion | flops 18350080 | bytes 2293760 | tf_op jit(solution)/shard_map/while/body/eval_jaxpr/vmap()/reduce_sum | solution.py:92
  144.4 8.6 %select_reduce_fusion.5 = f32[16,128,256]{2,1,0:T(8,128)S(1)} fusion(f32[16,12,128]{2,1,0:T(8,128)S(1)} %copy.95, s32[16,12,128]{2,1,0:T(8,128)S(1)} %copy.94), kind=kLoop, calls=%fused_computation.22 | loop fusion | flops 18350080 | bytes 2293760 | tf_op jit(solution)/shard_map/while/body/eval_jaxpr/vmap()/reduce_sum | solution.py:92
  153.9 8.6 %select_reduce_fusion.4 = f32[16,128,256]{2,1,0:T(8,128)S(1)} fusion(f32[16,12,128]{2,1,0:T(8,128)S(1)} %copy.99, s32[16,12,128]{2,1,0:T(8,128)S(1)} %copy.98), kind=kLoop, calls=%fused_computation.20 | loop fusion | flops 18350080 | bytes 2293760 | tf_op jit(solution)/shard_map/while/body/eval_jaxpr/vmap()/reduce_sum | solution.py:92
  163.3 8.6 %select_reduce_fusion.3 = f32[16,128,256]{2,1,0:T(8,128)S(1)} fusion(f32[16,12,128]{2,1,0:T(8,128)S(1)} %copy.103, s32[16,12,128]{2,1,0:T(8,128)S(1)} %copy.102), kind=kLoop, calls=%fused_computation.18 | loop fusion | flops 18350080 | bytes 2293760 | tf_op jit(solution)/shard_map/while/body/eval_jaxpr/vmap()/reduce_sum | solution.py:92
  172.8 8.6 %select_reduce_fusion.2 = f32[16,128,256]{2,1,0:T(8,128)S(1)} fusion(f32[16,12,128]{2,1,0:T(8,128)S(1)} %copy.107, s32[16,12,128]{2,1,0:T(8,128)S(1)} %copy.106), kind=kLoop, calls=%fused_computation.16 | loop fusion | flops 18350080 | bytes 2293760 | tf_op jit(solution)/shard_map/while/body/eval_jaxpr/vmap()/reduce_sum | solution.py:92
  182.3 8.6 %select_reduce_fusion.1 = f32[16,128,256]{2,1,0:T(8,128)S(1)} fusion(f32[16,12,128]{2,1,0:T(8,128)S(1)} %copy.111, s32[16,12,128]{2,1,0:T(8,128)S(1)} %copy.110), kind=kLoop, calls=%fused_computation.14 | loop fusion | flops 18350080 | bytes 2293760 | tf_op jit(solution)/shard_map/while/body/eval_jaxpr/vmap()/reduce_sum | solution.py:92
  (192 shorter events, 40.4 us)
Async XLA Ops:
  0.0 25.9 %copy-start.1 = (bf16[4,4,8192]{2,1,0:T(4,128)(2,1)S(1)}, bf16[4,4,8192]{2,1,0:T(4,128)(2,1)}, u32[]{:S(2)}) copy-start(bf16[4,4,8192]{2,1,0:T(4,128)(2,1)} %param.13) | copy-start | bytes 786436
  0.0 25.9 %copy-start = (f32[4,8192]{1,0:T(4,128)S(1)}, f32[4,8192]{1,0:T(4,128)}, u32[]{:S(2)}) copy-start(f32[4,8192]{1,0:T(4,128)} %param.14) | copy-start | bytes 393220
  0.0 19.0 %copy-start.14 = (s32[64,1]{0,1:T(1,128)S(1)}, s32[64,1]{0,1:T(1,128)}, u32[]{:S(2)}) copy-start(s32[64,1]{0,1:T(1,128)} %param.16) | copy-start | bytes 772
  1.1 5.1 %collective-permute-start.1 = (bf16[4,4096]{1,0:T(4,128)(2,1)S(1)}, bf16[4,4096]{1,0:T(4,128)(2,1)S(1)}, u32[]{:S(2)}, u32[]{:S(2)}) collective-permute-start(bf16[4,4096]{1,0:T(4,128)(2,1)S(1)} %get-tuple-element.213), channel_id=1, source_target_pairs={{8,0},{16,8},{24,16},{32,24},{40,32},{48,40},{56,48},{64,56},{72,6... | collective-permute-start | bytes 98312 | tf_op jit(solution)/shard_map/ppermute | solution.py:31
  4.3 8.6 %collective-permute-start = (bf16[4,4096]{1,0:T(4,128)(2,1)S(1)}, bf16[4,4096]{1,0:T(4,128)(2,1)S(1)}, u32[]{:S(2)}, u32[]{:S(2)}) collective-permute-start(bf16[4,4096]{1,0:T(4,128)(2,1)S(1)} %get-tuple-element.212), channel_id=1, source_target_pairs={{0,8},{8,16},{16,24},{24,32},{32,40},{40,48},{48,56},{56,64},{64,7... | collective-permute-start | bytes 98312 | tf_op jit(solution)/shard_map/ppermute | solution.py:30
  14.6 4.4 %collective-permute-start.3 = (bf16[4,4096]{1,0:T(4,128)(2,1)S(1)}, bf16[4,4096]{1,0:T(4,128)(2,1)S(1)}, u32[]{:S(2)}, u32[]{:S(2)}) collective-permute-start(bf16[4,4096]{1,0:T(4,128)(2,1)S(1)} %get-tuple-element.211), channel_id=1, source_target_pairs={{8,0},{16,8},{24,16},{32,24},{40,32},{48,40},{56,48},{64,56},{72,6... | collective-permute-start | bytes 98312 | tf_op jit(solution)/shard_map/ppermute | solution.py:31
  16.5 8.6 %collective-permute-start.2 = (bf16[4,4096]{1,0:T(4,128)(2,1)S(1)}, bf16[4,4096]{1,0:T(4,128)(2,1)S(1)}, u32[]{:S(2)}, u32[]{:S(2)}) collective-permute-start(bf16[4,4096]{1,0:T(4,128)(2,1)S(1)} %get-tuple-element.210), channel_id=1, source_target_pairs={{0,8},{8,16},{16,24},{24,32},{32,40},{40,48},{48,56},{56,64},{64,7... | collective-permute-start | bytes 98312 | tf_op jit(solution)/shard_map/ppermute | solution.py:30
  25.2 16.6 %copy-start.12 = (bf16[12,8192]{1,0:T(8,128)(2,1)S(1)}, bf16[12,8192]{1,0:T(8,128)(2,1)}, u32[]{:S(2)}) copy-start(bf16[12,8192]{1,0:T(8,128)(2,1)} %param.19) | copy-start | bytes 589828
  25.5 16.3 %copy-start.8 = (s32[12,8192]{1,0:T(8,128)S(1)}, s32[12,8192]{1,0:T(8,128)}, u32[]{:S(2)}) copy-start(s32[12,8192]{1,0:T(8,128)} %param.18) | copy-start | bytes 1179652
  26.0 4.5 %collective-permute-start.5 = (bf16[4,4096]{1,0:T(4,128)(2,1)S(1)}, bf16[4,4096]{1,0:T(4,128)(2,1)S(1)}, u32[]{:S(2)}, u32[]{:S(2)}) collective-permute-start(bf16[4,4096]{1,0:T(4,128)(2,1)S(1)} %get-tuple-element.209), channel_id=1, source_target_pairs={{8,0},{16,8},{24,16},{32,24},{40,32},{48,40},{56,48},{64,56},{72,6... | collective-permute-start | bytes 98312 | tf_op jit(solution)/shard_map/ppermute | solution.py:31
  27.9 8.6 %collective-permute-start.4 = (bf16[4,4096]{1,0:T(4,128)(2,1)S(1)}, bf16[4,4096]{1,0:T(4,128)(2,1)S(1)}, u32[]{:S(2)}, u32[]{:S(2)}) collective-permute-start(bf16[4,4096]{1,0:T(4,128)(2,1)S(1)} %get-tuple-element.208), channel_id=1, source_target_pairs={{0,8},{8,16},{16,24},{24,32},{32,40},{40,48},{48,56},{56,64},{64,7... | collective-permute-start | bytes 98312 | tf_op jit(solution)/shard_map/ppermute | solution.py:30
  30.5 11.4 %copy-start.15 = (s32[64]{0:T(128)S(1)}, s32[64]{0:T(128)}, u32[]{:S(2)}) copy-start(s32[64]{0:T(128)} %param.17) | copy-start | bytes 772
  37.3 4.6 %collective-permute-start.7 = (bf16[4,4096]{1,0:T(4,128)(2,1)S(1)}, bf16[4,4096]{1,0:T(4,128)(2,1)S(1)}, u32[]{:S(2)}, u32[]{:S(2)}) collective-permute-start(bf16[4,4096]{1,0:T(4,128)(2,1)S(1)} %get-tuple-element.207), channel_id=1, source_target_pairs={{8,0},{16,8},{24,16},{32,24},{40,32},{48,40},{56,48},{64,56},{72,6... | collective-permute-start | bytes 98312 | tf_op jit(solution)/shard_map/ppermute | solution.py:31
  39.3 8.6 %collective-permute-start.6 = (bf16[4,4096]{1,0:T(4,128)(2,1)S(1)}, bf16[4,4096]{1,0:T(4,128)(2,1)S(1)}, u32[]{:S(2)}, u32[]{:S(2)}) collective-permute-start(bf16[4,4096]{1,0:T(4,128)(2,1)S(1)} %get-tuple-element.206), channel_id=1, source_target_pairs={{0,8},{8,16},{16,24},{24,32},{32,40},{40,48},{48,56},{56,64},{64,7... | collective-permute-start | bytes 98312 | tf_op jit(solution)/shard_map/ppermute | solution.py:30
  50.0 62.1 %collective-permute-start.8 = (bf16[42,64,128]{2,1,0:T(8,128)(2,1)S(1)}, bf16[42,64,128]{2,1,0:T(8,128)(2,1)}, u32[]{:S(2)}, u32[]{:S(2)}) collective-permute-start(bf16[42,64,128]{2,1,0:T(8,128)(2,1)S(1)} %constant_dynamic-update-slice_fusion), channel_id=1, source_target_pairs={{24,0},{32,8},{40,16},{48,24},{56,32},{64,40},{72,48},{80,56},{88,... | collective-permute-start | bytes 2064392 | tf_op jit(solution)/shard_map/ppermute | solution.py:52
  52.0 64.5 %collective-permute-start.9 = (bf16[42,64,128]{2,1,0:T(8,128)(2,1)S(1)}, bf16[42,64,128]{2,1,0:T(8,128)(2,1)S(1)}, u32[]{:S(2)}, u32[]{:S(2)}) collective-permute-start(bf16[42,64,128]{2,1,0:T(8,128)(2,1)S(1)} %constant_dynamic-update-slice_fusion), channel_id=1, source_target_pairs={{16,0},{24,8},{32,16},{40,24},{48,32},{56,40},{64,48},{72,56},{80,... | collective-permute-start | bytes 2064392 | tf_op jit(solution)/shard_map/ppermute | solution.py:52
  53.9 62.7 %collective-permute-start.10 = (bf16[42,64,128]{2,1,0:T(8,128)(2,1)S(1)}, bf16[42,64,128]{2,1,0:T(8,128)(2,1)S(1)}, u32[]{:S(2)}, u32[]{:S(2)}) collective-permute-start(bf16[42,64,128]{2,1,0:T(8,128)(2,1)S(1)} %constant_dynamic-update-slice_fusion), channel_id=1, source_target_pairs={{8,0},{16,8},{24,16},{32,24},{40,32},{48,40},{56,48},{64,56},{72,6... | collective-permute-start | bytes 2064392 | tf_op jit(solution)/shard_map/ppermute | solution.py:52
  55.8 61.2 %collective-permute-start.11 = (bf16[42,64,128]{2,1,0:T(8,128)(2,1)S(1)}, bf16[42,64,128]{2,1,0:T(8,128)(2,1)}, u32[]{:S(2)}, u32[]{:S(2)}) collective-permute-start(bf16[42,64,128]{2,1,0:T(8,128)(2,1)S(1)} %constant_dynamic-update-slice_fusion), channel_id=1, source_target_pairs={{0,8},{8,16},{16,24},{24,32},{32,40},{40,48},{48,56},{56,64},{64,7... | collective-permute-start | bytes 2064392 | tf_op jit(solution)/shard_map/ppermute | solution.py:52
  58.2 62.0 %collective-permute-start.12 = (bf16[42,64,128]{2,1,0:T(8,128)(2,1)S(1)}, bf16[42,64,128]{2,1,0:T(8,128)(2,1)S(1)}, u32[]{:S(2)}, u32[]{:S(2)}) collective-permute-start(bf16[42,64,128]{2,1,0:T(8,128)(2,1)S(1)} %constant_dynamic-update-slice_fusion), channel_id=1, source_target_pairs={{0,16},{8,24},{16,32},{24,40},{32,48},{40,56},{48,64},{56,72},{64,... | collective-permute-start | bytes 2064392 | tf_op jit(solution)/shard_map/ppermute | solution.py:52
  62.4 21.1 %copy-start.11 = (f32[4,8192]{1,0:T(4,128)S(1)}, f32[4,8192]{1,0:T(4,128)}, u32[]{:S(2)}) copy-start(f32[4,8192]{1,0:T(4,128)} %get-tuple-element.175) | copy-start | bytes 393220
  112.1 21.4 %collective-permute-start.13 = (bf16[42,64,128]{2,1,0:T(8,128)(2,1)S(1)}, bf16[42,64,128]{2,1,0:T(8,128)(2,1)S(1)}, u32[]{:S(2)}, u32[]{:S(2)}) collective-permute-start(bf16[42,64,128]{2,1,0:T(8,128)(2,1)S(1)} %constant_dynamic-update-slice_fusion), channel_id=1, source_target_pairs={{0,24},{8,32},{16,40},{24,48},{32,56},{40,64},{48,72},{56,80},{64,... | collective-permute-start | bytes 2064392 | tf_op jit(solution)/shard_map/ppermute | solution.py:52
  118.4 15.6 %copy-start.3 = (bf16[16,42,128]{2,0,1:T(8,128)(2,1)}, bf16[16,42,128]{2,0,1:T(8,128)(2,1)S(1)}, u32[]{:S(2)}) copy-start(bf16[16,42,128]{2,0,1:T(8,128)(2,1)S(1)} %convolution_convert_fusion.4) | copy-start | bytes 516100
  119.8 14.3 %copy-start.4 = (bf16[16,42,128]{2,0,1:T(8,128)(2,1)}, bf16[16,42,128]{2,0,1:T(8,128)(2,1)S(1)}, u32[]{:S(2)}) copy-start(bf16[16,42,128]{2,0,1:T(8,128)(2,1)S(1)} %convolution_convert_fusion.3) | copy-start | bytes 516100
  120.7 13.9 %copy-start.6 = (bf16[16,42,128]{2,0,1:T(8,128)(2,1)}, bf16[16,42,128]{2,0,1:T(8,128)(2,1)S(1)}, u32[]{:S(2)}) copy-start(bf16[16,42,128]{2,0,1:T(8,128)(2,1)S(1)} %convolution_convert_fusion.2) | copy-start | bytes 516100
  (15 other events, 103.4 us)
where the time goes:
time: 198 us; the launch traced here: 197 us
  other arithmetic  78 us (39%)
  waiting for transfers between devices  37.3 us (19%)
  starting transfers between devices  32.1 us (16%)
  blocking collectives  26.4 us (13%)
  matrix products  16.4 us (8%)
  local copies, waits for them, and re-layouts  5.52 us (3%)
    reduce_sum x8, other arithmetic, spread_one(): jnp.sum(jnp.where(matches, weight_item.astype(jnp.float32)[:, :, None], 0...  69.2 us
    all_gather x1, blocking collectives, prefix(): lax.all_gather(shard.astype(jnp.bfloat16 if shard.dtype == jnp.float32 el...  26.4 us
    ppermute x4, waiting for transfers between devices, extended(): before = lax.ppermute(last, axis, up)  24.6 us
    ppermute x6, starting transfers between devices, shifted_2(): return lax.ppermute(shard, axis, pairs)  14 us
    ppermute x6, waiting for transfers between devices, shifted_2(): return lax.ppermute(shard, axis, pairs)  12.7 us
    ppermute x4, starting transfers between devices, extended(): before = lax.ppermute(last, axis, up)  9.14 us
    ppermute x4, starting transfers between devices, extended(): after = lax.ppermute(first, axis, down)  8.96 us
    dot_general x8, matrix products, spread_one(): jnp.dot(value_rows.astype(jnp.float32), spread_matrix, precision=lax.Prec...  6.47 us
  transfers between devices with their start and end apart: 14, of which 5 were waited for; matrix products, arithmetic and copies ran while one was open for 15% of the time, Pallas kernels for 0%

commit v1 on v0

v1 whole, which is shorter than its diff:
```python
import jax
import jax.numpy as jnp
from jax import lax
from jax.experimental import pallas as pl
from jax.experimental.pallas import tpu as pltpu
from jax.sharding import PartitionSpec as P

NLON = 4096
BLK = 128
WIN = 256
SWEEPS = 4
REACH = 3
HOME = 32
OFFCAP = 16

F32 = jnp.float32
BF16 = jnp.bfloat16
STEN = 12
NBLK = 64
CELLS = 8192
NWIN = CELLS // WIN
OFFSETS = (1, -1, 2, -2, 3, -3)
SLOTS = HOME + OFFCAP * len(OFFSETS)
BASES = {0: 0, **{by: HOME + OFFCAP * i for i, by in enumerate(OFFSETS)}}
HALO = NLON // BLK
ROUTE = 2 * STEN + 1
ENTRIES = 2 * SLOTS
UNROLL = 4
REMAINDER = 1e-6


def vmem():
    return pl.BlockSpec(memory_space=pltpu.VMEM)


def smem():
    return pl.BlockSpec(memory_space=pltpu.SMEM)


def hbm():
    return pl.BlockSpec(memory_space=pl.ANY)


def lanes(i):
    return slice(i * BLK, (i + 1) * BLK)


def call(kernel, outs, ins, scratch, cost, limit):
    return pl.pallas_call(
        kernel,
        out_shape=[jax.ShapeDtypeStruct(shape, dtype) for shape, dtype, _ in outs],
        out_specs=[spec for _, _, spec in outs],
        in_specs=ins,
        scratch_shapes=scratch,
        compiler_params=pltpu.CompilerParams(vmem_limit_bytes=limit << 20),
        cost_estimate=pl.CostEstimate(flops=cost * 1000000, bytes_accessed=cost * 3000000, transcendentals=0),
    )


def pack_kernel(me, dest, win, adj, helm, cell, weight, slots, a_home, b_home, *rest):
    parcels, (count, a_all, b_all) = rest[: len(OFFSETS)], rest[len(OFFSETS) :]
    for by in range(-REACH, REACH + 1):
        count[by + REACH] = BASES[by]
    a_all[...] = jnp.zeros_like(a_all)
    b_all[...] = jnp.zeros_like(b_all)
    for b in range(NBLK):
        route = dest[b] - me[0] + REACH
        slot = count[route]
        count[route] = slot + 1
        slots[b] = slot
        a_all[pl.ds(slot, STEN, stride=SLOTS), :] = weight[:, lanes(b)].astype(F32)
        a_all[pl.ds(STEN * SLOTS + slot, STEN, stride=SLOTS), :] = cell[:, lanes(b)].astype(F32)
        a_all[pl.ds(2 * STEN * SLOTS + slot, 1), :] = jnp.full((1, BLK), win[b] + 1, jnp.int32).astype(F32)
        b_all[slot] = jnp.concatenate([adj[f, :, lanes(b)].astype(F32) for f in range(4)], axis=0).astype(BF16)
    for r in range(ROUTE):
        a_home[r] = a_all[r * SLOTS : r * SLOTS + HOME, :].astype(BF16)
    b_home[...] = b_all[:HOME]
    for by, parcel in zip(OFFSETS, parcels):
        at = HALO if abs(by) < 3 else 0
        base = BASES[by]
        for r in range(ROUTE):
            parcel[at + r] = a_all[r * SLOTS + base : r * SLOTS + base + OFFCAP, :].astype(BF16)
        parcel[at + ROUTE : at + ROUTE + OFFCAP] = b_all[base : base + OFFCAP]
    for i in range(HALO):
        piece = jnp.concatenate(
            [
                adj[0, :, lanes(i)].astype(F32),
                adj[0, :, lanes(HALO + i)].astype(F32),
                helm[:, lanes(i)],
                helm[:, lanes(HALO + i)],
            ],
            axis=0,
        ).astype(BF16)
        for by, parcel in zip(OFFSETS, parcels):
            if abs(by) < 3:
                parcel[i] = piece


def solve_kernel(slots, adj, helm, n2, n1, s1, s2, local, totals, f_home, *rest):
    f_out, (halo, f_all, t_all, sems) = rest[: len(OFFSETS)], rest[len(OFFSETS) :]
    copies = []
    for i, parcel in enumerate((n2, n1, s1, s2)):
        copy = pltpu.make_async_copy(parcel.at[pl.ds(0, HALO)], halo.at[i], sems.at[i])
        copy.start()
        copies.append(copy)
    f_all[...] = jnp.zeros_like(f_all)
    for copy in copies:
        copy.wait()
    rhs, coef = [], []
    for band in range(5):
        if band == 2:
            rhs.append(jnp.concatenate([adj[0, :, :NLON].astype(F32), adj[0, :, NLON:].astype(F32)], axis=0))
            coef.append(jnp.concatenate([helm[:, :NLON], helm[:, NLON:]], axis=0))
        else:
            at = band - (band > 2)
            tiles = [halo[at, i].astype(F32) for i in range(HALO)]
            rhs.append(jnp.concatenate([t[:8] for t in tiles], axis=1))
            coef.append(jnp.concatenate([t[8:] for t in tiles], axis=1))
    scale = [1.0 / (1.0 + 4.0 * c) for c in coef]
    solved = [r * s for r, s in zip(rhs, scale)]
    upper = lax.broadcasted_iota(jnp.int32, (8, NLON), 0) < 4
    for wanted in ((0, 1, 2, 3, 4), (1, 2, 3), (1, 2, 3), (2,)):
        shifted = [c * s for c, s in zip(coef, solved)]
        turned = [pltpu.roll(p, 4, 0) for p in shifted]
        fresh = list(solved)
        for band in wanted:
            p = shifted[band]
            north = turned[max(band - 1, 0)]
            south = turned[min(band + 1, 4)]
            total = turned[band] + jnp.where(upper, north, south)
            total = total + pltpu.roll(p, 1, 1) + pltpu.roll(p, NLON - 1, 1)
            fresh[band] = (rhs[band] + total) * scale[band]
        solved = fresh
    mine = solved[2]
    for r in range(2):
        sums = mine[4 * r : 4 * r + 1]
        local[4 * r : 4 * r + 1, :] = sums
        for level in range(1, 4):
            sums = sums + mine[4 * r + level : 4 * r + level + 1]
            local[4 * r + level : 4 * r + level + 1, :] = sums
        for i in range(HALO):
            t_all[HALO * r + i : HALO * r + i + 1, :] = sums[:, lanes(i)]
            f_all[pl.ds(slots[HALO * r + i] * 4, 4), :] = mine[4 * r : 4 * r + 4, lanes(i)]
    totals_here = t_all[...].astype(BF16)
    for i in range(totals.shape[0]):
        totals[i] = totals_here
    f_home[...] = f_all[: HOME * 4].astype(BF16)
    for by, out in zip(OFFSETS, f_out):
        out[...] = f_all[BASES[by] * 4 : (BASES[by] + OFFCAP) * 4].astype(BF16)


def matrix_kernel(a_home, *rest):
    parcels = rest[: len(OFFSETS)]
    mats, entry_slot, entry_win, entry_count, a_in, cells, merged, meta, meta_s, sems, meta_sem = rest[len(OFFSETS) :]
    copies = []
    for i, (by, parcel) in enumerate(zip(OFFSETS, parcels)):
        at = HALO if abs(by) < 3 else 0
        copy = pltpu.make_async_copy(parcel.at[pl.ds(at, ROUTE)], a_in.at[i], sems.at[i])
        copy.start()
        copies.append(copy)

    lane = lax.broadcasted_iota(jnp.int32, (8, BLK), 1)
    row = lax.broadcasted_iota(jnp.int32, (8, BLK), 0)

    def merge(base, load):
        w = [load(k) for k in range(STEN)]
        c = [load(STEN + k) for k in range(STEN)]
        total = list(w)
        for k in range(STEN):
            for m in range(k):
                same = c[k] == c[m]
                total[k] = total[k] + jnp.where(same, w[m], 0.0)
                total[m] = total[m] + jnp.where(same, w[k], 0.0)
        lost = jnp.zeros((8, BLK), F32)
        held = jnp.zeros((8, BLK), F32)
        for k in range(STEN):
            high = total[k].astype(BF16).astype(F32)
            low = total[k] - high
            cells[k, base : base + 8, :] = c[k]
            merged[k, base : base + 8, :] = high
            merged[k, SLOTS + base : SLOTS + base + 8, :] = low
            lost = lost + low * low
            held = held + w[k] * w[k]
        more = jnp.sum(lost, axis=1, keepdims=True) > REMAINDER * jnp.sum(held, axis=1, keepdims=True)
        mark = load(2 * STEN)
        mark = jnp.where(mark > 0.0, mark + jnp.where(more, 64.0, 0.0), 0.0)
        return jnp.where(lane == row + base, mark, 0.0)

    marks = jnp.zeros((8, BLK), F32)
    for half in range(0, HOME, 16):
        pair = [a_home[r, half : half + 16, :].astype(F32) for r in range(ROUTE)]
        for part in (0, 8):
            marks = marks + merge(half + part, lambda r: pair[r][part : part + 8])
    for i, by in enumerate(OFFSETS):
        copies[i].wait()
        pair = [a_in[i, r].astype(F32) for r in range(ROUTE)]
        for part in (0, 8):
            marks = marks + merge(BASES[by] + part, lambda r: pair[r][part : part + 8])
    meta[...] = jnp.sum(marks, axis=0, keepdims=True).astype(jnp.int32)
    copy = pltpu.make_async_copy(meta, meta_s, meta_sem)
    copy.start()
    copy.wait()

    def enlist(i, n):
        for j in range(8):
            slot = i * 8 + j
            mark = meta_s[0, slot]
            window = (mark & 63) - 1
            entry_slot[n] = slot
            entry_win[n] = window
            n = n + (mark > 0).astype(jnp.int32)
            entry_slot[n] = slot + SLOTS
            entry_win[n] = window
            n = n + (mark >= 64).astype(jnp.int32)
        return n

    n = lax.fori_loop(0, SLOTS // 8, enlist, jnp.int32(0))
    entry_count[0] = n
    for j in range(UNROLL):
        entry_slot[n + j] = 0
        entry_win[n + j] = NWIN

    iota = lax.broadcasted_iota(jnp.int32, (16, BLK), 0).astype(F32)

    def build(i, carry):
        entry = entry_slot[i]
        slot = lax.rem(entry, SLOTS)
        c = [jnp.broadcast_to(cells[k, pl.ds(slot, 1), :], (16, BLK)).astype(BF16) for k in range(STEN)]
        w = [jnp.broadcast_to(merged[k, pl.ds(entry, 1), :], (16, BLK)).astype(BF16) for k in range(STEN)]
        for j in range(WIN // 16):
            here = (iota + 16.0 * j).astype(BF16)
            m = jnp.zeros((16, BLK), BF16)
            for k in range(STEN):
                m = jnp.where(c[k] == here, w[k], m)
            mats[i, 16 * j : 16 * j + 16, :] = m
        return carry

    lax.fori_loop(0, n, build, 0)


def spread_kernel(entry_slot, entry_win, entry_count, lev, geo, mats, b_home, f_home, local, above, *rest):
    parcels, f_in = rest[: len(OFFSETS)], rest[len(OFFSETS) : 2 * len(OFFSETS)]
    out, values, firsts, total, sems = rest[2 * len(OFFSETS) :]
    copies = []
    for i, (by, parcel) in enumerate(zip(OFFSETS, parcels)):
        at = (HALO if abs(by) < 3 else 0) + ROUTE
        copy = pltpu.make_async_copy(parcel.at[pl.ds(at, OFFCAP)], values.at[pl.ds(BASES[by], OFFCAP)], sems.at[i])
        copy.start()
        copies.append(copy)
    values[:HOME] = b_home[...]
    total[...] = jnp.zeros_like(total)
    firsts[: HOME * 4, :] = f_home[...].astype(F32)
    for by, part in zip(OFFSETS, f_in):
        firsts[BASES[by] * 4 : (BASES[by] + OFFCAP) * 4, :] = part[...].astype(F32)
    firsts[SLOTS * 4 :, :] = jnp.zeros((8, BLK), F32)
    for copy in copies:
        copy.wait()
    first_rows = lax.broadcasted_iota(jnp.int32, (8, BLK), 0) < 4

    def step(i, carry):
        parts = []
        for j in range(UNROLL):
            at = i * UNROLL + j
            slot = lax.rem(entry_slot[at], SLOTS)
            tile = values[slot].astype(F32)
            head = jnp.where(first_rows, firsts[pl.ds(slot * 4, 8), :], tile[:8])
            left = jnp.concatenate([head, tile[8:]], axis=0).astype(BF16)
            parts.append(
                lax.dot_general(left, mats[at], (((1,), (1,)), ((), ())), preferred_element_type=F32)
            )
        for j in range(UNROLL):
            start = pl.multiple_of(entry_win[i * UNROLL + j] * WIN, WIN)
            total[:, pl.ds(start, WIN)] += parts[j]
        return carry

    lax.fori_loop(0, (entry_count[0] + UNROLL - 1) // UNROLL, step, 0)

    sums = jnp.zeros((NBLK, BLK), F32)
    for peer in range(above.shape[0]):
        sums = sums + jnp.where(peer < lev[0], above[peer].astype(F32), 0.0)
    level = lax.broadcasted_iota(jnp.int32, (4, BLK), 0)
    factor = jnp.zeros((4, BLK), F32)
    for l in range(4):
        factor = jnp.where(level == l, geo[l], factor)
    for f in (0, 1, 3):
        out[f] = total[4 * f : 4 * f + 4, :CELLS]
    for b in range(NBLK):
        r = b // HALO
        term = factor * (local[4 * r : 4 * r + 4, lanes(b % HALO)] + sums[b : b + 1])
        out[2, :, lanes(b)] = total[8:12, lanes(b)] + term


def moved(parcel, by):
    peers = lax.axis_size("tile")
    return lax.ppermute(parcel, "tile", [(i, i + by) for i in range(peers) if 0 <= i + by < peers])


def body(adj_in, helm_coef, geo_coef, dest_tile, src_window, src_cell, interp_w):
    me = lax.axis_index("tile").astype(jnp.int32)[None]
    lev = lax.axis_index("lev").astype(jnp.int32)[None]
    peers = lax.axis_size("lev")
    directions = len(OFFSETS)

    def parcel_of(by):
        return (ROUTE + OFFCAP + (HALO if abs(by) < 3 else 0), 16, BLK)

    slots, a_home, b_home, *parcels = call(
        pack_kernel,
        [
            ((NBLK,), jnp.int32, smem()),
            ((ROUTE, HOME, BLK), BF16, vmem()),
            ((HOME, 16, BLK), BF16, vmem()),
        ]
        + [(parcel_of(by), BF16, vmem()) for by in OFFSETS],
        [smem()] * 3 + [vmem()] * 4,
        [
            pltpu.SMEM((2 * REACH + 1,), jnp.int32),
            pltpu.VMEM((ROUTE * SLOTS, BLK), F32),
            pltpu.VMEM((SLOTS, 16, BLK), BF16),
        ],
        1,
        32,
    )(me, dest_tile[:, 0], src_window, adj_in, helm_coef, src_cell, interp_w)
    arrived = [moved(parcel, by) for by, parcel in zip(OFFSETS, parcels)]
    arrived_from = dict(zip(OFFSETS, arrived))

    local, totals, f_home, *f_out = call(
        solve_kernel,
        [
            ((8, NLON), F32, vmem()),
            ((peers, NBLK, BLK), BF16, vmem()),
            ((HOME * 4, BLK), BF16, vmem()),
        ]
        + [((OFFCAP * 4, BLK), BF16, vmem())] * directions,
        [smem()] + [vmem()] * 2 + [hbm()] * 4,
        [
            pltpu.VMEM((4, HALO, 16, BLK), BF16),
            pltpu.VMEM((SLOTS * 4, BLK), F32),
            pltpu.VMEM((NBLK, BLK), F32),
            pltpu.SemaphoreType.DMA((4,)),
        ],
        2,
        32,
    )(slots, adj_in, helm_coef, *(arrived_from[by] for by in (2, 1, -1, -2)))
    above = lax.all_to_all(totals, "lev", 0, 0)
    f_in = [moved(part, by) for by, part in zip(OFFSETS, f_out)]

    mats, entry_slot, entry_win, entry_count = call(
        matrix_kernel,
        [
            ((ENTRIES, WIN, BLK), BF16, vmem()),
            ((ENTRIES + 8,), jnp.int32, smem()),
            ((ENTRIES + 8,), jnp.int32, smem()),
            ((1,), jnp.int32, smem()),
        ],
        [vmem()] + [hbm()] * directions,
        [
            pltpu.VMEM((directions, ROUTE, 16, BLK), BF16),
            pltpu.VMEM((STEN, SLOTS, BLK), F32),
            pltpu.VMEM((STEN, 2 * SLOTS, BLK), F32),
            pltpu.VMEM((1, BLK), jnp.int32),
            pltpu.SMEM((1, BLK), jnp.int32),
            pltpu.SemaphoreType.DMA((directions,)),
            pltpu.SemaphoreType.DMA,
        ],
        8,
        40,
    )(a_home, *arrived)

    return call(
        spread_kernel,
        [((4, 4, CELLS), F32, vmem())],
        [smem()] * 5 + [vmem()] * 5 + [hbm()] * directions + [vmem()] * directions,
        [
            pltpu.VMEM((SLOTS, 16, BLK), BF16),
            pltpu.VMEM((SLOTS * 4 + 8, BLK), F32),
            pltpu.VMEM((16, CELLS + WIN), F32),
            pltpu.SemaphoreType.DMA((directions,)),
        ],
        5,
        40,
    )(entry_slot, entry_win, entry_count, lev, geo_coef, mats, b_home, f_home, local, above, *arrived, *f_in)[0]


def solution(mesh):
    placed = (
        P(None, "lev", "tile"),
        P("lev", "tile"),
        P("lev"),
        P("tile", None),
        P("tile"),
        P(None, "tile"),
        P(None, "tile"),
    )
    return jax.shard_map(
        body, mesh=mesh, in_specs=placed, out_specs=P(None, "lev", "tile"), check_vma=False
    )
```

time: 198 us -> 105 us (0.53)
  the two profiles are of different devices: /device:TPU:256 before, /device:TPU:264 now
where the time goes in v1:
time: 105 us
  starting transfers between devices  62 us (59%)
  Pallas kernels  30.4 us (29%)
  local copies, waits for them, and re-layouts  7.66 us (7%)
  waiting for transfers between devices  4.27 us (4%)
    ppermute x12, starting transfers between devices, moved(): lax.ppermute(parcel, 'tile', [(i, i + by) for i in range(peers) if 0 <= i...  54.4 us
    pallas_call x1, Pallas kernels, body(): call(matrix_kernel, [((ENTRIES, WIN, BLK), BF16, vmem()), ((ENTRIES + 8,)...  14.2 us
    pallas_call x1, Pallas kernels, body(): call(spread_kernel, [((4, 4, CELLS), F32, vmem())], [smem()] * 5 + [vmem(...  11.1 us
    unnamed x18, local copies, waits for them, and re-layouts  7.66 us
    all_to_all x1, starting transfers between devices, body(): above = lax.all_to_all(totals, 'lev', 0, 0)  7.56 us
    ppermute x12, waiting for transfers between devices, moved(): lax.ppermute(parcel, 'tile', [(i, i + by) for i in range(peers) if 0 <= i...  4.27 us
    pallas_call x1, Pallas kernels, body(): call(solve_kernel, [((8, NLON), F32, vmem()), ((peers, NBLK, BLK), BF16,...  3.03 us
    pallas_call x1, Pallas kernels, body(): call(pack_kernel, [((NBLK,), jnp.int32, smem()), ((ROUTE, HOME, BLK), BF1...  2.12 us
  transfers between devices with their start and end apart: 13, of which 2 were waited for; matrix products, arithmetic and copies ran while one was open for 0% of the time, Pallas kernels for 14%

profile of v1, /device:TPU:264, one launch (start us, length us, event | category | flops | bytes accessed | tf_op | source)
XLA Modules:
  0.0 104.6 jit_solution(1336884176522454955)
XLA Ops:
  0.0 0.9 copy-done
  1.0 0.9 copy-done.2
  1.9 1.0 copy-done.4
  2.9 0.9 copy-done.5
  5.2 2.1 %shard_map.73 = (s32[64]{0:T(128)S(1)}, bf16[25,32,128]{2,1,0:T(8,128)(2,1)S(1)}, bf16[32,16,128]{2,1,0:T(8,128)(2,1)S(1)}, bf16[73,16,128]{2,1,0:T(8,128)(2,1)S...) custom-call(s32[1]{0:T(128)} %bitcast.me, ...), custom_call_target="tpu_custom_call" | custom-call | flops 1000000 | bytes 3000000 | tf_op jit(solution)/shard_map/pallas_call | solution.py:307
  7.3 1.9 %collective-permute-start = (bf16[73,16,128]{2,1,0:T(8,128)(2,1)S(1)}, bf16[73,16,128]{2,1,0:T(8,128)(2,1)S(1)}, u32[]{:S(2)}, u32[]{:S(2)}) collective-permute-start(bf16[73,16,128]{2,1,0:T(8,128)(2,1)S(1)} %get-tuple-element.28), channel_id=1, source_target_pairs={{0,8},{8,16},{16,24},{24,32},{32,40},{40,48},{48,56},{56,64},{64,7... | collective-permute-start | bytes 897032 | tf_op jit(solution)/shard_map/ppermute | solution.py:295
  9.2 7.0 %collective-permute-start.1 = (bf16[73,16,128]{2,1,0:T(8,128)(2,1)S(1)}, bf16[73,16,128]{2,1,0:T(8,128)(2,1)S(1)}, u32[]{:S(2)}, u32[]{:S(2)}) collective-permute-start(bf16[73,16,128]{2,1,0:T(8,128)(2,1)S(1)} %get-tuple-element.29), channel_id=1, source_target_pairs={{8,0},{16,8},{24,16},{32,24},{40,32},{48,40},{56,48},{64,56},{72,6... | collective-permute-start | bytes 897032 | tf_op jit(solution)/shard_map/ppermute | solution.py:295
  16.2 1.9 %collective-permute-start.2 = (bf16[73,16,128]{2,1,0:T(8,128)(2,1)S(1)}, bf16[73,16,128]{2,1,0:T(8,128)(2,1)S(1)}, u32[]{:S(2)}, u32[]{:S(2)}) collective-permute-start(bf16[73,16,128]{2,1,0:T(8,128)(2,1)S(1)} %get-tuple-element.30), channel_id=1, source_target_pairs={{0,16},{8,24},{16,32},{24,40},{32,48},{40,56},{48,64},{56,72},{64,... | collective-permute-start | bytes 897032 | tf_op jit(solution)/shard_map/ppermute | solution.py:295
  18.1 7.2 %collective-permute-start.3 = (bf16[73,16,128]{2,1,0:T(8,128)(2,1)S(1)}, bf16[73,16,128]{2,1,0:T(8,128)(2,1)S(1)}, u32[]{:S(2)}, u32[]{:S(2)}) collective-permute-start(bf16[73,16,128]{2,1,0:T(8,128)(2,1)S(1)} %get-tuple-element.31), channel_id=1, source_target_pairs={{16,0},{24,8},{32,16},{40,24},{48,32},{56,40},{64,48},{72,56},{80,... | collective-permute-start | bytes 897032 | tf_op jit(solution)/shard_map/ppermute | solution.py:295
  25.4 2.8 %collective-permute-done.2.rest_2_.n2 = bf16[73,16,128]{2,1,0:T(8,128)(2,1)S(1)} collective-permute-done((bf16[73,16,128]{2,1,0:T(8,128)(2,1)S(1)}, bf16[73,16,128]{2,1,0:T(8,128)(2,1)S(1)}, u32[]{:S(2)}, u32[]{:S(2)}) %collective-permute-start.2) | collective-permute-done | bytes 299040 | tf_op jit(solution)/shard_map/ppermute | solution.py:295
  28.2 1.5 %collective-permute-done.3.rest_3_.s2 = bf16[73,16,128]{2,1,0:T(8,128)(2,1)S(1)} collective-permute-done((bf16[73,16,128]{2,1,0:T(8,128)(2,1)S(1)}, bf16[73,16,128]{2,1,0:T(8,128)(2,1)S(1)}, u32[]{:S(2)}, u32[]{:S(2)}) %collective-permute-start.3) | collective-permute-done | bytes 299040 | tf_op jit(solution)/shard_map/ppermute | solution.py:295
  29.6 0.9 copy-done.1
  31.5 3.0 %shard_map.75 = (f32[8,4096]{1,0:T(8,128)S(1)}, bf16[8,64,128]{2,1,0:T(8,128)(2,1)}, bf16[128,128]{1,0:T(8,128)(2,1)S(1)}, bf16[64,128]{1,0:T(8,128)(2,1)S(1)}, ...) custom-call(s32[64]{0:T(128)S(1)} %get-tuple-element.39.slots, ...), custom_call_target="tpu_custom_call" | custom-call | flops 2000000 | bytes 6000000 | tf_op jit(solution)/shard_map/pallas_call | solution.py:327
  34.5 7.6 %all-to-all-start = ((bf16[8,64,128]{2,1,0:T(8,128)(2,1)}), bf16[8,64,128]{2,1,0:T(8,128)(2,1)S(1)}, u32[]{:S(2)}, u32[]{:S(2)}) async-start(bf16[8,64,128]{2,1,0:T(8,128)(2,1)} %get-tuple-element.42), calls=%async_computation | async-start | bytes 262144 | tf_op jit(solution)/shard_map/all_to_all | solution.py:345
  42.1 1.9 %collective-permute-start.4 = (bf16[41,16,128]{2,1,0:T(8,128)(2,1)S(1)}, bf16[41,16,128]{2,1,0:T(8,128)(2,1)S(1)}, u32[]{:S(2)}, u32[]{:S(2)}) collective-permute-start(bf16[41,16,128]{2,1,0:T(8,128)(2,1)S(1)} %get-tuple-element.32), channel_id=1, source_target_pairs={{0,24},{8,32},{16,40},{24,48},{32,56},{40,64},{48,72},{56,80},{64,... | collective-permute-start | bytes 503816 | tf_op jit(solution)/shard_map/ppermute | solution.py:295
  44.0 7.3 %collective-permute-start.5 = (bf16[41,16,128]{2,1,0:T(8,128)(2,1)S(1)}, bf16[41,16,128]{2,1,0:T(8,128)(2,1)S(1)}, u32[]{:S(2)}, u32[]{:S(2)}) collective-permute-start(bf16[41,16,128]{2,1,0:T(8,128)(2,1)S(1)} %get-tuple-element.33), channel_id=1, source_target_pairs={{24,0},{32,8},{40,16},{48,24},{56,32},{64,40},{72,48},{80,56},{88,... | collective-permute-start | bytes 503816 | tf_op jit(solution)/shard_map/ppermute | solution.py:295
  51.3 2.5 %collective-permute-start.6 = (bf16[64,128]{1,0:T(8,128)(2,1)S(1)}, bf16[64,128]{1,0:T(8,128)(2,1)S(1)}, u32[]{:S(2)}, u32[]{:S(2)}) collective-permute-start(bf16[64,128]{1,0:T(8,128)(2,1)S(1)} %get-tuple-element.43), channel_id=1, source_target_pairs={{0,8},{8,16},{16,24},{24,32},{32,40},{40,48},{48,56},{56,64},{64,7... | collective-permute-start | bytes 49160 | tf_op jit(solution)/shard_map/ppermute | solution.py:295
  53.7 6.4 %collective-permute-start.7 = (bf16[64,128]{1,0:T(8,128)(2,1)S(1)}, bf16[64,128]{1,0:T(8,128)(2,1)S(1)}, u32[]{:S(2)}, u32[]{:S(2)}) collective-permute-start(bf16[64,128]{1,0:T(8,128)(2,1)S(1)} %get-tuple-element.44), channel_id=1, source_target_pairs={{8,0},{16,8},{24,16},{32,24},{40,32},{48,40},{56,48},{64,56},{72,6... | collective-permute-start | bytes 49160 | tf_op jit(solution)/shard_map/ppermute | solution.py:295
  60.2 1.9 %collective-permute-start.8 = (bf16[64,128]{1,0:T(8,128)(2,1)S(1)}, bf16[64,128]{1,0:T(8,128)(2,1)S(1)}, u32[]{:S(2)}, u32[]{:S(2)}) collective-permute-start(bf16[64,128]{1,0:T(8,128)(2,1)S(1)} %get-tuple-element.45), channel_id=1, source_target_pairs={{0,16},{8,24},{16,32},{24,40},{32,48},{40,56},{48,64},{56,72},{64,... | collective-permute-start | bytes 49160 | tf_op jit(solution)/shard_map/ppermute | solution.py:295
  62.1 7.2 %collective-permute-start.9 = (bf16[64,128]{1,0:T(8,128)(2,1)S(1)}, bf16[64,128]{1,0:T(8,128)(2,1)S(1)}, u32[]{:S(2)}, u32[]{:S(2)}) collective-permute-start(bf16[64,128]{1,0:T(8,128)(2,1)S(1)} %get-tuple-element.46), channel_id=1, source_target_pairs={{16,0},{24,8},{32,16},{40,24},{48,32},{56,40},{64,48},{72,56},{80,... | collective-permute-start | bytes 49160 | tf_op jit(solution)/shard_map/ppermute | solution.py:295
  69.4 1.9 %collective-permute-start.10 = (bf16[64,128]{1,0:T(8,128)(2,1)S(1)}, bf16[64,128]{1,0:T(8,128)(2,1)S(1)}, u32[]{:S(2)}, u32[]{:S(2)}) collective-permute-start(bf16[64,128]{1,0:T(8,128)(2,1)S(1)} %get-tuple-element.47), channel_id=1, source_target_pairs={{0,24},{8,32},{16,40},{24,48},{32,56},{40,64},{48,72},{56,80},{64,... | collective-permute-start | bytes 49160 | tf_op jit(solution)/shard_map/ppermute | solution.py:295
  71.3 7.3 %collective-permute-start.11 = (bf16[64,128]{1,0:T(8,128)(2,1)S(1)}, bf16[64,128]{1,0:T(8,128)(2,1)S(1)}, u32[]{:S(2)}, u32[]{:S(2)}) collective-permute-start(bf16[64,128]{1,0:T(8,128)(2,1)S(1)} %get-tuple-element.48), channel_id=1, source_target_pairs={{24,0},{32,8},{40,16},{48,24},{56,32},{64,40},{72,48},{80,56},{88,... | collective-permute-start | bytes 49160 | tf_op jit(solution)/shard_map/ppermute | solution.py:295
  78.6 14.2 %shard_map.74 = (bf16[256,256,128]{2,1,0:T(8,128)(2,1)}, s32[264]{0:T(512)S(1)}, s32[264]{0:T(512)S(1)}, s32[1]{0:T(128)}) custom-call(bf16[25,32,128]{2,1,0:T(8,128)(2,1)S(1)} %get-tuple-element.27.a_home, bf16[73,16,128]{2,1,0:T(8,128)(2,1)S(1)} %collective-permute-done.rest_0_.n1, bf16[73,16,128]{2,1,0:T(8,128)(2,1)S(1)} %collective-permute-done.1.rest_1_.s1, ...), custom_call_target="tpu_custom_call" | custom-call | flops 8000000 | bytes 24000000 | tf_op jit(solution)/shard_map/pallas_call | solution.py:348
  93.5 11.1 %shard_map.76 = f32[4,4,8192]{2,1,0:T(4,128)} custom-call(s32[264]{0:T(512)S(1)} %get-tuple-element.34.entry_slot, s32[264]{0:T(512)S(1)} %get-tuple-element.35.entry_win, s32[1]{0:T(128)} %get-tuple-element.36.entry_count, s32[1]{0:T(128)} %bitcast.2.lev, f32[4]{0:T(128)S(1)} %copy-done.6, bf16[256,256,128]{2,1,0:T(8,128)(2,1)} %get-tuple-element.37.mats, ...), custom_call_target="tpu_custom_call" | custom-call | flops 5000000 | bytes 15000000 | tf_op jit(solution)/shard_map/pallas_call | solution.py:370
  (24 shorter events, 2.9 us)
Async XLA Ops:
  0.0 0.9 copy-start
  1.0 0.9 copy-start.2
  1.9 1.0 copy-start.4
  2.9 0.9 copy-start.5
  3.8 0.7 copy-start.7
  4.5 0.7 copy-start.8
  7.3 18.1 %collective-permute-start = (bf16[73,16,128]{2,1,0:T(8,128)(2,1)S(1)}, bf16[73,16,128]{2,1,0:T(8,128)(2,1)S(1)}, u32[]{:S(2)}, u32[]{:S(2)}) collective-permute-start(bf16[73,16,128]{2,1,0:T(8,128)(2,1)S(1)} %get-tuple-element.28), channel_id=1, source_target_pairs={{0,8},{8,16},{16,24},{24,32},{32,40},{40,48},{48,56},{56,64},{64,7... | collective-permute-start | bytes 897032 | tf_op jit(solution)/shard_map/ppermute | solution.py:295
  9.2 16.2 %collective-permute-start.1 = (bf16[73,16,128]{2,1,0:T(8,128)(2,1)S(1)}, bf16[73,16,128]{2,1,0:T(8,128)(2,1)S(1)}, u32[]{:S(2)}, u32[]{:S(2)}) collective-permute-start(bf16[73,16,128]{2,1,0:T(8,128)(2,1)S(1)} %get-tuple-element.29), channel_id=1, source_target_pairs={{8,0},{16,8},{24,16},{32,24},{40,32},{48,40},{56,48},{64,56},{72,6... | collective-permute-start | bytes 897032 | tf_op jit(solution)/shard_map/ppermute | solution.py:295
  16.2 12.0 %collective-permute-start.2 = (bf16[73,16,128]{2,1,0:T(8,128)(2,1)S(1)}, bf16[73,16,128]{2,1,0:T(8,128)(2,1)S(1)}, u32[]{:S(2)}, u32[]{:S(2)}) collective-permute-start(bf16[73,16,128]{2,1,0:T(8,128)(2,1)S(1)} %get-tuple-element.30), channel_id=1, source_target_pairs={{0,16},{8,24},{16,32},{24,40},{32,48},{40,56},{48,64},{56,72},{64,... | collective-permute-start | bytes 897032 | tf_op jit(solution)/shard_map/ppermute | solution.py:295
  18.1 11.5 %collective-permute-start.3 = (bf16[73,16,128]{2,1,0:T(8,128)(2,1)S(1)}, bf16[73,16,128]{2,1,0:T(8,128)(2,1)S(1)}, u32[]{:S(2)}, u32[]{:S(2)}) collective-permute-start(bf16[73,16,128]{2,1,0:T(8,128)(2,1)S(1)} %get-tuple-element.31), channel_id=1, source_target_pairs={{16,0},{24,8},{32,16},{40,24},{48,32},{56,40},{64,48},{72,56},{80,... | collective-permute-start | bytes 897032 | tf_op jit(solution)/shard_map/ppermute | solution.py:295
  29.6 0.9 copy-start.1
  30.6 0.9 copy-start.3
  34.5 58.3 %all-to-all-start = ((bf16[8,64,128]{2,1,0:T(8,128)(2,1)}), bf16[8,64,128]{2,1,0:T(8,128)(2,1)S(1)}, u32[]{:S(2)}, u32[]{:S(2)}) async-start(bf16[8,64,128]{2,1,0:T(8,128)(2,1)} %get-tuple-element.42), calls=%async_computation | async-start | bytes 262144 | tf_op jit(solution)/shard_map/all_to_all | solution.py:345
  42.1 20.0 %collective-permute-start.4 = (bf16[41,16,128]{2,1,0:T(8,128)(2,1)S(1)}, bf16[41,16,128]{2,1,0:T(8,128)(2,1)S(1)}, u32[]{:S(2)}, u32[]{:S(2)}) collective-permute-start(bf16[41,16,128]{2,1,0:T(8,128)(2,1)S(1)} %get-tuple-element.32), channel_id=1, source_target_pairs={{0,24},{8,32},{16,40},{24,48},{32,56},{40,64},{48,72},{56,80},{64,... | collective-permute-start | bytes 503816 | tf_op jit(solution)/shard_map/ppermute | solution.py:295
  44.0 25.4 %collective-permute-start.5 = (bf16[41,16,128]{2,1,0:T(8,128)(2,1)S(1)}, bf16[41,16,128]{2,1,0:T(8,128)(2,1)S(1)}, u32[]{:S(2)}, u32[]{:S(2)}) collective-permute-start(bf16[41,16,128]{2,1,0:T(8,128)(2,1)S(1)} %get-tuple-element.33), channel_id=1, source_target_pairs={{24,0},{32,8},{40,16},{48,24},{56,32},{64,40},{72,48},{80,56},{88,... | collective-permute-start | bytes 503816 | tf_op jit(solution)/shard_map/ppermute | solution.py:295
  51.3 20.0 %collective-permute-start.6 = (bf16[64,128]{1,0:T(8,128)(2,1)S(1)}, bf16[64,128]{1,0:T(8,128)(2,1)S(1)}, u32[]{:S(2)}, u32[]{:S(2)}) collective-permute-start(bf16[64,128]{1,0:T(8,128)(2,1)S(1)} %get-tuple-element.43), channel_id=1, source_target_pairs={{0,8},{8,16},{16,24},{24,32},{32,40},{40,48},{48,56},{56,64},{64,7... | collective-permute-start | bytes 49160 | tf_op jit(solution)/shard_map/ppermute | solution.py:295
  53.7 39.0 %collective-permute-start.7 = (bf16[64,128]{1,0:T(8,128)(2,1)S(1)}, bf16[64,128]{1,0:T(8,128)(2,1)S(1)}, u32[]{:S(2)}, u32[]{:S(2)}) collective-permute-start(bf16[64,128]{1,0:T(8,128)(2,1)S(1)} %get-tuple-element.44), channel_id=1, source_target_pairs={{8,0},{16,8},{24,16},{32,24},{40,32},{48,40},{56,48},{64,56},{72,6... | collective-permute-start | bytes 49160 | tf_op jit(solution)/shard_map/ppermute | solution.py:295
  60.2 32.6 %collective-permute-start.8 = (bf16[64,128]{1,0:T(8,128)(2,1)S(1)}, bf16[64,128]{1,0:T(8,128)(2,1)S(1)}, u32[]{:S(2)}, u32[]{:S(2)}) collective-permute-start(bf16[64,128]{1,0:T(8,128)(2,1)S(1)} %get-tuple-element.45), channel_id=1, source_target_pairs={{0,16},{8,24},{16,32},{24,40},{32,48},{40,56},{48,64},{56,72},{64,... | collective-permute-start | bytes 49160 | tf_op jit(solution)/shard_map/ppermute | solution.py:295
  62.1 30.7 %collective-permute-start.9 = (bf16[64,128]{1,0:T(8,128)(2,1)S(1)}, bf16[64,128]{1,0:T(8,128)(2,1)S(1)}, u32[]{:S(2)}, u32[]{:S(2)}) collective-permute-start(bf16[64,128]{1,0:T(8,128)(2,1)S(1)} %get-tuple-element.46), channel_id=1, source_target_pairs={{16,0},{24,8},{32,16},{40,24},{48,32},{56,40},{64,48},{72,56},{80,... | collective-permute-start | bytes 49160 | tf_op jit(solution)/shard_map/ppermute | solution.py:295
  69.4 23.4 %collective-permute-start.10 = (bf16[64,128]{1,0:T(8,128)(2,1)S(1)}, bf16[64,128]{1,0:T(8,128)(2,1)S(1)}, u32[]{:S(2)}, u32[]{:S(2)}) collective-permute-start(bf16[64,128]{1,0:T(8,128)(2,1)S(1)} %get-tuple-element.47), channel_id=1, source_target_pairs={{0,24},{8,32},{16,40},{24,48},{32,56},{40,64},{48,72},{56,80},{64,... | collective-permute-start | bytes 49160 | tf_op jit(solution)/shard_map/ppermute | solution.py:295
  71.3 21.5 %collective-permute-start.11 = (bf16[64,128]{1,0:T(8,128)(2,1)S(1)}, bf16[64,128]{1,0:T(8,128)(2,1)S(1)}, u32[]{:S(2)}, u32[]{:S(2)}) collective-permute-start(bf16[64,128]{1,0:T(8,128)(2,1)S(1)} %get-tuple-element.48), channel_id=1, source_target_pairs={{24,0},{32,8},{40,16},{48,24},{56,32},{64,40},{72,48},{80,56},{88,... | collective-permute-start | bytes 49160 | tf_op jit(solution)/shard_map/ppermute | solution.py:295
  92.8 0.7 copy-start.6

commit v2 on v1

v2 whole, which is shorter than its diff:
```python
import jax
import jax.numpy as jnp
from jax import lax
from jax.experimental import pallas as pl
from jax.experimental.pallas import tpu as pltpu
from jax.sharding import PartitionSpec as P

NLON = 4096
BLK = 128
WIN = 256
SWEEPS = 4
REACH = 3
HOME = 32
OFFCAP = 16

F32 = jnp.float32
BF16 = jnp.bfloat16
STEN = 12
NBLK = 64
CELLS = 8192
NWIN = CELLS // WIN
OFFSETS = (-3, -2, -1, 1, 2, 3)
GROUPS = len(OFFSETS)
SLOTS = HOME + OFFCAP * GROUPS
HALO = NLON // BLK
ROUTE = 2 * STEN + 1
LOAD = ROUTE + OFFCAP
RELAY = HALO + LOAD
LOWS = HALO // 2
OWN = HALO + LOWS + 1 + LOAD
EARLY = HOME + 3 * OFFCAP
LATE = 3 * OFFCAP
PACK = 4
RING = 4
REMAINDER = 1e-6


def vmem():
    return pl.BlockSpec(memory_space=pltpu.VMEM)


def smem():
    return pl.BlockSpec(memory_space=pltpu.SMEM)


def hbm():
    return pl.BlockSpec(memory_space=pl.ANY)


def lanes(i):
    return slice(i * BLK, (i + 1) * BLK)


def base_of(by):
    return 0 if by == 0 else HOME + OFFCAP * OFFSETS.index(by)


def either(core, first, second):
    return pl.multiple_of(jnp.where(core == 0, base_of(first), base_of(second)), OFFCAP)


def launch(copies):
    copies = [pltpu.make_async_copy(*copy) for copy in copies]
    for copy in copies:
        copy.start()
    return copies


def finish(copies):
    for copy in copies:
        copy.wait()


def call(kernel, outs, ins, scratch, cost, limit):
    return pl.pallas_call(
        kernel,
        out_shape=[jax.ShapeDtypeStruct(shape, dtype) for shape, dtype, _ in outs],
        out_specs=[spec for _, _, spec in outs],
        in_specs=ins,
        scratch_shapes=scratch,
        compiler_params=pltpu.CompilerParams(vmem_limit_bytes=limit << 20),
        cost_estimate=pl.CostEstimate(flops=cost * 1000000, bytes_accessed=cost * 3000000, transcendentals=0),
    )


def pack_kernel(
    me, dest_in, win_in, adj_in, helm_in, cell_in, weight_in,
    slots, a_home, b_home, own, plus, minus, cross,
    dest, win, adj, helm, cell, weight, count, a_all, b_all, sems,
):
    pairs = ((dest_in, dest), (win_in, win), (adj_in, adj), (helm_in, helm), (cell_in, cell), (weight_in, weight))
    copies = launch([(a, b, sems.at[i]) for i, (a, b) in enumerate(pairs)])
    core = lax.rem(me[0], 2)
    for by in range(-REACH, REACH + 1):
        count[by + REACH] = base_of(by)
    a_all[...] = jnp.zeros_like(a_all)
    b_all[...] = jnp.zeros_like(b_all)
    finish(copies)
    lane = lax.broadcasted_iota(jnp.int32, (16, BLK), 1)
    table = jnp.zeros((16, BLK), jnp.int32)
    for b in range(NBLK):
        route = dest[b] - me[0] + REACH
        slot = count[route]
        count[route] = slot + 1
        slots[b] = slot
        table = jnp.where(lane == b, slot, table)
        a_all[pl.ds(slot, STEN, stride=SLOTS), :] = weight[:, lanes(b)].astype(F32)
        a_all[pl.ds(STEN * SLOTS + slot, STEN, stride=SLOTS), :] = cell[:, lanes(b)].astype(F32)
        a_all[pl.ds(2 * STEN * SLOTS + slot, 1), :] = jnp.full((1, BLK), win[b] + 1, jnp.int32).astype(F32)
        b_all[slot] = jnp.concatenate([adj[f, :, lanes(b)].astype(F32) for f in range(4)], axis=0).astype(BF16)
    for r in range(ROUTE):
        a_home[r] = a_all[r * SLOTS : r * SLOTS + HOME, :].astype(BF16)
    b_home[...] = b_all[:HOME]
    loads = (
        (own, HALO + LOWS + 1, either(core, 1, -1)),
        (plus, HALO, either(core, 3, 1)),
        (plus, RELAY, either(core, 2, 2)),
        (minus, HALO, either(core, -1, -3)),
        (minus, RELAY, either(core, -2, -2)),
        (cross, 0, either(core, -3, 3)),
    )
    for parcel, at, base in loads:
        for r in range(ROUTE):
            parcel[at + r] = a_all[pl.ds(r * SLOTS + base, OFFCAP), :].astype(BF16)
        parcel[at + ROUTE : at + LOAD] = b_all[pl.ds(base, OFFCAP)]
    rest = []
    for i in range(HALO):
        coef = jnp.concatenate([helm[:, lanes(i)], helm[:, lanes(HALO + i)]], axis=0)
        rest.append(coef - coef.astype(BF16).astype(F32))
        first = [adj[0, :, lanes(i)].astype(F32), adj[0, :, lanes(HALO + i)].astype(F32)]
        piece = jnp.concatenate(first + [coef], axis=0).astype(BF16)
        for parcel in (own, plus, minus):
            parcel[i] = piece
    for i in range(LOWS):
        own[HALO + i] = jnp.concatenate(rest[2 * i : 2 * i + 2], axis=0).astype(BF16)
    own[HALO + LOWS] = table.astype(F32).astype(BF16)


def relay_kernel(own, plus, minus, out, sems):
    finish(
        launch(
            [
                (own, out.at[pl.ds(0, OWN)], sems.at[0]),
                (plus.at[pl.ds(0, RELAY)], out.at[pl.ds(OWN, RELAY)], sems.at[1]),
                (minus.at[pl.ds(0, RELAY)], out.at[pl.ds(OWN + RELAY, RELAY)], sems.at[2]),
            ]
        )
    )


def solve_kernel(
    me, slots, adj_in, helm_in, own, plus, minus, mate,
    local, totals, f_home, f_mate, f_plus, f_minus, f_cross,
    adj, helm, halo, lows, rhs, coef, result, table, table_s, mine_all, mate_all, t_all, sems, table_sem,
):
    core = lax.rem(me[0], 2)
    tables = launch([(mate.at[pl.ds(HALO, LOWS + 1)], lows, sems.at[8])])
    pairs = (
        (adj_in.at[0], adj),
        (helm_in, helm),
        (plus.at[pl.ds(0, HALO)], halo.at[core]),
        (mate.at[pl.ds(OWN, HALO)], halo.at[1 - core]),
        (own.at[pl.ds(0, HALO)], halo.at[2 + core]),
        (mate.at[pl.ds(0, HALO)], halo.at[3 - core]),
        (minus.at[pl.ds(0, HALO)], halo.at[4 + core]),
        (mate.at[pl.ds(OWN + RELAY, HALO)], halo.at[5 - core]),
    )
    copies = launch([(a, b, sems.at[i]) for i, (a, b) in enumerate(pairs)])
    mine_all[...] = jnp.zeros_like(mine_all)
    mate_all[...] = jnp.zeros_like(mate_all)
    finish(tables)
    table[...] = lows[LOWS].astype(F32)[:1].astype(jnp.int32)
    tables = launch([(table, table_s, table_sem)])
    finish(copies)
    for band in range(6):
        for i in range(HALO):
            tile = halo[band, i].astype(F32)
            rhs[band, :, lanes(i)] = tile[:8]
            coef[band, :, lanes(i)] = tile[8:]
    for i in range(LOWS):
        tile = lows[i].astype(F32)
        coef[3 - core, :, lanes(2 * i)] += tile[:8]
        coef[3 - core, :, lanes(2 * i + 1)] += tile[8:]
    coef[2 + core] = jnp.concatenate([helm[:, :NLON], helm[:, NLON:]], axis=0)
    right = [rhs[band] for band in range(6)]
    factor = [coef[band] for band in range(6)]
    scale = [1.0 / (1.0 + 4.0 * c) for c in factor]
    solved = [r * s for r, s in zip(right, scale)]
    upper = lax.broadcasted_iota(jnp.int32, (8, NLON), 0) < 4
    for wanted in ((0, 1, 2, 3, 4, 5), (1, 2, 3, 4), (1, 2, 3, 4), (2, 3)):
        shifted = [c * s for c, s in zip(factor, solved)]
        turned = [pltpu.roll(p, 4, 0) for p in shifted]
        fresh = list(solved)
        for band in wanted:
            p = shifted[band]
            north = turned[max(band - 1, 0)]
            south = turned[min(band + 1, 5)]
            total = turned[band] + jnp.where(upper, north, south)
            total = total + pltpu.roll(p, 1, 1) + pltpu.roll(p, NLON - 1, 1)
            fresh[band] = (right[band] + total) * scale[band]
        solved = fresh
    result[0] = solved[2]
    result[1] = solved[3]
    mine = result[core]
    other = result[1 - core]
    finish(tables)
    for r in range(2):
        sums = mine[4 * r : 4 * r + 1]
        local[4 * r : 4 * r + 1, :] = sums
        for level in range(1, 4):
            sums = sums + mine[4 * r + level : 4 * r + level + 1]
            local[4 * r + level : 4 * r + level + 1, :] = sums
        for i in range(HALO):
            b = HALO * r + i
            t_all[b : b + 1, :] = sums[:, lanes(i)]
            mine_all[pl.ds(slots[b] * 4, 4), :] = mine[4 * r : 4 * r + 4, lanes(i)]
            mate_all[pl.ds(table_s[0, b] * 4, 4), :] = other[4 * r : 4 * r + 4, lanes(i)]
    totals_here = t_all[...].astype(BF16)
    for i in range(totals.shape[0]):
        totals[i] = totals_here

    def part(source, first, second):
        return source[pl.ds(either(core, first, second) * 4, OFFCAP * 4), :].astype(BF16)

    f_home[...] = mine_all[: HOME * 4].astype(BF16)
    f_mate[...] = part(mate_all, -1, 1)
    f_plus[: OFFCAP * 4] = part(mine_all, 2, 2)
    f_plus[OFFCAP * 4 :] = part(mate_all, 1, 3)
    f_minus[: OFFCAP * 4] = part(mine_all, -2, -2)
    f_minus[OFFCAP * 4 :] = part(mate_all, -3, -1)
    f_cross[...] = part(mine_all, -3, 3)


def matrix_kernel(count, home, offsets, *refs):
    a_home = refs[0] if home else None
    parcels, refs = refs[home : home + len(offsets)], refs[home + len(offsets) :]
    mats, entry_slot, entry_win, entry_count, a_in, cells, merged, ring, meta, meta_s, sems, ring_sems, meta_sem = refs
    copies = launch([(p.at[pl.ds(at, ROUTE)], a_in.at[i], sems.at[i]) for i, (p, at) in enumerate(zip(parcels, offsets))])

    lane = lax.broadcasted_iota(jnp.int32, (8, BLK), 1)
    row = lax.broadcasted_iota(jnp.int32, (8, BLK), 0)

    def merge(base, load):
        w = [load(k) for k in range(STEN)]
        c = [load(STEN + k) for k in range(STEN)]
        total = list(w)
        for k in range(STEN):
            for m in range(k):
                same = c[k] == c[m]
                total[k] = total[k] + jnp.where(same, w[m], 0.0)
                total[m] = total[m] + jnp.where(same, w[k], 0.0)
        lost = jnp.zeros((8, BLK), F32)
        held = jnp.zeros((8, BLK), F32)
        for k in range(STEN):
            high = total[k].astype(BF16).astype(F32)
            low = total[k] - high
            cells[k, base : base + 8, :] = c[k]
            merged[k, base : base + 8, :] = high
            merged[k, count + base : count + base + 8, :] = low
            lost = lost + low * low
            held = held + w[k] * w[k]
        more = jnp.sum(lost, axis=1, keepdims=True) > REMAINDER * jnp.sum(held, axis=1, keepdims=True)
        mark = load(2 * STEN)
        mark = jnp.where(mark > 0.0, mark + jnp.where(more, 64.0, 0.0), 0.0)
        return jnp.where(lane == row + base, mark, 0.0)

    marks = jnp.zeros((8, BLK), F32)
    for at in range(0, HOME if home else 0, 16):
        pair = [a_home[r, at : at + 16, :].astype(F32) for r in range(ROUTE)]
        for half in (0, 8):
            marks = marks + merge(at + half, lambda r: pair[r][half : half + 8])
    for i in range(len(offsets)):
        copies[i].wait()
        pair = [a_in[i, r].astype(F32) for r in range(ROUTE)]
        at = (HOME if home else 0) + OFFCAP * i
        for half in (0, 8):
            marks = marks + merge(at + half, lambda r: pair[r][half : half + 8])
    meta[...] = jnp.sum(marks, axis=0, keepdims=True).astype(jnp.int32)
    finish(launch([(meta, meta_s, meta_sem)]))

    def enlist(i, n):
        for j in range(8):
            slot = i * 8 + j
            mark = meta_s[0, slot]
            window = (mark & 63) - 1
            entry_slot[n] = slot
            entry_win[n] = window
            n = n + (mark > 0).astype(jnp.int32)
            entry_slot[n] = slot + count
            entry_win[n] = window
            n = n + (mark >= 64).astype(jnp.int32)
        return n

    n = lax.fori_loop(0, count // 8, enlist, jnp.int32(0))
    entry_count[0] = n
    for j in range(PACK):
        entry_slot[n + j] = 0
        entry_win[n + j] = NWIN

    iota = lax.broadcasted_iota(jnp.int32, (16, BLK), 0).astype(F32)

    def stored(group):
        at = lax.rem(group, 2)
        return pltpu.make_async_copy(ring.at[at], mats.at[pl.ds(group * PACK, PACK)], ring_sems.at[at])

    def build(group, carry):
        @pl.when(group >= 2)
        def _():
            stored(group - 2).wait()

        for j in range(PACK):
            entry = entry_slot[group * PACK + j]
            slot = lax.rem(entry, count)
            c = [jnp.broadcast_to(cells[k, pl.ds(slot, 1), :], (16, BLK)).astype(BF16) for k in range(STEN)]
            w = [jnp.broadcast_to(merged[k, pl.ds(entry, 1), :], (16, BLK)).astype(BF16) for k in range(STEN)]
            for i in range(WIN // 16):
                here = (iota + 16.0 * i).astype(BF16)
                m = jnp.zeros((16, BLK), BF16)
                for k in range(STEN):
                    m = jnp.where(c[k] == here, w[k], m)
                ring[lax.rem(group, 2), j, 16 * i : 16 * i + 16, :] = m
        stored(group).start()
        return carry

    groups = (n + PACK - 1) // PACK
    lax.fori_loop(0, groups, build, 0)

    @pl.when(groups >= 2)
    def _():
        stored(groups - 2).wait()

    @pl.when(groups >= 1)
    def _():
        stored(groups - 1).wait()


def spread_kernel(
    me, lev, geo_in, slot1, win1, count1, mats1, slot2, win2, count2, mats2,
    b_home, plus, minus, cross, mate, f_home, f_mate, f_plus, f_minus, f_cross, local, above,
    out, geo, values, firsts, total, ring, sems, ring_sems,
):
    core = lax.rem(me[0], 2)
    parts = (
        (plus, RELAY + ROUTE),
        (minus, RELAY + ROUTE),
        (cross, ROUTE),
        (mate, HALO + LOWS + 1 + ROUTE),
        (mate, OWN + HALO + ROUTE),
        (mate, OWN + RELAY + HALO + ROUTE),
    )
    pairs = [(b_home, values.at[pl.ds(0, HOME)])]
    pairs += [
        (p.at[pl.ds(at, OFFCAP)], values.at[pl.ds(HOME + OFFCAP * i, OFFCAP)]) for i, (p, at) in enumerate(parts)
    ]
    pairs += [(geo_in, geo)]
    copies = launch([(a, b, sems.at[i]) for i, (a, b) in enumerate(pairs)])
    loops = ((slot1, win1, count1, mats1, 0, EARLY), (slot2, win2, count2, mats2, EARLY, LATE))

    def fetched(mats, lane, group):
        at = lax.rem(group, RING)
        return pltpu.make_async_copy(mats.at[pl.ds(group * PACK, PACK)], ring.at[lane, at], ring_sems.at[lane, at])

    for lane, (_, _, count, mats, _, _) in enumerate(loops):
        groups = (count[0] + PACK - 1) // PACK
        for g in range(RING):

            @pl.when(g < groups)
            def _():
                fetched(mats, lane, g).start()

    total[...] = jnp.zeros_like(total)
    half = OFFCAP * 4
    pieces = (
        f_plus[:half], f_minus[:half], f_cross[...], f_mate[...], f_plus[half:], f_minus[half:],
    )
    firsts[: HOME * 4, :] = f_home[...].astype(F32)
    for i, piece in enumerate(pieces):
        firsts[HOME * 4 + half * i : HOME * 4 + half * (i + 1), :] = piece.astype(F32)
    firsts[SLOTS * 4 :, :] = jnp.zeros((8, BLK), F32)
    finish(copies)
    first_rows = lax.broadcasted_iota(jnp.int32, (8, BLK), 0) < 4

    for lane, (slots, wins, count, mats, base, size) in enumerate(loops):
        groups = (count[0] + PACK - 1) // PACK

        def step(group, carry):
            fetched(mats, lane, group).wait()
            products = []
            for j in range(PACK):
                slot = base + lax.rem(slots[group * PACK + j], size)
                tile = values[slot].astype(F32)
                head = jnp.where(first_rows, firsts[pl.ds(slot * 4, 8), :], tile[:8])
                left = jnp.concatenate([head, tile[8:]], axis=0).astype(BF16)
                mat = ring[lane, lax.rem(group, RING), j]
                products.append(lax.dot_general(left, mat, (((1,), (1,)), ((), ())), preferred_element_type=F32))

            for j in range(PACK):
                start = pl.multiple_of(wins[group * PACK + j] * WIN, WIN)
                total[:, pl.ds(start, WIN)] += products[j]

            @pl.when(group + RING < groups)
            def _():
                fetched(mats, lane, group + RING).start()

            return carry

        lax.fori_loop(0, groups, step, 0)

    sums = jnp.zeros((NBLK, BLK), F32)
    for peer in range(above.shape[0]):
        sums = sums + jnp.where(peer < lev[0], above[peer].astype(F32), 0.0)
    level = lax.broadcasted_iota(jnp.int32, (4, BLK), 0)
    factor = jnp.zeros((4, BLK), F32)
    for i in range(4):
        factor = jnp.where(level == i, geo[i], factor)
    for f in (0, 1, 3):
        out[f] = total[4 * f : 4 * f + 4, :CELLS]
    for b in range(NBLK):
        r = b // HALO
        term = factor * (local[4 * r : 4 * r + 4, lanes(b % HALO)] + sums[b : b + 1])
        out[2, :, lanes(b)] = total[8:12, lanes(b)] + term


def moved(parcel, by):
    peers = lax.axis_size("tile")
    return lax.ppermute(parcel, "tile", [(i, i + by) for i in range(peers) if 0 <= i + by < peers])


def swapped(parcel):
    return lax.ppermute(parcel, "tile", [(i, i ^ 1) for i in range(lax.axis_size("tile"))])


def crossed(parcel):
    peers = lax.axis_size("tile")
    pairs = [(i, i + (3 if i % 2 else -3)) for i in range(peers)]
    return lax.ppermute(parcel, "tile", [(i, j) for i, j in pairs if 0 <= j < peers])


def matrices(home, parts):
    count = (HOME if home else 0) + OFFCAP * len(parts)
    entries = 2 * count
    return call(
        lambda *refs: matrix_kernel(count, len(home), [at for _, at in parts], *refs),
        [
            ((entries, WIN, BLK), BF16, hbm()),
            ((entries + 8,), jnp.int32, smem()),
            ((entries + 8,), jnp.int32, smem()),
            ((1,), jnp.int32, smem()),
        ],
        [vmem()] * len(home) + [hbm()] * len(parts),
        [
            pltpu.VMEM((len(parts), ROUTE, 16, BLK), BF16),
            pltpu.VMEM((STEN, count, BLK), F32),
            pltpu.VMEM((STEN, 2 * count, BLK), F32),
            pltpu.VMEM((2, PACK, WIN, BLK), BF16),
            pltpu.VMEM((1, BLK), jnp.int32),
            pltpu.SMEM((1, BLK), jnp.int32),
            pltpu.SemaphoreType.DMA((len(parts),)),
            pltpu.SemaphoreType.DMA((2,)),
            pltpu.SemaphoreType.DMA,
        ],
        4,
        16,
    )(*home, *[parcel for parcel, _ in parts])


def body(adj_in, helm_coef, geo_coef, dest_tile, src_window, src_cell, interp_w):
    me = lax.axis_index("tile").astype(jnp.int32)[None]
    lev = lax.axis_index("lev").astype(jnp.int32)[None]
    peers = lax.axis_size("lev")

    def parcel(entries):
        return ((entries, 16, BLK), BF16, vmem())

    def strip(blocks):
        return ((blocks * 4, BLK), BF16, vmem())

    slots, a_home, b_home, own, plus, minus, cross = call(
        pack_kernel,
        [
            ((NBLK,), jnp.int32, smem()),
            ((ROUTE, HOME, BLK), BF16, vmem()),
            parcel(HOME),
            parcel(OWN),
            parcel(RELAY + LOAD),
            parcel(RELAY + LOAD),
            parcel(LOAD),
        ],
        [smem()] + [hbm()] * 6,
        [
            pltpu.SMEM((NBLK,), jnp.int32),
            pltpu.SMEM((NBLK,), jnp.int32),
            pltpu.VMEM(adj_in.shape, BF16),
            pltpu.VMEM(helm_coef.shape, F32),
            pltpu.VMEM(src_cell.shape, jnp.int32),
            pltpu.VMEM(interp_w.shape, BF16),
            pltpu.SMEM((2 * REACH + 1,), jnp.int32),
            pltpu.VMEM((ROUTE * SLOTS, BLK), F32),
            pltpu.VMEM((SLOTS, 16, BLK), BF16),
            pltpu.SemaphoreType.DMA((6,)),
        ],
        1,
        24,
    )(me, dest_tile[:, 0], src_window, adj_in, helm_coef, src_cell, interp_w)
    plus = moved(plus, 2)
    minus = moved(minus, -2)
    cross = crossed(cross)

    relayed = call(
        relay_kernel,
        [((OWN + 2 * RELAY, 16, BLK), BF16, hbm())],
        [hbm()] * 3,
        [pltpu.SemaphoreType.DMA((3,))],
        1,
        16,
    )(own, plus, minus)[0]
    mate = swapped(relayed)

    early = matrices([a_home], [(plus, RELAY), (minus, RELAY), (cross, 0)])

    local, totals, f_home, f_mate, f_plus, f_minus, f_cross = call(
        solve_kernel,
        [
            ((8, NLON), F32, vmem()),
            ((peers, NBLK, BLK), BF16, vmem()),
            strip(HOME),
            strip(OFFCAP),
            strip(2 * OFFCAP),
            strip(2 * OFFCAP),
            strip(OFFCAP),
        ],
        [smem()] * 2 + [hbm()] * 6,
        [
            pltpu.VMEM(adj_in.shape[1:], BF16),
            pltpu.VMEM(helm_coef.shape, F32),
            pltpu.VMEM((6, HALO, 16, BLK), BF16),
            pltpu.VMEM((LOWS + 1, 16, BLK), BF16),
            pltpu.VMEM((6, 8, NLON), F32),
            pltpu.VMEM((6, 8, NLON), F32),
            pltpu.VMEM((2, 8, NLON), F32),
            pltpu.VMEM((1, BLK), jnp.int32),
            pltpu.SMEM((1, BLK), jnp.int32),
            pltpu.VMEM((SLOTS * 4, BLK), F32),
            pltpu.VMEM((SLOTS * 4, BLK), F32),
            pltpu.VMEM((NBLK, BLK), F32),
            pltpu.SemaphoreType.DMA((9,)),
            pltpu.SemaphoreType.DMA,
        ],
        2,
        24,
    )(me, slots, adj_in, helm_coef, own, plus, minus, mate)
    above = lax.all_to_all(totals, "lev", 0, 0)
    f_plus = moved(f_plus, 2)
    f_minus = moved(f_minus, -2)
    f_cross = crossed(f_cross)

    late = matrices(
        [],
        [(mate, HALO + LOWS + 1), (mate, OWN + HALO), (mate, OWN + RELAY + HALO)],
    )

    def lists(found):
        mats, entry_slot, entry_win, entry_count = found
        return entry_slot, entry_win, entry_count, mats

    listed = [smem()] * 3 + [hbm()]
    return call(
        spread_kernel,
        [((4, 4, CELLS), F32, vmem())],
        [smem()] * 2 + [hbm()] + listed * 2 + [hbm()] * 5 + [vmem()] * 7,
        [
            pltpu.SMEM((4,), F32),
            pltpu.VMEM((SLOTS, 16, BLK), BF16),
            pltpu.VMEM((SLOTS * 4 + 8, BLK), F32),
            pltpu.VMEM((16, CELLS + WIN), F32),
            pltpu.VMEM((2, RING, PACK, WIN, BLK), BF16),
            pltpu.SemaphoreType.DMA((GROUPS + 2,)),
            pltpu.SemaphoreType.DMA((2, RING)),
        ],
        4,
        24,
    )(
        me, lev, geo_coef, *lists(early), *lists(late),
        b_home, plus, minus, cross, mate, f_home, f_mate, f_plus, f_minus, f_cross, local, above,
    )[0]


def solution(mesh):
    placed = (
        P(None, "lev", "tile"),
        P("lev", "tile"),
        P("lev"),
        P("tile", None),
        P("tile"),
        P(None, "tile"),
        P(None, "tile"),
    )
    return jax.shard_map(
        body, mesh=mesh, in_specs=placed, out_specs=P(None, "lev", "tile"), check_vma=False
    )
```

time: 105 us -> 94.9 us (0.904)
  the two profiles are of different devices: /device:TPU:264 before, /device:TPU:333 now
where the time goes in v2:
time: 94.9 us; the launch traced here: 94.3 us
  starting transfers between devices  32 us (34%)
  Pallas kernels  29 us (31%)
  local copies, waits for them, and re-layouts  20.4 us (21%)
  waiting for transfers between devices  12.8 us (13%)
    unnamed x26, local copies, waits for them, and re-layouts  20.4 us
    pallas_call x2, Pallas kernels, matrices(): call(lambda *refs: matrix_kernel(count, len(home), [at for _, at in parts...  12.8 us
    ppermute x4, starting transfers between devices, moved(): lax.ppermute(parcel, 'tile', [(i, i + by) for i in range(peers) if 0 <= i...  11.9 us
    ppermute x4, waiting for transfers between devices, moved(): lax.ppermute(parcel, 'tile', [(i, i + by) for i in range(peers) if 0 <= i...  10.7 us
    pallas_call x1, Pallas kernels, body(): call(spread_kernel, [((4, 4, CELLS), F32, vmem())], [smem()] * 2 + [hbm()...  9.48 us
    ppermute x2, starting transfers between devices, crossed(): lax.ppermute(parcel, 'tile', [(i, j) for i, j in pairs if 0 <= j < peers])  9.27 us
    all_to_all x1, starting transfers between devices, body(): above = lax.all_to_all(totals, 'lev', 0, 0)  7 us
    pallas_call x1, Pallas kernels, body(): call(solve_kernel, [((8, NLON), F32, vmem()), ((peers, NBLK, BLK), BF16,...  4.32 us
  transfers between devices with their start and end apart: 8, of which 3 were waited for; matrix products, arithmetic and copies ran while one was open for 0% of the time, Pallas kernels for 14%

profile of v2, /device:TPU:333, one launch (start us, length us, event | category | flops | bytes accessed | tf_op | source)
XLA Modules:
  0.0 94.3 jit_solution(6283250259613083225)
XLA Ops:
  0.0 1.0 %copy-done.4 = bf16[4,4,8192]{2,1,0:T(4,128)(2,1)S(1)} copy-done((bf16[4,4,8192]{2,1,0:T(4,128)(2,1)S(1)}, bf16[4,4,8192]{2,1,0:T(4,128)(2,1)}, u32[]{:S(2)}) %copy-start.4) | copy-done | bytes 262168
  1.9 1.0 %copy-done.8 = s32[12,8192]{1,0:T(8,128)S(1)} copy-done((s32[12,8192]{1,0:T(8,128)S(1)}, s32[12,8192]{1,0:T(8,128)}, u32[]{:S(2)}) %copy-start.8) | copy-done | bytes 393240
  2.9 0.9 %copy-done.9 = bf16[12,8192]{1,0:T(8,128)(2,1)S(1)} copy-done((bf16[12,8192]{1,0:T(8,128)(2,1)S(1)}, bf16[12,8192]{1,0:T(8,128)(2,1)}, u32[]{:S(2)}) %copy-start.9) | copy-done | bytes 196632
  5.2 2.0 %shard_map.73 = (s32[64]{0:T(128)S(1)}, bf16[25,32,128]{2,1,0:T(8,128)(2,1)S(1)}, bf16[32,16,128]{2,1,0:T(8,128)(2,1)S(1)}, bf16[90,16,128]{2,1,0:T(8,128)(2,1)S...) custom-call(s32[1]{0:T(128)} %bitcast.me, ...), custom_call_target="tpu_custom_call" | custom-call | flops 1000000 | bytes 3000000 | tf_op jit(solution)/shard_map/pallas_call | solution.py:478
  7.2 2.8 %collective-permute-start = (bf16[114,16,128]{2,1,0:T(8,128)(2,1)S(1)}, bf16[114,16,128]{2,1,0:T(8,128)(2,1)S(1)}, u32[]{:S(2)}, u32[]{:S(2)}) collective-permute-start(bf16[114,16,128]{2,1,0:T(8,128)(2,1)S(1)} %get-tuple-element.28), channel_id=1, source_target_pairs={{0,16},{8,24},{16,32},{24,40},{32,48},{40,56},{48,64},{56,72},{64,... | collective-permute-start | bytes 1400840 | tf_op jit(solution)/shard_map/ppermute | solution.py:426
  10.1 2.5 %collective-permute-start.1 = (bf16[114,16,128]{2,1,0:T(8,128)(2,1)S(1)}, bf16[114,16,128]{2,1,0:T(8,128)(2,1)S(1)}, u32[]{:S(2)}, u32[]{:S(2)}) collective-permute-start(bf16[114,16,128]{2,1,0:T(8,128)(2,1)S(1)} %get-tuple-element.29), channel_id=1, source_target_pairs={{16,0},{24,8},{32,16},{40,24},{48,32},{56,40},{64,48},{72,56},{80,... | collective-permute-start | bytes 1400840 | tf_op jit(solution)/shard_map/ppermute | solution.py:426
  12.5 8.2 %collective-permute-done.refs_1_.plus = bf16[114,16,128]{2,1,0:T(8,128)(2,1)S(1)} collective-permute-done((bf16[114,16,128]{2,1,0:T(8,128)(2,1)S(1)}, bf16[114,16,128]{2,1,0:T(8,128)(2,1)S(1)}, u32[]{:S(2)}, u32[]{:S(2)}) %collective-permute-start) | collective-permute-done | bytes 466976 | tf_op jit(solution)/shard_map/ppermute | solution.py:426
  20.7 2.5 %collective-permute-done.1.refs_2_.minus = bf16[114,16,128]{2,1,0:T(8,128)(2,1)S(1)} collective-permute-done((bf16[114,16,128]{2,1,0:T(8,128)(2,1)S(1)}, bf16[114,16,128]{2,1,0:T(8,128)(2,1)S(1)}, u32[]{:S(2)}, u32[]{:S(2)}) %collective-permute-start.1) | collective-permute-done | bytes 466976 | tf_op jit(solution)/shard_map/ppermute | solution.py:426
  23.5 3.8 %collective-permute-start.3 = (bf16[236,16,128]{2,1,0:T(8,128)(2,1)S(1)}, bf16[236,16,128]{2,1,0:T(8,128)(2,1)S(1)}, u32[]{:S(2)}, u32[]{:S(2)}) collective-permute-start(bf16[236,16,128]{2,1,0:T(8,128)(2,1)S(1)} %shard_map.75), channel_id=1, source_target_pairs={{0,8},{8,0},{16,24},{24,16},{32,40},{40,32},{48,56},{56,48},{64,72... | collective-permute-start | bytes 2899976 | tf_op jit(solution)/shard_map/ppermute | solution.py:430
  27.3 2.1 %collective-permute-done.3.refs_0_.refs_1_.refs_2_.mate = bf16[236,16,128]{2,1,0:T(8,128)(2,1)S(1)} collective-permute-done((bf16[236,16,128]{2,1,0:T(8,128)(2,1)S(1)}, bf16[236,16,128]{2,1,0:T(8,128)(2,1)S(1)}, u32[]{:S(2)}, u32[]{:S(2)}) %collective-permute-start.3) | collective-permute-done | bytes 966688 | tf_op jit(solution)/shard_map/ppermute | solution.py:430
  29.4 0.9 %copy-done.5 = bf16[4,4,8192]{2,1,0:T(4,128)(2,1)S(1)} copy-done((bf16[4,4,8192]{2,1,0:T(4,128)(2,1)S(1)}, bf16[4,4,8192]{2,1,0:T(4,128)(2,1)}, u32[]{:S(2)}) %copy-start.5) | copy-done | bytes 262168
  31.3 4.3 %shard_map.77 = (f32[8,4096]{1,0:T(8,128)S(1)}, bf16[8,64,128]{2,1,0:T(8,128)(2,1)}, bf16[128,128]{1,0:T(8,128)(2,1)S(1)}, bf16[64,128]{1,0:T(8,128)(2,1)S(1)}, ...) custom-call(s32[1]{0:T(128)} %bitcast.me, s32[64]{0:T(128)S(1)} %get-tuple-element.41.slots, ...), custom_call_target="tpu_custom_call" | custom-call | flops 2000000 | bytes 6000000 | tf_op jit(solution)/shard_map/pallas_call | solution.py:521
  35.6 7.0 %all-to-all-start = ((bf16[8,64,128]{2,1,0:T(8,128)(2,1)}), bf16[8,64,128]{2,1,0:T(8,128)(2,1)S(1)}, u32[]{:S(2)}, u32[]{:S(2)}) async-start(bf16[8,64,128]{2,1,0:T(8,128)(2,1)} %get-tuple-element.48), calls=%async_computation | async-start | bytes 262144 | tf_op jit(solution)/shard_map/all_to_all | solution.py:552
  42.6 4.3 %collective-permute-start.2 = (bf16[41,16,128]{2,1,0:T(8,128)(2,1)S(1)}, bf16[41,16,128]{2,1,0:T(8,128)(2,1)S(1)}, u32[]{:S(2)}, u32[]{:S(2)}) collective-permute-start(bf16[41,16,128]{2,1,0:T(8,128)(2,1)S(1)} %get-tuple-element.30), channel_id=1, source_target_pairs={{8,32},{24,48},{32,8},{40,64},{48,24},{56,80},{64,40},{72,96},{80,... | collective-permute-start | bytes 503816 | tf_op jit(solution)/shard_map/ppermute | solution.py:436
  46.9 3.6 %collective-permute-start.4 = (bf16[128,128]{1,0:T(8,128)(2,1)S(1)}, bf16[128,128]{1,0:T(8,128)(2,1)S(1)}, u32[]{:S(2)}, u32[]{:S(2)}) collective-permute-start(bf16[128,128]{1,0:T(8,128)(2,1)S(1)} %get-tuple-element.44), channel_id=1, source_target_pairs={{0,16},{8,24},{16,32},{24,40},{32,48},{40,56},{48,64},{56,72},{64,... | collective-permute-start | bytes 98312 | tf_op jit(solution)/shard_map/ppermute | solution.py:426
  50.5 3.1 %collective-permute-start.5 = (bf16[128,128]{1,0:T(8,128)(2,1)S(1)}, bf16[128,128]{1,0:T(8,128)(2,1)S(1)}, u32[]{:S(2)}, u32[]{:S(2)}) collective-permute-start(bf16[128,128]{1,0:T(8,128)(2,1)S(1)} %get-tuple-element.45), channel_id=1, source_target_pairs={{16,0},{24,8},{32,16},{40,24},{48,32},{56,40},{64,48},{72,56},{80,... | collective-permute-start | bytes 98312 | tf_op jit(solution)/shard_map/ppermute | solution.py:426
  53.6 5.0 %collective-permute-start.6 = (bf16[64,128]{1,0:T(8,128)(2,1)S(1)}, bf16[64,128]{1,0:T(8,128)(2,1)S(1)}, u32[]{:S(2)}, u32[]{:S(2)}) collective-permute-start(bf16[64,128]{1,0:T(8,128)(2,1)S(1)} %get-tuple-element.46), channel_id=1, source_target_pairs={{8,32},{24,48},{32,8},{40,64},{48,24},{56,80},{64,40},{72,96},{80,... | collective-permute-start | bytes 49160 | tf_op jit(solution)/shard_map/ppermute | solution.py:436
  58.6 7.8 %shard_map.74 = (bf16[160,256,128]{2,1,0:T(8,128)(2,1)S(1)}, s32[168]{0:T(256)S(1)}, s32[168]{0:T(256)S(1)}, s32[1]{0:T(128)}) custom-call(bf16[25,32,128]{2,1,0:T(8,128)(2,1)S(1)} %get-tuple-element.27.refs_0_, bf16[114,16,128]{2,1,0:T(8,128)(2,1)S(1)} %collective-permute-done.refs_1_.plus, bf16[114,16,128]{2,1,0:T(8,128)(2,1)S(1)} %collective-permute-done.1.refs_2_.minus, ...), custom_call_target="tpu_custom_call" | custom-call | flops 4000000 | bytes 12000000 | tf_op jit(solution)/shard_map/pallas_call | solution.py:442
  66.4 4.0 %copy-done = bf16[160,256,128]{2,1,0:T(8,128)(2,1)} copy-done((bf16[160,256,128]{2,1,0:T(8,128)(2,1)}, bf16[160,256,128]{2,1,0:T(8,128)(2,1)S(1)}, u32[]{:S(2)}) %copy-start) | copy-done | bytes 10485784
  70.4 5.0 %shard_map.76 = (bf16[96,256,128]{2,1,0:T(8,128)(2,1)S(1)}, s32[104]{0:T(128)S(1)}, s32[104]{0:T(128)S(1)}, s32[1]{0:T(128)}) custom-call(bf16[236,16,128]{2,1,0:T(8,128)(2,1)S(1)} %collective-permute-done.3.refs_0_.refs_1_.refs_2_.mate, bf16[236,16,128]{2,1,0:T(8,128)(2,1)S(1)} %collective-permute-done.3.refs_0_.refs_1_.refs_2_.mate, ...), custom_call_target="tpu_custom_call" | custom-call | flops 4000000 | bytes 12000000 | tf_op jit(solution)/shard_map/pallas_call | solution.py:442
  75.4 2.6 %copy-done.2 = bf16[96,256,128]{2,1,0:T(8,128)(2,1)} copy-done((bf16[96,256,128]{2,1,0:T(8,128)(2,1)}, bf16[96,256,128]{2,1,0:T(8,128)(2,1)S(1)}, u32[]{:S(2)}) %copy-start.2) | copy-done | bytes 6291480
  78.1 4.0 %copy-done.1 = bf16[160,256,128]{2,1,0:T(8,128)(2,1)S(1)} copy-done((bf16[160,256,128]{2,1,0:T(8,128)(2,1)S(1)}, bf16[160,256,128]{2,1,0:T(8,128)(2,1)}, u32[]{:S(2)}) %copy-start.1) | copy-done | bytes 10485784
  82.0 2.8 %copy-done.3 = bf16[96,256,128]{2,1,0:T(8,128)(2,1)S(1)} copy-done((bf16[96,256,128]{2,1,0:T(8,128)(2,1)S(1)}, bf16[96,256,128]{2,1,0:T(8,128)(2,1)}, u32[]{:S(2)}) %copy-start.3) | copy-done | bytes 6291480
  84.8 9.5 %shard_map.78 = f32[4,4,8192]{2,1,0:T(4,128)} custom-call(s32[1]{0:T(128)} %bitcast.me, s32[1]{0:T(128)} %bitcast.1.lev, f32[4]{0:T(128)S(1)} %copy-done.12, s32[168]{0:T(256)S(1)} %get-tuple-element.31.slot1, s32[168]{0:T(256)S(1)} %get-tuple-element.32.win1, s32[1]{0:T(128)} %get-tuple-element.33.count1, bf16[160,256,128]{2,1,0:T(8,128)(2,1)S(1)} %copy-done.1, ...), custom_call_target="tpu_custom_call" | custom-call | flops 4000000 | bytes 12000000 | tf_op jit(solution)/shard_map/pallas_call | solution.py:567
  (24 shorter events, 3.5 us)
Async XLA Ops:
  0.0 78.0 %copy-start.12 = (f32[4]{0:T(128)S(1)}, f32[4]{0:T(128)}, u32[]{:S(2)}) copy-start(f32[4]{0:T(128)} %geo_in.1) | copy-start | bytes 52
  0.0 1.0 %copy-start.4 = (bf16[4,4,8192]{2,1,0:T(4,128)(2,1)S(1)}, bf16[4,4,8192]{2,1,0:T(4,128)(2,1)}, u32[]{:S(2)}) copy-start(bf16[4,4,8192]{2,1,0:T(4,128)(2,1)} %adj_in.3) | copy-start | bytes 786436
  1.0 0.9 copy-start.6
  1.9 1.0 %copy-start.8 = (s32[12,8192]{1,0:T(8,128)S(1)}, s32[12,8192]{1,0:T(8,128)}, u32[]{:S(2)}) copy-start(s32[12,8192]{1,0:T(8,128)} %cell_in.1) | copy-start | bytes 1179652
  2.9 0.9 %copy-start.9 = (bf16[12,8192]{1,0:T(8,128)(2,1)S(1)}, bf16[12,8192]{1,0:T(8,128)(2,1)}, u32[]{:S(2)}) copy-start(bf16[12,8192]{1,0:T(8,128)(2,1)} %weight_in.1) | copy-start | bytes 589828
  3.9 0.7 copy-start.10
  4.5 0.7 copy-start.11
  7.2 13.5 %collective-permute-start = (bf16[114,16,128]{2,1,0:T(8,128)(2,1)S(1)}, bf16[114,16,128]{2,1,0:T(8,128)(2,1)S(1)}, u32[]{:S(2)}, u32[]{:S(2)}) collective-permute-start(bf16[114,16,128]{2,1,0:T(8,128)(2,1)S(1)} %get-tuple-element.28), channel_id=1, source_target_pairs={{0,16},{8,24},{16,32},{24,40},{32,48},{40,56},{48,64},{56,72},{64,... | collective-permute-start | bytes 1400840 | tf_op jit(solution)/shard_map/ppermute | solution.py:426
  10.1 13.1 %collective-permute-start.1 = (bf16[114,16,128]{2,1,0:T(8,128)(2,1)S(1)}, bf16[114,16,128]{2,1,0:T(8,128)(2,1)S(1)}, u32[]{:S(2)}, u32[]{:S(2)}) collective-permute-start(bf16[114,16,128]{2,1,0:T(8,128)(2,1)S(1)} %get-tuple-element.29), channel_id=1, source_target_pairs={{16,0},{24,8},{32,16},{40,24},{48,32},{56,40},{64,48},{72,56},{80,... | collective-permute-start | bytes 1400840 | tf_op jit(solution)/shard_map/ppermute | solution.py:426
  23.5 5.9 %collective-permute-start.3 = (bf16[236,16,128]{2,1,0:T(8,128)(2,1)S(1)}, bf16[236,16,128]{2,1,0:T(8,128)(2,1)S(1)}, u32[]{:S(2)}, u32[]{:S(2)}) collective-permute-start(bf16[236,16,128]{2,1,0:T(8,128)(2,1)S(1)} %shard_map.75), channel_id=1, source_target_pairs={{0,8},{8,0},{16,24},{24,16},{32,40},{40,32},{48,56},{56,48},{64,72... | collective-permute-start | bytes 2899976 | tf_op jit(solution)/shard_map/ppermute | solution.py:430
  29.4 0.9 %copy-start.5 = (bf16[4,4,8192]{2,1,0:T(4,128)(2,1)S(1)}, bf16[4,4,8192]{2,1,0:T(4,128)(2,1)}, u32[]{:S(2)}) copy-start(bf16[4,4,8192]{2,1,0:T(4,128)(2,1)} %adj_in.3) | copy-start | bytes 786436
  30.4 0.9 copy-start.7
  35.6 42.4 %all-to-all-start = ((bf16[8,64,128]{2,1,0:T(8,128)(2,1)}), bf16[8,64,128]{2,1,0:T(8,128)(2,1)S(1)}, u32[]{:S(2)}, u32[]{:S(2)}) async-start(bf16[8,64,128]{2,1,0:T(8,128)(2,1)} %get-tuple-element.48), calls=%async_computation | async-start | bytes 262144 | tf_op jit(solution)/shard_map/all_to_all | solution.py:552
  42.6 15.9 %collective-permute-start.2 = (bf16[41,16,128]{2,1,0:T(8,128)(2,1)S(1)}, bf16[41,16,128]{2,1,0:T(8,128)(2,1)S(1)}, u32[]{:S(2)}, u32[]{:S(2)}) collective-permute-start(bf16[41,16,128]{2,1,0:T(8,128)(2,1)S(1)} %get-tuple-element.30), channel_id=1, source_target_pairs={{8,32},{24,48},{32,8},{40,64},{48,24},{56,80},{64,40},{72,96},{80,... | collective-permute-start | bytes 503816 | tf_op jit(solution)/shard_map/ppermute | solution.py:436
  46.9 31.1 %collective-permute-start.4 = (bf16[128,128]{1,0:T(8,128)(2,1)S(1)}, bf16[128,128]{1,0:T(8,128)(2,1)S(1)}, u32[]{:S(2)}, u32[]{:S(2)}) collective-permute-start(bf16[128,128]{1,0:T(8,128)(2,1)S(1)} %get-tuple-element.44), channel_id=1, source_target_pairs={{0,16},{8,24},{16,32},{24,40},{32,48},{40,56},{48,64},{56,72},{64,... | collective-permute-start | bytes 98312 | tf_op jit(solution)/shard_map/ppermute | solution.py:426
  50.5 27.5 %collective-permute-start.5 = (bf16[128,128]{1,0:T(8,128)(2,1)S(1)}, bf16[128,128]{1,0:T(8,128)(2,1)S(1)}, u32[]{:S(2)}, u32[]{:S(2)}) collective-permute-start(bf16[128,128]{1,0:T(8,128)(2,1)S(1)} %get-tuple-element.45), channel_id=1, source_target_pairs={{16,0},{24,8},{32,16},{40,24},{48,32},{56,40},{64,48},{72,56},{80,... | collective-permute-start | bytes 98312 | tf_op jit(solution)/shard_map/ppermute | solution.py:426
  53.6 24.4 %collective-permute-start.6 = (bf16[64,128]{1,0:T(8,128)(2,1)S(1)}, bf16[64,128]{1,0:T(8,128)(2,1)S(1)}, u32[]{:S(2)}, u32[]{:S(2)}) collective-permute-start(bf16[64,128]{1,0:T(8,128)(2,1)S(1)} %get-tuple-element.46), channel_id=1, source_target_pairs={{8,32},{24,48},{32,8},{40,64},{48,24},{56,80},{64,40},{72,96},{80,... | collective-permute-start | bytes 49160 | tf_op jit(solution)/shard_map/ppermute | solution.py:436
  66.4 4.0 %copy-start = (bf16[160,256,128]{2,1,0:T(8,128)(2,1)}, bf16[160,256,128]{2,1,0:T(8,128)(2,1)S(1)}, u32[]{:S(2)}) copy-start(bf16[160,256,128]{2,1,0:T(8,128)(2,1)S(1)} %get-tuple-element.34.mats1) | copy-start | bytes 31457284
  75.4 2.6 %copy-start.2 = (bf16[96,256,128]{2,1,0:T(8,128)(2,1)}, bf16[96,256,128]{2,1,0:T(8,128)(2,1)S(1)}, u32[]{:S(2)}) copy-start(bf16[96,256,128]{2,1,0:T(8,128)(2,1)S(1)} %get-tuple-element.39.mats2) | copy-start | bytes 18874372
  78.1 4.0 %copy-start.1 = (bf16[160,256,128]{2,1,0:T(8,128)(2,1)S(1)}, bf16[160,256,128]{2,1,0:T(8,128)(2,1)}, u32[]{:S(2)}) copy-start(bf16[160,256,128]{2,1,0:T(8,128)(2,1)} %copy-done) | copy-start | bytes 31457284
  82.0 2.8 %copy-start.3 = (bf16[96,256,128]{2,1,0:T(8,128)(2,1)S(1)}, bf16[96,256,128]{2,1,0:T(8,128)(2,1)}, u32[]{:S(2)}) copy-start(bf16[96,256,128]{2,1,0:T(8,128)(2,1)} %copy-done.2) | copy-start | bytes 18874372

commit v3 on v2

--- a/solution.py
+++ b/solution.py
@@ -43,8 +43,16 @@
     return pl.BlockSpec(memory_space=pltpu.SMEM)
 
 
+def free():
+    return pl.BlockSpec(memory_space=pl.ANY)
+
+
 def hbm():
-    return pl.BlockSpec(memory_space=pl.ANY)
+    return pl.BlockSpec(memory_space=pltpu.HBM)
+
+
+def kept(array):
+    return pltpu.with_memory_space_constraint(array, pltpu.HBM)
 
 
 def lanes(i):
@@ -74,8 +82,8 @@
 def call(kernel, outs, ins, scratch, cost, limit):
     return pl.pallas_call(
         kernel,
-        out_shape=[jax.ShapeDtypeStruct(shape, dtype) for shape, dtype, _ in outs],
-        out_specs=[spec for _, _, spec in outs],
+        out_shape=[(out[3] if out[3:] else jax.ShapeDtypeStruct)(out[0], out[1]) for out in outs],
+        out_specs=[out[2] for out in outs],
         in_specs=ins,
         scratch_shapes=scratch,
         compiler_params=pltpu.CompilerParams(vmem_limit_bytes=limit << 20),
@@ -149,14 +157,13 @@
 
 
 def solve_kernel(
-    me, slots, adj_in, helm_in, own, plus, minus, mate,
+    me, slots, _, helm_in, own, plus, minus, mate,
     local, totals, f_home, f_mate, f_plus, f_minus, f_cross,
-    adj, helm, halo, lows, rhs, coef, result, table, table_s, mine_all, mate_all, t_all, sems, table_sem,
+    helm, halo, lows, rhs, coef, result, table, table_s, mine_all, mate_all, t_all, sems, table_sem,
 ):
     core = lax.rem(me[0], 2)
-    tables = launch([(mate.at[pl.ds(HALO, LOWS + 1)], lows, sems.at[8])])
+    tables = launch([(mate.at[pl.ds(HALO, LOWS + 1)], lows, sems.at[7])])
     pairs = (
-        (adj_in.at[0], adj),
         (helm_in, helm),
         (plus.at[pl.ds(0, HALO)], halo.at[core]),
         (mate.at[pl.ds(OWN, HALO)], halo.at[1 - core]),
@@ -442,12 +449,12 @@
     return call(
         lambda *refs: matrix_kernel(count, len(home), [at for _, at in parts], *refs),
         [
-            ((entries, WIN, BLK), BF16, hbm()),
+            ((entries, WIN, BLK), BF16, hbm(), pltpu.HBM),
             ((entries + 8,), jnp.int32, smem()),
             ((entries + 8,), jnp.int32, smem()),
             ((1,), jnp.int32, smem()),
         ],
-        [vmem()] * len(home) + [hbm()] * len(parts),
+        [vmem()] * len(home) + [free()] * len(parts),
         [
             pltpu.VMEM((len(parts), ROUTE, 16, BLK), BF16),
             pltpu.VMEM((STEN, count, BLK), F32),
@@ -501,15 +508,15 @@
         ],
         1,
         24,
-    )(me, dest_tile[:, 0], src_window, adj_in, helm_coef, src_cell, interp_w)
+    )(me, *map(kept, (dest_tile[:, 0], src_window, adj_in, helm_coef, src_cell, interp_w)))
     plus = moved(plus, 2)
     minus = moved(minus, -2)
     cross = crossed(cross)
 
     relayed = call(
         relay_kernel,
-        [((OWN + 2 * RELAY, 16, BLK), BF16, hbm())],
-        [hbm()] * 3,
+        [((OWN + 2 * RELAY, 16, BLK), BF16, free())],
+        [free()] * 3,
         [pltpu.SemaphoreType.DMA((3,))],
         1,
         16,
@@ -529,9 +536,8 @@
             strip(2 * OFFCAP),
             strip(OFFCAP),
         ],
-        [smem()] * 2 + [hbm()] * 6,
+        [smem()] * 3 + [hbm()] + [free()] * 4,
         [
-            pltpu.VMEM(adj_in.shape[1:], BF16),
             pltpu.VMEM(helm_coef.shape, F32),
             pltpu.VMEM((6, HALO, 16, BLK), BF16),
             pltpu.VMEM((LOWS + 1, 16, BLK), BF16),
@@ -543,12 +549,12 @@
             pltpu.VMEM((SLOTS * 4, BLK), F32),
             pltpu.VMEM((SLOTS * 4, BLK), F32),
             pltpu.VMEM((NBLK, BLK), F32),
-            pltpu.SemaphoreType.DMA((9,)),
+            pltpu.SemaphoreType.DMA((8,)),
             pltpu.SemaphoreType.DMA,
         ],
         2,
         24,
-    )(me, slots, adj_in, helm_coef, own, plus, minus, mate)
+    )(me, slots, early[3], kept(helm_coef), own, plus, minus, mate)
     above = lax.all_to_all(totals, "lev", 0, 0)
     f_plus = moved(f_plus, 2)
     f_minus = moved(f_minus, -2)
@@ -561,13 +567,13 @@
 
     def lists(found):
         mats, entry_slot, entry_win, entry_count = found
-        return entry_slot, entry_win, entry_count, mats
+        return entry_slot, entry_win, entry_count, kept(mats)
 
     listed = [smem()] * 3 + [hbm()]
     return call(
         spread_kernel,
         [((4, 4, CELLS), F32, vmem())],
-        [smem()] * 2 + [hbm()] + listed * 2 + [hbm()] * 5 + [vmem()] * 7,
+        [smem()] * 2 + [hbm()] + listed * 2 + [free()] * 5 + [vmem()] * 7,
         [
             pltpu.SMEM((4,), F32),
             pltpu.VMEM((SLOTS, 16, BLK), BF16),
@@ -580,7 +586,7 @@
         4,
         24,
     )(
-        me, lev, geo_coef, *lists(early), *lists(late),
+        me, lev, kept(geo_coef), *lists(early), *lists(late),
         b_home, plus, minus, cross, mate, f_home, f_mate, f_plus, f_minus, f_cross, local, above,
     )[0]
 

time: 94.9 us -> 85.3 us (0.90)
  the two profiles are of different devices: /device:TPU:333 before, /device:TPU:207 now
where the time goes in v3:
time: 85.3 us; the launch traced here: 84.8 us
  starting transfers between devices  31.2 us (37%)
  Pallas kernels  30.5 us (36%)
  waiting for transfers between devices  22.9 us (27%)
    ppermute x4, waiting for transfers between devices, moved(): lax.ppermute(parcel, 'tile', [(i, i + by) for i in range(peers) if 0 <= i...  14.5 us
    pallas_call x2, Pallas kernels, matrices(): call(lambda *refs: matrix_kernel(count, len(home), [at for _, at in parts...  14.3 us
    ppermute x4, starting transfers between devices, moved(): lax.ppermute(parcel, 'tile', [(i, i + by) for i in range(peers) if 0 <= i...  12.3 us
    pallas_call x1, Pallas kernels, body(): call(spread_kernel, [((4, 4, CELLS), F32, vmem())], [smem()] * 2 + [hbm()...  8.52 us
    ppermute x2, waiting for transfers between devices, crossed(): lax.ppermute(parcel, 'tile', [(i, j) for i, j in pairs if 0 <= j < peers])  8.37 us
    ppermute x2, starting transfers between devices, crossed(): lax.ppermute(parcel, 'tile', [(i, j) for i, j in pairs if 0 <= j < peers])  8.14 us
    all_to_all x1, starting transfers between devices, body(): above = lax.all_to_all(totals, 'lev', 0, 0)  7 us
    pallas_call x1, Pallas kernels, body(): call(solve_kernel, [((8, NLON), F32, vmem()), ((peers, NBLK, BLK), BF16,...  4.62 us
  transfers between devices with their start and end apart: 8, of which 3 were waited for; matrix products, arithmetic and copies ran while one was open for 0% of the time, Pallas kernels for 17%

profile of v3, /device:TPU:207, one launch (start us, length us, event | category | flops | bytes accessed | tf_op | source)
XLA Modules:
  0.0 84.8 jit_solution(17524246210612593319)
XLA Ops:
  0.0 2.7 %shard_map.73 = (s32[64]{0:T(128)S(1)}, bf16[25,32,128]{2,1,0:T(8,128)(2,1)S(1)}, bf16[32,16,128]{2,1,0:T(8,128)(2,1)S(1)}, bf16[90,16,128]{2,1,0:T(8,128)(2,1)S...) custom-call(s32[1]{0:T(128)} %bitcast.me, s32[64]{0:T(128)} %bitcast.3, ...), custom_call_target="tpu_custom_call" | custom-call | flops 1000000 | bytes 3000000 | tf_op jit(solution)/shard_map/pallas_call | solution.py:485
  2.7 5.1 %collective-permute-start = (bf16[114,16,128]{2,1,0:T(8,128)(2,1)S(1)}, bf16[114,16,128]{2,1,0:T(8,128)(2,1)S(1)}, u32[]{:S(2)}, u32[]{:S(2)}) collective-permute-start(bf16[114,16,128]{2,1,0:T(8,128)(2,1)S(1)} %get-tuple-element.28), channel_id=1, source_target_pairs={{0,16},{8,24},{16,32},{24,40},{32,48},{40,56},{48,64},{56,72},{64,... | collective-permute-start | bytes 1400840 | tf_op jit(solution)/shard_map/ppermute | solution.py:433
  7.9 1.9 %collective-permute-start.1 = (bf16[114,16,128]{2,1,0:T(8,128)(2,1)S(1)}, bf16[114,16,128]{2,1,0:T(8,128)(2,1)S(1)}, u32[]{:S(2)}, u32[]{:S(2)}) collective-permute-start(bf16[114,16,128]{2,1,0:T(8,128)(2,1)S(1)} %get-tuple-element.29), channel_id=1, source_target_pairs={{16,0},{24,8},{32,16},{40,24},{48,32},{56,40},{64,48},{72,56},{80,... | collective-permute-start | bytes 1400840 | tf_op jit(solution)/shard_map/ppermute | solution.py:433
  9.8 7.4 %collective-permute-done.refs_1_.plus = bf16[114,16,128]{2,1,0:T(8,128)(2,1)S(1)} collective-permute-done((bf16[114,16,128]{2,1,0:T(8,128)(2,1)S(1)}, bf16[114,16,128]{2,1,0:T(8,128)(2,1)S(1)}, u32[]{:S(2)}, u32[]{:S(2)}) %collective-permute-start) | collective-permute-done | bytes 466976 | tf_op jit(solution)/shard_map/ppermute | solution.py:433
  17.2 7.1 %collective-permute-done.1.refs_2_.minus = bf16[114,16,128]{2,1,0:T(8,128)(2,1)S(1)} collective-permute-done((bf16[114,16,128]{2,1,0:T(8,128)(2,1)S(1)}, bf16[114,16,128]{2,1,0:T(8,128)(2,1)S(1)}, u32[]{:S(2)}, u32[]{:S(2)}) %collective-permute-start.1) | collective-permute-done | bytes 466976 | tf_op jit(solution)/shard_map/ppermute | solution.py:433
  24.3 0.3 shard_map.75
  24.7 3.8 %collective-permute-start.3 = (bf16[236,16,128]{2,1,0:T(8,128)(2,1)S(1)}, bf16[236,16,128]{2,1,0:T(8,128)(2,1)S(1)}, u32[]{:S(2)}, u32[]{:S(2)}) collective-permute-start(bf16[236,16,128]{2,1,0:T(8,128)(2,1)S(1)} %shard_map.75), channel_id=1, source_target_pairs={{0,8},{8,0},{16,24},{24,16},{32,40},{40,32},{48,56},{56,48},{64,72... | collective-permute-start | bytes 2899976 | tf_op jit(solution)/shard_map/ppermute | solution.py:437
  28.4 1.9 %collective-permute-start.2 = (bf16[41,16,128]{2,1,0:T(8,128)(2,1)S(1)}, bf16[41,16,128]{2,1,0:T(8,128)(2,1)S(1)}, u32[]{:S(2)}, u32[]{:S(2)}) collective-permute-start(bf16[41,16,128]{2,1,0:T(8,128)(2,1)S(1)} %get-tuple-element.30), channel_id=1, source_target_pairs={{8,32},{24,48},{32,8},{40,64},{48,24},{56,80},{64,40},{72,96},{80,... | collective-permute-start | bytes 503816 | tf_op jit(solution)/shard_map/ppermute | solution.py:443
  30.4 8.4 %collective-permute-done.2.refs_3_.cross = bf16[41,16,128]{2,1,0:T(8,128)(2,1)S(1)} collective-permute-done((bf16[41,16,128]{2,1,0:T(8,128)(2,1)S(1)}, bf16[41,16,128]{2,1,0:T(8,128)(2,1)S(1)}, u32[]{:S(2)}, u32[]{:S(2)}) %collective-permute-start.2) | collective-permute-done | bytes 167968 | tf_op jit(solution)/shard_map/ppermute | solution.py:443
  38.7 8.7 %shard_map.74 = (bf16[160,256,128]{2,1,0:T(8,128)(2,1)}, s32[168]{0:T(256)S(1)}, s32[168]{0:T(256)S(1)}, s32[1]{0:T(128)}) custom-call(bf16[25,32,128]{2,1,0:T(8,128)(2,1)S(1)} %get-tuple-element.27.refs_0_, bf16[114,16,128]{2,1,0:T(8,128)(2,1)S(1)} %collective-permute-done.refs_1_.plus, bf16[114,16,128]{2,1,0:T(8,128)(2,1)S(1)} %collective-permute-done.1.refs_2_.minus, ...), custom_call_target="tpu_custom_call" | custom-call | flops 4000000 | bytes 12000000 | tf_op jit(solution)/shard_map/pallas_call | solution.py:449
  47.4 0.0 collective-permute-done.3.refs_0_.refs_1_.refs_2_.mate
  47.5 4.6 %shard_map.77 = (f32[8,4096]{1,0:T(8,128)S(1)}, bf16[8,64,128]{2,1,0:T(8,128)(2,1)}, bf16[128,128]{1,0:T(8,128)(2,1)S(1)}, bf16[64,128]{1,0:T(8,128)(2,1)S(1)}, ...) custom-call(s32[1]{0:T(128)} %bitcast.me, s32[64]{0:T(128)S(1)} %get-tuple-element.41.slots, ...), custom_call_target="tpu_custom_call" | custom-call | flops 2000000 | bytes 6000000 | tf_op jit(solution)/shard_map/pallas_call | solution.py:528
  52.1 7.0 %all-to-all-start = ((bf16[8,64,128]{2,1,0:T(8,128)(2,1)}), bf16[8,64,128]{2,1,0:T(8,128)(2,1)S(1)}, u32[]{:S(2)}, u32[]{:S(2)}) async-start(bf16[8,64,128]{2,1,0:T(8,128)(2,1)} %get-tuple-element.48), calls=%async_computation | async-start | bytes 262144 | tf_op jit(solution)/shard_map/all_to_all | solution.py:558
  59.1 1.9 %collective-permute-start.4 = (bf16[128,128]{1,0:T(8,128)(2,1)S(1)}, bf16[128,128]{1,0:T(8,128)(2,1)S(1)}, u32[]{:S(2)}, u32[]{:S(2)}) collective-permute-start(bf16[128,128]{1,0:T(8,128)(2,1)S(1)} %get-tuple-element.44), channel_id=1, source_target_pairs={{0,16},{8,24},{16,32},{24,40},{32,48},{40,56},{48,64},{56,72},{64,... | collective-permute-start | bytes 98312 | tf_op jit(solution)/shard_map/ppermute | solution.py:433
  61.0 3.4 %collective-permute-start.5 = (bf16[128,128]{1,0:T(8,128)(2,1)S(1)}, bf16[128,128]{1,0:T(8,128)(2,1)S(1)}, u32[]{:S(2)}, u32[]{:S(2)}) collective-permute-start(bf16[128,128]{1,0:T(8,128)(2,1)S(1)} %get-tuple-element.45), channel_id=1, source_target_pairs={{16,0},{24,8},{32,16},{40,24},{48,32},{56,40},{64,48},{72,56},{80,... | collective-permute-start | bytes 98312 | tf_op jit(solution)/shard_map/ppermute | solution.py:433
  64.4 6.2 %collective-permute-start.6 = (bf16[64,128]{1,0:T(8,128)(2,1)S(1)}, bf16[64,128]{1,0:T(8,128)(2,1)S(1)}, u32[]{:S(2)}, u32[]{:S(2)}) collective-permute-start(bf16[64,128]{1,0:T(8,128)(2,1)S(1)} %get-tuple-element.46), channel_id=1, source_target_pairs={{8,32},{24,48},{32,8},{40,64},{48,24},{56,80},{64,40},{72,96},{80,... | collective-permute-start | bytes 49160 | tf_op jit(solution)/shard_map/ppermute | solution.py:443
  70.6 5.6 %shard_map.76 = (bf16[96,256,128]{2,1,0:T(8,128)(2,1)}, s32[104]{0:T(128)S(1)}, s32[104]{0:T(128)S(1)}, s32[1]{0:T(128)}) custom-call(bf16[236,16,128]{2,1,0:T(8,128)(2,1)S(1)} %collective-permute-done.3.refs_0_.refs_1_.refs_2_.mate, bf16[236,16,128]{2,1,0:T(8,128)(2,1)S(1)} %collective-permute-done.3.refs_0_.refs_1_.refs_2_.mate, ...), custom_call_target="tpu_custom_call" | custom-call | flops 4000000 | bytes 12000000 | tf_op jit(solution)/shard_map/pallas_call | solution.py:449
  76.2 0.0 collective-permute-done.6.f_cross
  76.2 0.0 collective-permute-done.4.f_plus
  76.2 0.0 collective-permute-done.5.f_minus
  76.3 0.0 all-to-all-done.above
  76.3 8.5 %shard_map.78 = f32[4,4,8192]{2,1,0:T(4,128)} custom-call(s32[1]{0:T(128)} %bitcast.me, s32[1]{0:T(128)} %bitcast.1.lev, f32[4]{0:T(128)} %geo_in.1, s32[168]{0:T(256)S(1)} %get-tuple-element.31.slot1, s32[168]{0:T(256)S(1)} %get-tuple-element.32.win1, s32[1]{0:T(128)} %get-tuple-element.33._.count1, bf16[160,256,128]{2,1,0:T(8,128)(2,1)} %get-tuple-element.34.mats1, ...), custom_call_target="tpu_custom_call" | custom-call | flops 4000000 | bytes 12000000 | tf_op jit(solution)/shard_map/pallas_call | solution.py:573
Async XLA Ops:
  2.7 14.5 %collective-permute-start = (bf16[114,16,128]{2,1,0:T(8,128)(2,1)S(1)}, bf16[114,16,128]{2,1,0:T(8,128)(2,1)S(1)}, u32[]{:S(2)}, u32[]{:S(2)}) collective-permute-start(bf16[114,16,128]{2,1,0:T(8,128)(2,1)S(1)} %get-tuple-element.28), channel_id=1, source_target_pairs={{0,16},{8,24},{16,32},{24,40},{32,48},{40,56},{48,64},{56,72},{64,... | collective-permute-start | bytes 1400840 | tf_op jit(solution)/shard_map/ppermute | solution.py:433
  7.9 16.5 %collective-permute-start.1 = (bf16[114,16,128]{2,1,0:T(8,128)(2,1)S(1)}, bf16[114,16,128]{2,1,0:T(8,128)(2,1)S(1)}, u32[]{:S(2)}, u32[]{:S(2)}) collective-permute-start(bf16[114,16,128]{2,1,0:T(8,128)(2,1)S(1)} %get-tuple-element.29), channel_id=1, source_target_pairs={{16,0},{24,8},{32,16},{40,24},{48,32},{56,40},{64,48},{72,56},{80,... | collective-permute-start | bytes 1400840 | tf_op jit(solution)/shard_map/ppermute | solution.py:433
  24.7 22.8 %collective-permute-start.3 = (bf16[236,16,128]{2,1,0:T(8,128)(2,1)S(1)}, bf16[236,16,128]{2,1,0:T(8,128)(2,1)S(1)}, u32[]{:S(2)}, u32[]{:S(2)}) collective-permute-start(bf16[236,16,128]{2,1,0:T(8,128)(2,1)S(1)} %shard_map.75), channel_id=1, source_target_pairs={{0,8},{8,0},{16,24},{24,16},{32,40},{40,32},{48,56},{56,48},{64,72... | collective-permute-start | bytes 2899976 | tf_op jit(solution)/shard_map/ppermute | solution.py:437
  28.4 10.3 %collective-permute-start.2 = (bf16[41,16,128]{2,1,0:T(8,128)(2,1)S(1)}, bf16[41,16,128]{2,1,0:T(8,128)(2,1)S(1)}, u32[]{:S(2)}, u32[]{:S(2)}) collective-permute-start(bf16[41,16,128]{2,1,0:T(8,128)(2,1)S(1)} %get-tuple-element.30), channel_id=1, source_target_pairs={{8,32},{24,48},{32,8},{40,64},{48,24},{56,80},{64,40},{72,96},{80,... | collective-permute-start | bytes 503816 | tf_op jit(solution)/shard_map/ppermute | solution.py:443
  52.1 24.2 %all-to-all-start = ((bf16[8,64,128]{2,1,0:T(8,128)(2,1)}), bf16[8,64,128]{2,1,0:T(8,128)(2,1)S(1)}, u32[]{:S(2)}, u32[]{:S(2)}) async-start(bf16[8,64,128]{2,1,0:T(8,128)(2,1)} %get-tuple-element.48), calls=%async_computation | async-start | bytes 262144 | tf_op jit(solution)/shard_map/all_to_all | solution.py:558
  59.1 17.2 %collective-permute-start.4 = (bf16[128,128]{1,0:T(8,128)(2,1)S(1)}, bf16[128,128]{1,0:T(8,128)(2,1)S(1)}, u32[]{:S(2)}, u32[]{:S(2)}) collective-permute-start(bf16[128,128]{1,0:T(8,128)(2,1)S(1)} %get-tuple-element.44), channel_id=1, source_target_pairs={{0,16},{8,24},{16,32},{24,40},{32,48},{40,56},{48,64},{56,72},{64,... | collective-permute-start | bytes 98312 | tf_op jit(solution)/shard_map/ppermute | solution.py:433
  61.0 15.3 %collective-permute-start.5 = (bf16[128,128]{1,0:T(8,128)(2,1)S(1)}, bf16[128,128]{1,0:T(8,128)(2,1)S(1)}, u32[]{:S(2)}, u32[]{:S(2)}) collective-permute-start(bf16[128,128]{1,0:T(8,128)(2,1)S(1)} %get-tuple-element.45), channel_id=1, source_target_pairs={{16,0},{24,8},{32,16},{40,24},{48,32},{56,40},{64,48},{72,56},{80,... | collective-permute-start | bytes 98312 | tf_op jit(solution)/shard_map/ppermute | solution.py:433
  64.4 11.9 %collective-permute-start.6 = (bf16[64,128]{1,0:T(8,128)(2,1)S(1)}, bf16[64,128]{1,0:T(8,128)(2,1)S(1)}, u32[]{:S(2)}, u32[]{:S(2)}) collective-permute-start(bf16[64,128]{1,0:T(8,128)(2,1)S(1)} %get-tuple-element.46), channel_id=1, source_target_pairs={{8,32},{24,48},{32,8},{40,64},{48,24},{56,80},{64,40},{72,96},{80,... | collective-permute-start | bytes 49160 | tf_op jit(solution)/shard_map/ppermute | solution.py:443

commit v4 on v3

--- a/solution.py
+++ b/solution.py
@@ -28,10 +28,10 @@
 RELAY = HALO + LOAD
 LOWS = HALO // 2
 OWN = HALO + LOWS + 1 + LOAD
-EARLY = HOME + 3 * OFFCAP
-LATE = 3 * OFFCAP
+MIDDLE = 2 * OFFCAP
+LATE = 4 * OFFCAP
 PACK = 4
-RING = 4
+RING = 8
 REMAINDER = 1e-6
 
 
@@ -144,7 +144,7 @@
     own[HALO + LOWS] = table.astype(F32).astype(BF16)
 
 
-def relay_kernel(own, plus, minus, out, sems):
+def relay_kernel(_, own, plus, minus, out, sems):
     finish(
         launch(
             [
@@ -307,13 +307,13 @@
     iota = lax.broadcasted_iota(jnp.int32, (16, BLK), 0).astype(F32)
 
     def stored(group):
-        at = lax.rem(group, 2)
+        at = lax.rem(group, RING)
         return pltpu.make_async_copy(ring.at[at], mats.at[pl.ds(group * PACK, PACK)], ring_sems.at[at])
 
     def build(group, carry):
-        @pl.when(group >= 2)
+        @pl.when(group >= RING)
         def _():
-            stored(group - 2).wait()
+            stored(group - RING).wait()
 
         for j in range(PACK):
             entry = entry_slot[group * PACK + j]
@@ -325,24 +325,22 @@
                 m = jnp.zeros((16, BLK), BF16)
                 for k in range(STEN):
                     m = jnp.where(c[k] == here, w[k], m)
-                ring[lax.rem(group, 2), j, 16 * i : 16 * i + 16, :] = m
+                ring[lax.rem(group, RING), j, 16 * i : 16 * i + 16, :] = m
         stored(group).start()
         return carry
 
     groups = (n + PACK - 1) // PACK
     lax.fori_loop(0, groups, build, 0)
-
-    @pl.when(groups >= 2)
-    def _():
-        stored(groups - 2).wait()
-
-    @pl.when(groups >= 1)
-    def _():
-        stored(groups - 1).wait()
+    for back in range(1, RING + 1):
+
+        @pl.when(groups >= back)
+        def _():
+            stored(groups - back).wait()
 
 
 def spread_kernel(
-    me, lev, geo_in, slot1, win1, count1, mats1, slot2, win2, count2, mats2,
+    me, lev, geo_in,
+    slot1, win1, count1, mats1, slot2, win2, count2, mats2, slot3, win3, count3, mats3,
     b_home, plus, minus, cross, mate, f_home, f_mate, f_plus, f_minus, f_cross, local, above,
     out, geo, values, firsts, total, ring, sems, ring_sems,
 ):
@@ -361,7 +359,11 @@
     ]
     pairs += [(geo_in, geo)]
     copies = launch([(a, b, sems.at[i]) for i, (a, b) in enumerate(pairs)])
-    loops = ((slot1, win1, count1, mats1, 0, EARLY), (slot2, win2, count2, mats2, EARLY, LATE))
+    loops = (
+        (slot1, win1, count1, mats1, 0, HOME),
+        (slot2, win2, count2, mats2, HOME, MIDDLE),
+        (slot3, win3, count3, mats3, HOME + MIDDLE, LATE),
+    )
 
     def fetched(mats, lane, group):
         at = lax.rem(group, RING)
@@ -443,7 +445,7 @@
     return lax.ppermute(parcel, "tile", [(i, j) for i, j in pairs if 0 <= j < peers])
 
 
-def matrices(home, parts):
+def matrices(home, parts, cost):
     count = (HOME if home else 0) + OFFCAP * len(parts)
     entries = 2 * count
     return call(
@@ -456,17 +458,17 @@
         ],
         [vmem()] * len(home) + [free()] * len(parts),
         [
-            pltpu.VMEM((len(parts), ROUTE, 16, BLK), BF16),
+            pltpu.VMEM((max(len(parts), 1), ROUTE, 16, BLK), BF16),
             pltpu.VMEM((STEN, count, BLK), F32),
             pltpu.VMEM((STEN, 2 * count, BLK), F32),
-            pltpu.VMEM((2, PACK, WIN, BLK), BF16),
+            pltpu.VMEM((RING, PACK, WIN, BLK), BF16),
             pltpu.VMEM((1, BLK), jnp.int32),
             pltpu.SMEM((1, BLK), jnp.int32),
-            pltpu.SemaphoreType.DMA((len(parts),)),
-            pltpu.SemaphoreType.DMA((2,)),
+            pltpu.SemaphoreType.DMA((max(len(parts), 1),)),
+            pltpu.SemaphoreType.DMA((RING,)),
             pltpu.SemaphoreType.DMA,
         ],
-        4,
+        cost,
         16,
     )(*home, *[parcel for parcel, _ in parts])
 
@@ -512,18 +514,19 @@
     plus = moved(plus, 2)
     minus = moved(minus, -2)
     cross = crossed(cross)
+    first = matrices([a_home], [], 40)
 
     relayed = call(
         relay_kernel,
         [((OWN + 2 * RELAY, 16, BLK), BF16, free())],
-        [free()] * 3,
+        [smem()] + [free()] * 3,
         [pltpu.SemaphoreType.DMA((3,))],
         1,
         16,
-    )(own, plus, minus)[0]
+    )(first[3], own, plus, minus)[0]
     mate = swapped(relayed)
 
-    early = matrices([a_home], [(plus, RELAY), (minus, RELAY), (cross, 0)])
+    middle = matrices([], [(plus, RELAY), (minus, RELAY)], 10)
 
     local, totals, f_home, f_mate, f_plus, f_minus, f_cross = call(
         solve_kernel,
@@ -554,7 +557,7 @@
         ],
         2,
         24,
-    )(me, slots, early[3], kept(helm_coef), own, plus, minus, mate)
+    )(me, slots, middle[3], kept(helm_coef), own, plus, minus, mate)
     above = lax.all_to_all(totals, "lev", 0, 0)
     f_plus = moved(f_plus, 2)
     f_minus = moved(f_minus, -2)
@@ -562,7 +565,8 @@
 
     late = matrices(
         [],
-        [(mate, HALO + LOWS + 1), (mate, OWN + HALO), (mate, OWN + RELAY + HALO)],
+        [(cross, 0), (mate, HALO + LOWS + 1), (mate, OWN + HALO), (mate, OWN + RELAY + HALO)],
+        4,
     )
 
     def lists(found):
@@ -573,20 +577,20 @@
     return call(
         spread_kernel,
         [((4, 4, CELLS), F32, vmem())],
-        [smem()] * 2 + [hbm()] + listed * 2 + [free()] * 5 + [vmem()] * 7,
+        [smem()] * 2 + [hbm()] + listed * 3 + [free()] * 5 + [vmem()] * 7,
         [
             pltpu.SMEM((4,), F32),
             pltpu.VMEM((SLOTS, 16, BLK), BF16),
             pltpu.VMEM((SLOTS * 4 + 8, BLK), F32),
             pltpu.VMEM((16, CELLS + WIN), F32),
-            pltpu.VMEM((2, RING, PACK, WIN, BLK), BF16),
+            pltpu.VMEM((3, RING, PACK, WIN, BLK), BF16),
             pltpu.SemaphoreType.DMA((GROUPS + 2,)),
-            pltpu.SemaphoreType.DMA((2, RING)),
+            pltpu.SemaphoreType.DMA((3, RING)),
         ],
         4,
         24,
     )(
-        me, lev, kept(geo_coef), *lists(early), *lists(late),
+        me, lev, kept(geo_coef), *lists(first), *lists(middle), *lists(late),
         b_home, plus, minus, cross, mate, f_home, f_mate, f_plus, f_minus, f_cross, local, above,
     )[0]
 

time: 85.3 us -> 75.5 us (0.89)
  the two profiles are of different devices: /device:TPU:207 before, /device:TPU:205 now
where the time goes in v4:
time: 75.5 us; the launch traced here: 75 us
  starting transfers between devices  34.1 us (45%)
  Pallas kernels  32.8 us (43%)
  waiting for transfers between devices  7.98 us (11%)
    pallas_call x3, Pallas kernels, matrices(): call(lambda *refs: matrix_kernel(count, len(home), [at for _, at in parts...  14.7 us
    ppermute x4, starting transfers between devices, moved(): lax.ppermute(parcel, 'tile', [(i, i + by) for i in range(peers) if 0 <= i...  12.9 us
    ppermute x2, starting transfers between devices, crossed(): lax.ppermute(parcel, 'tile', [(i, j) for i, j in pairs if 0 <= j < peers])  10.7 us
    pallas_call x1, Pallas kernels, body(): call(spread_kernel, [((4, 4, CELLS), F32, vmem())], [smem()] * 2 + [hbm()...  9.75 us
    ppermute x4, waiting for transfers between devices, moved(): lax.ppermute(parcel, 'tile', [(i, i + by) for i in range(peers) if 0 <= i...  7.97 us
    all_to_all x1, starting transfers between devices, body(): above = lax.all_to_all(totals, 'lev', 0, 0)  7 us
    pallas_call x1, Pallas kernels, body(): call(solve_kernel, [((8, NLON), F32, vmem()), ((peers, NBLK, BLK), BF16,...  4.68 us
    ppermute x1, starting transfers between devices, swapped(): lax.ppermute(parcel, 'tile', [(i, i ^ 1) for i in range(lax.axis_size('ti...  3.46 us
  transfers between devices with their start and end apart: 8, of which 2 were waited for; matrix products, arithmetic and copies ran while one was open for 0% of the time, Pallas kernels for 20%

profile of v4, /device:TPU:205, one launch (start us, length us, event | category | flops | bytes accessed | tf_op | source)
XLA Modules:
  0.0 75.0 jit_solution(309280291068125003)
XLA Ops:
  0.0 2.7 %shard_map.73 = (s32[64]{0:T(128)S(1)}, bf16[25,32,128]{2,1,0:T(8,128)(2,1)S(1)}, bf16[32,16,128]{2,1,0:T(8,128)(2,1)S(1)}, bf16[90,16,128]{2,1,0:T(8,128)(2,1)S...) custom-call(s32[1]{0:T(128)} %bitcast.me, s32[64]{0:T(128)} %bitcast.3, ...), custom_call_target="tpu_custom_call" | custom-call | flops 1000000 | bytes 3000000 | tf_op jit(solution)/shard_map/pallas_call | solution.py:487
  2.7 2.8 %collective-permute-start = (bf16[114,16,128]{2,1,0:T(8,128)(2,1)S(1)}, bf16[114,16,128]{2,1,0:T(8,128)(2,1)S(1)}, u32[]{:S(2)}, u32[]{:S(2)}) collective-permute-start(bf16[114,16,128]{2,1,0:T(8,128)(2,1)S(1)} %get-tuple-element.36), channel_id=1, source_target_pairs={{0,16},{8,24},{16,32},{24,40},{32,48},{40,56},{48,64},{56,72},{64,... | collective-permute-start | bytes 1400840 | tf_op jit(solution)/shard_map/ppermute | solution.py:435
  5.6 2.5 %collective-permute-start.1 = (bf16[114,16,128]{2,1,0:T(8,128)(2,1)S(1)}, bf16[114,16,128]{2,1,0:T(8,128)(2,1)S(1)}, u32[]{:S(2)}, u32[]{:S(2)}) collective-permute-start(bf16[114,16,128]{2,1,0:T(8,128)(2,1)S(1)} %get-tuple-element.37), channel_id=1, source_target_pairs={{16,0},{24,8},{32,16},{40,24},{48,32},{56,40},{64,48},{72,56},{80,... | collective-permute-start | bytes 1400840 | tf_op jit(solution)/shard_map/ppermute | solution.py:435
  8.0 4.8 %shard_map.74 = (bf16[64,256,128]{2,1,0:T(8,128)(2,1)}, s32[72]{0:T(128)S(1)}, s32[72]{0:T(128)S(1)}, s32[1]{0:T(128)}) custom-call(bf16[25,32,128]{2,1,0:T(8,128)(2,1)S(1)} %get-tuple-element.31.refs_0_), custom_call_target="tpu_custom_call" | custom-call | flops 40000000 | bytes 120000000 | tf_op jit(solution)/shard_map/pallas_call | solution.py:451
  12.8 3.4 %collective-permute-done.refs_0_.plus = bf16[114,16,128]{2,1,0:T(8,128)(2,1)S(1)} collective-permute-done((bf16[114,16,128]{2,1,0:T(8,128)(2,1)S(1)}, bf16[114,16,128]{2,1,0:T(8,128)(2,1)S(1)}, u32[]{:S(2)}, u32[]{:S(2)}) %collective-permute-start) | collective-permute-done | bytes 466976 | tf_op jit(solution)/shard_map/ppermute | solution.py:435
  16.2 4.6 %collective-permute-done.1.refs_1_.minus = bf16[114,16,128]{2,1,0:T(8,128)(2,1)S(1)} collective-permute-done((bf16[114,16,128]{2,1,0:T(8,128)(2,1)S(1)}, bf16[114,16,128]{2,1,0:T(8,128)(2,1)S(1)}, u32[]{:S(2)}, u32[]{:S(2)}) %collective-permute-start.1) | collective-permute-done | bytes 466976 | tf_op jit(solution)/shard_map/ppermute | solution.py:435
  20.8 0.9 %shard_map.76 = bf16[236,16,128]{2,1,0:T(8,128)(2,1)S(1)} custom-call(s32[1]{0:T(128)} %get-tuple-element.34._.count1, bf16[90,16,128]{2,1,0:T(8,128)(2,1)S(1)} %get-tuple-element.43.own, bf16[114,16,128]{2,1,0:T(8,128)(2,1)S(1)} %collective-permute-done.refs_0_.plus, bf16[114,16,128]{2,1,0:T(8,128)(2,1)S(1)} %collective-permute-done.1.refs_1_.minus), custom_call_target="tpu_custom_call" | custom-call | flops 1000000 | bytes 3000000 | tf_op jit(solution)/shard_map/pallas_call | solution.py:519
  21.8 3.5 %collective-permute-start.3 = (bf16[236,16,128]{2,1,0:T(8,128)(2,1)S(1)}, bf16[236,16,128]{2,1,0:T(8,128)(2,1)S(1)}, u32[]{:S(2)}, u32[]{:S(2)}) collective-permute-start(bf16[236,16,128]{2,1,0:T(8,128)(2,1)S(1)} %shard_map.76), channel_id=1, source_target_pairs={{0,8},{8,0},{16,24},{24,16},{32,40},{40,32},{48,56},{56,48},{64,72... | collective-permute-start | bytes 2899976 | tf_op jit(solution)/shard_map/ppermute | solution.py:439
  25.2 3.6 %shard_map.75 = (bf16[64,256,128]{2,1,0:T(8,128)(2,1)}, s32[72]{0:T(128)S(1)}, s32[72]{0:T(128)S(1)}, s32[1]{0:T(128)}) custom-call(bf16[114,16,128]{2,1,0:T(8,128)(2,1)S(1)} %collective-permute-done.refs_0_.plus, bf16[114,16,128]{2,1,0:T(8,128)(2,1)S(1)} %collective-permute-done.1.refs_1_.minus), custom_call_target="tpu_custom_call" | custom-call | flops 10000000 | bytes 30000000 | tf_op jit(solution)/shard_map/pallas_call | solution.py:451
  28.8 0.0 collective-permute-done.3.refs_1_.refs_2_.refs_3_.mate
  28.8 4.7 %shard_map.78 = (f32[8,4096]{1,0:T(8,128)S(1)}, bf16[8,64,128]{2,1,0:T(8,128)(2,1)}, bf16[128,128]{1,0:T(8,128)(2,1)S(1)}, bf16[64,128]{1,0:T(8,128)(2,1)S(1)}, ...) custom-call(s32[1]{0:T(128)} %bitcast.me, s32[64]{0:T(128)S(1)} %get-tuple-element.49.slots, ...), custom_call_target="tpu_custom_call" | custom-call | flops 2000000 | bytes 6000000 | tf_op jit(solution)/shard_map/pallas_call | solution.py:531
  33.5 7.0 %all-to-all-start = ((bf16[8,64,128]{2,1,0:T(8,128)(2,1)}), bf16[8,64,128]{2,1,0:T(8,128)(2,1)S(1)}, u32[]{:S(2)}, u32[]{:S(2)}) async-start(bf16[8,64,128]{2,1,0:T(8,128)(2,1)} %get-tuple-element.56), calls=%async_computation | async-start | bytes 262144 | tf_op jit(solution)/shard_map/all_to_all | solution.py:561
  40.5 5.0 %collective-permute-start.2 = (bf16[41,16,128]{2,1,0:T(8,128)(2,1)S(1)}, bf16[41,16,128]{2,1,0:T(8,128)(2,1)S(1)}, u32[]{:S(2)}, u32[]{:S(2)}) collective-permute-start(bf16[41,16,128]{2,1,0:T(8,128)(2,1)S(1)} %get-tuple-element.42), channel_id=1, source_target_pairs={{8,32},{24,48},{32,8},{40,64},{48,24},{56,80},{64,40},{72,96},{80,... | collective-permute-start | bytes 503816 | tf_op jit(solution)/shard_map/ppermute | solution.py:445
  45.5 4.1 %collective-permute-start.4 = (bf16[128,128]{1,0:T(8,128)(2,1)S(1)}, bf16[128,128]{1,0:T(8,128)(2,1)S(1)}, u32[]{:S(2)}, u32[]{:S(2)}) collective-permute-start(bf16[128,128]{1,0:T(8,128)(2,1)S(1)} %get-tuple-element.52), channel_id=1, source_target_pairs={{0,16},{8,24},{16,32},{24,40},{32,48},{40,56},{48,64},{56,72},{64,... | collective-permute-start | bytes 98312 | tf_op jit(solution)/shard_map/ppermute | solution.py:435
  49.6 3.5 %collective-permute-start.5 = (bf16[128,128]{1,0:T(8,128)(2,1)S(1)}, bf16[128,128]{1,0:T(8,128)(2,1)S(1)}, u32[]{:S(2)}, u32[]{:S(2)}) collective-permute-start(bf16[128,128]{1,0:T(8,128)(2,1)S(1)} %get-tuple-element.53), channel_id=1, source_target_pairs={{16,0},{24,8},{32,16},{40,24},{48,32},{56,40},{64,48},{72,56},{80,... | collective-permute-start | bytes 98312 | tf_op jit(solution)/shard_map/ppermute | solution.py:435
  53.2 5.7 %collective-permute-start.6 = (bf16[64,128]{1,0:T(8,128)(2,1)S(1)}, bf16[64,128]{1,0:T(8,128)(2,1)S(1)}, u32[]{:S(2)}, u32[]{:S(2)}) collective-permute-start(bf16[64,128]{1,0:T(8,128)(2,1)S(1)} %get-tuple-element.54), channel_id=1, source_target_pairs={{8,32},{24,48},{32,8},{40,64},{48,24},{56,80},{64,40},{72,96},{80,... | collective-permute-start | bytes 49160 | tf_op jit(solution)/shard_map/ppermute | solution.py:445
  58.9 0.0 collective-permute-done.2.refs_0_.cross
  58.9 6.3 %shard_map.77 = (bf16[128,256,128]{2,1,0:T(8,128)(2,1)}, s32[136]{0:T(256)S(1)}, s32[136]{0:T(256)S(1)}, s32[1]{0:T(128)}) custom-call(bf16[41,16,128]{2,1,0:T(8,128)(2,1)S(1)} %collective-permute-done.2.refs_0_.cross, bf16[236,16,128]{2,1,0:T(8,128)(2,1)S(1)} %collective-permute-done.3.refs_1_.refs_2_.refs_3_.mate, ...), custom_call_target="tpu_custom_call" | custom-call | flops 4000000 | bytes 12000000 | tf_op jit(solution)/shard_map/pallas_call | solution.py:451
  65.2 0.0 collective-permute-done.6.f_cross
  65.2 0.0 collective-permute-done.4.f_plus
  65.2 0.0 collective-permute-done.5.f_minus
  65.2 0.0 all-to-all-done.above
  65.2 9.8 %shard_map.79 = f32[4,4,8192]{2,1,0:T(4,128)} custom-call(s32[1]{0:T(128)} %bitcast.me, s32[1]{0:T(128)} %bitcast.1.lev, f32[4]{0:T(128)} %geo_in.1, s32[72]{0:T(128)S(1)} %get-tuple-element.32.slot1, s32[72]{0:T(128)S(1)} %get-tuple-element.33.win1, s32[1]{0:T(128)} %get-tuple-element.34._.count1, bf16[64,256,128]{2,1,0:T(8,128)(2,1)} %get-tuple-element.35.mats1, ...), custom_call_target="tpu_custom_call" | custom-call | flops 4000000 | bytes 12000000 | tf_op jit(solution)/shard_map/pallas_call | solution.py:577
Async XLA Ops:
  2.7 13.5 %collective-permute-start = (bf16[114,16,128]{2,1,0:T(8,128)(2,1)S(1)}, bf16[114,16,128]{2,1,0:T(8,128)(2,1)S(1)}, u32[]{:S(2)}, u32[]{:S(2)}) collective-permute-start(bf16[114,16,128]{2,1,0:T(8,128)(2,1)S(1)} %get-tuple-element.36), channel_id=1, source_target_pairs={{0,16},{8,24},{16,32},{24,40},{32,48},{40,56},{48,64},{56,72},{64,... | collective-permute-start | bytes 1400840 | tf_op jit(solution)/shard_map/ppermute | solution.py:435
  5.6 15.2 %collective-permute-start.1 = (bf16[114,16,128]{2,1,0:T(8,128)(2,1)S(1)}, bf16[114,16,128]{2,1,0:T(8,128)(2,1)S(1)}, u32[]{:S(2)}, u32[]{:S(2)}) collective-permute-start(bf16[114,16,128]{2,1,0:T(8,128)(2,1)S(1)} %get-tuple-element.37), channel_id=1, source_target_pairs={{16,0},{24,8},{32,16},{40,24},{48,32},{56,40},{64,48},{72,56},{80,... | collective-permute-start | bytes 1400840 | tf_op jit(solution)/shard_map/ppermute | solution.py:435
  21.8 7.1 %collective-permute-start.3 = (bf16[236,16,128]{2,1,0:T(8,128)(2,1)S(1)}, bf16[236,16,128]{2,1,0:T(8,128)(2,1)S(1)}, u32[]{:S(2)}, u32[]{:S(2)}) collective-permute-start(bf16[236,16,128]{2,1,0:T(8,128)(2,1)S(1)} %shard_map.76), channel_id=1, source_target_pairs={{0,8},{8,0},{16,24},{24,16},{32,40},{40,32},{48,56},{56,48},{64,72... | collective-permute-start | bytes 2899976 | tf_op jit(solution)/shard_map/ppermute | solution.py:439
  33.5 31.7 %all-to-all-start = ((bf16[8,64,128]{2,1,0:T(8,128)(2,1)}), bf16[8,64,128]{2,1,0:T(8,128)(2,1)S(1)}, u32[]{:S(2)}, u32[]{:S(2)}) async-start(bf16[8,64,128]{2,1,0:T(8,128)(2,1)} %get-tuple-element.56), calls=%async_computation | async-start | bytes 262144 | tf_op jit(solution)/shard_map/all_to_all | solution.py:561
  40.5 18.4 %collective-permute-start.2 = (bf16[41,16,128]{2,1,0:T(8,128)(2,1)S(1)}, bf16[41,16,128]{2,1,0:T(8,128)(2,1)S(1)}, u32[]{:S(2)}, u32[]{:S(2)}) collective-permute-start(bf16[41,16,128]{2,1,0:T(8,128)(2,1)S(1)} %get-tuple-element.42), channel_id=1, source_target_pairs={{8,32},{24,48},{32,8},{40,64},{48,24},{56,80},{64,40},{72,96},{80,... | collective-permute-start | bytes 503816 | tf_op jit(solution)/shard_map/ppermute | solution.py:445
  45.5 19.7 %collective-permute-start.4 = (bf16[128,128]{1,0:T(8,128)(2,1)S(1)}, bf16[128,128]{1,0:T(8,128)(2,1)S(1)}, u32[]{:S(2)}, u32[]{:S(2)}) collective-permute-start(bf16[128,128]{1,0:T(8,128)(2,1)S(1)} %get-tuple-element.52), channel_id=1, source_target_pairs={{0,16},{8,24},{16,32},{24,40},{32,48},{40,56},{48,64},{56,72},{64,... | collective-permute-start | bytes 98312 | tf_op jit(solution)/shard_map/ppermute | solution.py:435
  49.6 15.6 %collective-permute-start.5 = (bf16[128,128]{1,0:T(8,128)(2,1)S(1)}, bf16[128,128]{1,0:T(8,128)(2,1)S(1)}, u32[]{:S(2)}, u32[]{:S(2)}) collective-permute-start(bf16[128,128]{1,0:T(8,128)(2,1)S(1)} %get-tuple-element.53), channel_id=1, source_target_pairs={{16,0},{24,8},{32,16},{40,24},{48,32},{56,40},{64,48},{72,56},{80,... | collective-permute-start | bytes 98312 | tf_op jit(solution)/shard_map/ppermute | solution.py:435
  53.2 12.0 %collective-permute-start.6 = (bf16[64,128]{1,0:T(8,128)(2,1)S(1)}, bf16[64,128]{1,0:T(8,128)(2,1)S(1)}, u32[]{:S(2)}, u32[]{:S(2)}) collective-permute-start(bf16[64,128]{1,0:T(8,128)(2,1)S(1)} %get-tuple-element.54), channel_id=1, source_target_pairs={{8,32},{24,48},{32,8},{40,64},{48,24},{56,80},{64,40},{72,96},{80,... | collective-permute-start | bytes 49160 | tf_op jit(solution)/shard_map/ppermute | solution.py:445

commit v5 on v4

--- a/solution.py
+++ b/solution.py
@@ -29,7 +29,8 @@
 LOWS = HALO // 2
 OWN = HALO + LOWS + 1 + LOAD
 MIDDLE = 2 * OFFCAP
-LATE = 4 * OFFCAP
+LATE = 3 * OFFCAP
+CROSS = LOAD + 4
 PACK = 4
 RING = 8
 REMAINDER = 1e-6
@@ -157,12 +158,13 @@
 
 
 def solve_kernel(
-    me, slots, _, helm_in, own, plus, minus, mate,
-    local, totals, f_home, f_mate, f_plus, f_minus, f_cross,
+    me, slots, _, helm_in, own, plus, minus, mate, cross_in,
+    local, totals, f_home, f_mate, f_plus, f_minus, cross,
     helm, halo, lows, rhs, coef, result, table, table_s, mine_all, mate_all, t_all, sems, table_sem,
 ):
     core = lax.rem(me[0], 2)
     tables = launch([(mate.at[pl.ds(HALO, LOWS + 1)], lows, sems.at[7])])
+    passed = launch([(cross_in, cross.at[pl.ds(0, LOAD)], sems.at[8])])
     pairs = (
         (helm_in, helm),
         (plus.at[pl.ds(0, HALO)], halo.at[core]),
@@ -235,57 +237,50 @@
     f_plus[OFFCAP * 4 :] = part(mate_all, 1, 3)
     f_minus[: OFFCAP * 4] = part(mine_all, -2, -2)
     f_minus[OFFCAP * 4 :] = part(mate_all, -3, -1)
-    f_cross[...] = part(mine_all, -3, 3)
-
-
-def matrix_kernel(count, home, offsets, *refs):
-    a_home = refs[0] if home else None
-    parcels, refs = refs[home : home + len(offsets)], refs[home + len(offsets) :]
-    mats, entry_slot, entry_win, entry_count, a_in, cells, merged, ring, meta, meta_s, sems, ring_sems, meta_sem = refs
-    copies = launch([(p.at[pl.ds(at, ROUTE)], a_in.at[i], sems.at[i]) for i, (p, at) in enumerate(zip(parcels, offsets))])
-
+    piece = part(mine_all, -3, 3)
+    for i in range(4):
+        cross[LOAD + i] = piece[16 * i : 16 * i + 16]
+    finish(passed)
+
+
+def merge(load, cells, merged, count, base):
+    w = [load(k) for k in range(STEN)]
+    c = [load(STEN + k) for k in range(STEN)]
+    total = list(w)
+    for k in range(STEN):
+        for m in range(k):
+            same = c[k] == c[m]
+            total[k] = total[k] + jnp.where(same, w[m], 0.0)
+            total[m] = total[m] + jnp.where(same, w[k], 0.0)
+    lost = jnp.zeros((8, BLK), F32)
+    held = jnp.zeros((8, BLK), F32)
+    for k in range(STEN):
+        high = total[k].astype(BF16).astype(F32)
+        low = total[k] - high
+        cells[k, base : base + 8, :] = c[k]
+        merged[k, base : base + 8, :] = high
+        merged[k, count + base : count + base + 8, :] = low
+        lost = lost + low * low
+        held = held + w[k] * w[k]
+    more = jnp.sum(lost, axis=1, keepdims=True) > REMAINDER * jnp.sum(held, axis=1, keepdims=True)
+    mark = load(2 * STEN)
+    mark = jnp.where(mark > 0.0, mark + jnp.where(more, 64.0, 0.0), 0.0)
     lane = lax.broadcasted_iota(jnp.int32, (8, BLK), 1)
     row = lax.broadcasted_iota(jnp.int32, (8, BLK), 0)
-
-    def merge(base, load):
-        w = [load(k) for k in range(STEN)]
-        c = [load(STEN + k) for k in range(STEN)]
-        total = list(w)
-        for k in range(STEN):
-            for m in range(k):
-                same = c[k] == c[m]
-                total[k] = total[k] + jnp.where(same, w[m], 0.0)
-                total[m] = total[m] + jnp.where(same, w[k], 0.0)
-        lost = jnp.zeros((8, BLK), F32)
-        held = jnp.zeros((8, BLK), F32)
-        for k in range(STEN):
-            high = total[k].astype(BF16).astype(F32)
-            low = total[k] - high
-            cells[k, base : base + 8, :] = c[k]
-            merged[k, base : base + 8, :] = high
-            merged[k, count + base : count + base + 8, :] = low
-            lost = lost + low * low
-            held = held + w[k] * w[k]
-        more = jnp.sum(lost, axis=1, keepdims=True) > REMAINDER * jnp.sum(held, axis=1, keepdims=True)
-        mark = load(2 * STEN)
-        mark = jnp.where(mark > 0.0, mark + jnp.where(more, 64.0, 0.0), 0.0)
-        return jnp.where(lane == row + base, mark, 0.0)
-
+    return jnp.where(lane == row + base, mark, 0.0)
+
+
+def merge_all(groups, cells, merged, count, meta):
     marks = jnp.zeros((8, BLK), F32)
-    for at in range(0, HOME if home else 0, 16):
-        pair = [a_home[r, at : at + 16, :].astype(F32) for r in range(ROUTE)]
+    for i, group in enumerate(groups):
+        rows = group()
         for half in (0, 8):
-            marks = marks + merge(at + half, lambda r: pair[r][half : half + 8])
-    for i in range(len(offsets)):
-        copies[i].wait()
-        pair = [a_in[i, r].astype(F32) for r in range(ROUTE)]
-        at = (HOME if home else 0) + OFFCAP * i
-        for half in (0, 8):
-            marks = marks + merge(at + half, lambda r: pair[r][half : half + 8])
+            marks = marks + merge(lambda r: rows[r][half : half + 8], cells, merged, count, 16 * i + half)
     meta[...] = jnp.sum(marks, axis=0, keepdims=True).astype(jnp.int32)
-    finish(launch([(meta, meta_s, meta_sem)]))
-
-    def enlist(i, n):
+
+
+def enlist(meta_s, count, entry_slot, entry_win):
+    def eight(i, n):
         for j in range(8):
             slot = i * 8 + j
             mark = meta_s[0, slot]
@@ -298,122 +293,227 @@
             n = n + (mark >= 64).astype(jnp.int32)
         return n
 
-    n = lax.fori_loop(0, count // 8, enlist, jnp.int32(0))
-    entry_count[0] = n
+    n = lax.fori_loop(0, count // 8, eight, jnp.int32(0))
     for j in range(PACK):
         entry_slot[n + j] = 0
         entry_win[n + j] = NWIN
-
+    return n
+
+
+def build(group, cells, merged, count, entry_slot, target):
     iota = lax.broadcasted_iota(jnp.int32, (16, BLK), 0).astype(F32)
-
-    def stored(group):
+    for j in range(PACK):
+        entry = entry_slot[group * PACK + j]
+        slot = lax.rem(entry, count)
+        c = [jnp.broadcast_to(cells[k, pl.ds(slot, 1), :], (16, BLK)).astype(BF16) for k in range(STEN)]
+        w = [jnp.broadcast_to(merged[k, pl.ds(entry, 1), :], (16, BLK)).astype(BF16) for k in range(STEN)]
+        for i in range(WIN // 16):
+            here = (iota + 16.0 * i).astype(BF16)
+            m = jnp.zeros((16, BLK), BF16)
+            for k in range(STEN):
+                m = jnp.where(c[k] == here, w[k], m)
+            target[j, 16 * i : 16 * i + 16, :] = m
+
+
+def multiply(group, slots, base, size, values, firsts, source):
+    first_rows = lax.broadcasted_iota(jnp.int32, (8, BLK), 0) < 4
+    products = []
+    for j in range(PACK):
+        slot = base + lax.rem(slots[group * PACK + j], size)
+        tile = values[slot].astype(F32)
+        head = jnp.where(first_rows, firsts[pl.ds(slot * 4, 8), :], tile[:8])
+        left = jnp.concatenate([head, tile[8:]], axis=0).astype(BF16)
+        products.append(lax.dot_general(left, source[j], (((1,), (1,)), ((), ())), preferred_element_type=F32))
+    return products
+
+
+def add_up(group, wins, total, products):
+    for j in range(PACK):
+        start = pl.multiple_of(wins[group * PACK + j] * WIN, WIN)
+        total[:, pl.ds(start, WIN)] += products[j]
+
+
+def groups_of(n):
+    return (n + PACK - 1) // PACK
+
+
+def ringed(ring, sems, mats, out):
+    def copy(group):
         at = lax.rem(group, RING)
-        return pltpu.make_async_copy(ring.at[at], mats.at[pl.ds(group * PACK, PACK)], ring_sems.at[at])
-
-    def build(group, carry):
+        far, near = mats.at[pl.ds(group * PACK, PACK)], ring.at[at]
+        return pltpu.make_async_copy(*((near, far) if out else (far, near)), sems.at[at])
+
+    return copy
+
+
+def drain(stored, groups):
+    for back in range(1, RING + 1):
+
+        @pl.when(groups >= back)
+        def _():
+            stored(groups - back).wait()
+
+
+def prefetch(fetched, groups):
+    for g in range(RING):
+
+        @pl.when(g < groups)
+        def _():
+            fetched(g).start()
+
+
+def arrival(copy, tiles):
+    def rows():
+        copy.wait()
+        return [tiles[r].astype(F32) for r in range(ROUTE)]
+
+    return rows
+
+
+def matrix_kernel(count, home, offsets, *refs):
+    a_home = refs[0] if home else None
+    parcels, refs = refs[home : home + len(offsets)], refs[home + len(offsets) :]
+    mats, entry_slot, entry_win, entry_count, a_in, cells, merged, ring, meta, meta_s, sems, ring_sems, meta_sem = refs
+    copies = launch([(p.at[pl.ds(at, ROUTE)], a_in.at[i], sems.at[i]) for i, (p, at) in enumerate(zip(parcels, offsets))])
+
+    def own_rows(at):
+        return lambda: [a_home[r, at : at + 16, :].astype(F32) for r in range(ROUTE)]
+
+    parts = [own_rows(at) for at in range(0, HOME if home else 0, 16)]
+    parts += [arrival(copy, a_in.at[i]) for i, copy in enumerate(copies)]
+    merge_all(parts, cells, merged, count, meta)
+    finish(launch([(meta, meta_s, meta_sem)]))
+    n = enlist(meta_s, count, entry_slot, entry_win)
+    entry_count[0] = n
+    stored = ringed(ring, ring_sems, mats, True)
+
+    def step(group, carry):
         @pl.when(group >= RING)
         def _():
             stored(group - RING).wait()
 
-        for j in range(PACK):
-            entry = entry_slot[group * PACK + j]
-            slot = lax.rem(entry, count)
-            c = [jnp.broadcast_to(cells[k, pl.ds(slot, 1), :], (16, BLK)).astype(BF16) for k in range(STEN)]
-            w = [jnp.broadcast_to(merged[k, pl.ds(entry, 1), :], (16, BLK)).astype(BF16) for k in range(STEN)]
-            for i in range(WIN // 16):
-                here = (iota + 16.0 * i).astype(BF16)
-                m = jnp.zeros((16, BLK), BF16)
-                for k in range(STEN):
-                    m = jnp.where(c[k] == here, w[k], m)
-                ring[lax.rem(group, RING), j, 16 * i : 16 * i + 16, :] = m
+        build(group, cells, merged, count, entry_slot, ring.at[lax.rem(group, RING)])
         stored(group).start()
         return carry
 
-    groups = (n + PACK - 1) // PACK
-    lax.fori_loop(0, groups, build, 0)
-    for back in range(1, RING + 1):
-
-        @pl.when(groups >= back)
-        def _():
-            stored(groups - back).wait()
+    lax.fori_loop(0, groups_of(n), step, 0)
+    drain(stored, groups_of(n))
+
+
+def late_kernel(
+    mate, slot1, win1, count1, mats1, b_home, f_home,
+    mats, entry_slot, entry_win, entry_count, total,
+    a_in, cells, merged, meta, meta_s, firsts, out_ring, in_ring, sems, out_sems, in_sems, meta_sem,
+):
+    offsets = (HALO + LOWS + 1, OWN + HALO, OWN + RELAY + HALO)
+    copies = launch([(mate.at[pl.ds(at, ROUTE)], a_in.at[i], sems.at[i]) for i, at in enumerate(offsets)])
+    stored = ringed(out_ring, out_sems, mats, True)
+    fetched = ringed(in_ring, in_sems, mats1, False)
+    home_groups = groups_of(count1[0])
+    prefetch(fetched, home_groups)
+    total[...] = jnp.zeros_like(total)
+    firsts[: HOME * 4, :] = f_home[...].astype(F32)
+    firsts[HOME * 4 :, :] = jnp.zeros((8, BLK), F32)
+    merge_all([arrival(copy, a_in.at[i]) for i, copy in enumerate(copies)], cells, merged, LATE, meta)
+    finish(launch([(meta, meta_s, meta_sem)]))
+    n = enlist(meta_s, LATE, entry_slot, entry_win)
+    entry_count[0] = n
+    late_groups = groups_of(n)
+
+    def step(building, multiplying):
+        def run(group, carry):
+            at = lax.rem(group, RING)
+            if building:
+
+                @pl.when(group >= RING)
+                def _():
+                    stored(group - RING).wait()
+
+            if multiplying:
+                fetched(group).wait()
+                products = multiply(group, slot1, 0, HOME, b_home, firsts, in_ring.at[at])
+            if building:
+                build(group, cells, merged, LATE, entry_slot, out_ring.at[at])
+            if multiplying:
+                add_up(group, win1, total, products)
+
+                @pl.when(group + RING < home_groups)
+                def _():
+                    fetched(group + RING).start()
+
+            if building:
+                stored(group).start()
+            return carry
+
+        return run
+
+    both = jnp.minimum(home_groups, late_groups)
+    lax.fori_loop(0, both, step(True, True), 0)
+    lax.fori_loop(both, late_groups, step(True, False), 0)
+    lax.fori_loop(both, home_groups, step(False, True), 0)
+    drain(stored, late_groups)
 
 
 def spread_kernel(
-    me, lev, geo_in,
-    slot1, win1, count1, mats1, slot2, win2, count2, mats2, slot3, win3, count3, mats3,
-    b_home, plus, minus, cross, mate, f_home, f_mate, f_plus, f_minus, f_cross, local, above,
-    out, geo, values, firsts, total, ring, sems, ring_sems,
+    lev, geo_in, slot2, win2, count2, mats2, slot3, win3, count3, mats3,
+    plus, minus, cross, mate, f_mate, f_plus, f_minus, begun, local, above,
+    out, geo, values, firsts, total, ring, a_in, cells, merged, meta, meta_s, entry_slot, entry_win, fresh,
+    sems, ring_sems, meta_sem,
 ):
-    core = lax.rem(me[0], 2)
+    routes = launch([(cross.at[pl.ds(0, ROUTE)], a_in, sems.at[GROUPS + 1])])
     parts = (
         (plus, RELAY + ROUTE),
         (minus, RELAY + ROUTE),
-        (cross, ROUTE),
         (mate, HALO + LOWS + 1 + ROUTE),
         (mate, OWN + HALO + ROUTE),
         (mate, OWN + RELAY + HALO + ROUTE),
+        (cross, ROUTE),
     )
-    pairs = [(b_home, values.at[pl.ds(0, HOME)])]
-    pairs += [
-        (p.at[pl.ds(at, OFFCAP)], values.at[pl.ds(HOME + OFFCAP * i, OFFCAP)]) for i, (p, at) in enumerate(parts)
-    ]
+    pairs = [(p.at[pl.ds(at, OFFCAP)], values.at[pl.ds(OFFCAP * i, OFFCAP)]) for i, (p, at) in enumerate(parts)]
     pairs += [(geo_in, geo)]
     copies = launch([(a, b, sems.at[i]) for i, (a, b) in enumerate(pairs)])
-    loops = (
-        (slot1, win1, count1, mats1, 0, HOME),
-        (slot2, win2, count2, mats2, HOME, MIDDLE),
-        (slot3, win3, count3, mats3, HOME + MIDDLE, LATE),
-    )
-
-    def fetched(mats, lane, group):
-        at = lax.rem(group, RING)
-        return pltpu.make_async_copy(mats.at[pl.ds(group * PACK, PACK)], ring.at[lane, at], ring_sems.at[lane, at])
-
-    for lane, (_, _, count, mats, _, _) in enumerate(loops):
-        groups = (count[0] + PACK - 1) // PACK
-        for g in range(RING):
-
-            @pl.when(g < groups)
-            def _():
-                fetched(mats, lane, g).start()
-
-    total[...] = jnp.zeros_like(total)
+    loops = ((slot2, win2, count2, mats2, 0, MIDDLE), (slot3, win3, count3, mats3, MIDDLE, LATE))
+    fetches = [ringed(ring.at[i], ring_sems.at[i], loop[3], False) for i, loop in enumerate(loops)]
+    for fetched, loop in zip(fetches, loops):
+        prefetch(fetched, groups_of(loop[2][0]))
+    merge_all([arrival(routes[0], a_in)], cells, merged, OFFCAP, meta)
+    metas = launch([(meta, meta_s, meta_sem)])
+
+    total[...] = begun[...]
     half = OFFCAP * 4
-    pieces = (
-        f_plus[:half], f_minus[:half], f_cross[...], f_mate[...], f_plus[half:], f_minus[half:],
-    )
-    firsts[: HOME * 4, :] = f_home[...].astype(F32)
-    for i, piece in enumerate(pieces):
-        firsts[HOME * 4 + half * i : HOME * 4 + half * (i + 1), :] = piece.astype(F32)
-    firsts[SLOTS * 4 :, :] = jnp.zeros((8, BLK), F32)
+    for i, piece in enumerate((f_plus[:half], f_minus[:half], f_mate[...], f_plus[half:], f_minus[half:])):
+        firsts[half * i : half * (i + 1), :] = piece.astype(F32)
+    for i in range(4):
+        at = half * (GROUPS - 1) + 16 * i
+        firsts[at : at + 16, :] = cross[LOAD + i].astype(F32)
+    firsts[half * GROUPS :, :] = jnp.zeros((8, BLK), F32)
     finish(copies)
-    first_rows = lax.broadcasted_iota(jnp.int32, (8, BLK), 0) < 4
-
-    for lane, (slots, wins, count, mats, base, size) in enumerate(loops):
-        groups = (count[0] + PACK - 1) // PACK
+
+    for i, (fetched, (slots, wins, count, _, base, size)) in enumerate(zip(fetches, loops)):
+        groups = groups_of(count[0])
 
         def step(group, carry):
-            fetched(mats, lane, group).wait()
-            products = []
-            for j in range(PACK):
-                slot = base + lax.rem(slots[group * PACK + j], size)
-                tile = values[slot].astype(F32)
-                head = jnp.where(first_rows, firsts[pl.ds(slot * 4, 8), :], tile[:8])
-                left = jnp.concatenate([head, tile[8:]], axis=0).astype(BF16)
-                mat = ring[lane, lax.rem(group, RING), j]
-                products.append(lax.dot_general(left, mat, (((1,), (1,)), ((), ())), preferred_element_type=F32))
-
-            for j in range(PACK):
-                start = pl.multiple_of(wins[group * PACK + j] * WIN, WIN)
-                total[:, pl.ds(start, WIN)] += products[j]
+            fetched(group).wait()
+            products = multiply(group, slots, base, size, values, firsts, ring.at[i, lax.rem(group, RING)])
+            add_up(group, wins, total, products)
 
             @pl.when(group + RING < groups)
             def _():
-                fetched(mats, lane, group + RING).start()
+                fetched(group + RING).start()
 
             return carry
 
         lax.fori_loop(0, groups, step, 0)
+
+    finish(metas)
+    n = enlist(meta_s, OFFCAP, entry_slot, entry_win)
+
+    def last(group, carry):
+        build(group, cells, merged, OFFCAP, entry_slot, fresh)
+        add_up(group, entry_win, total, multiply(group, entry_slot, MIDDLE + LATE, OFFCAP, values, firsts, fresh))
+        return carry
+
+    lax.fori_loop(0, groups_of(n), last, 0)
 
     sums = jnp.zeros((NBLK, BLK), F32)
     for peer in range(above.shape[0]):
@@ -513,7 +613,6 @@
     )(me, *map(kept, (dest_tile[:, 0], src_window, adj_in, helm_coef, src_cell, interp_w)))
     plus = moved(plus, 2)
     minus = moved(minus, -2)
-    cross = crossed(cross)
     first = matrices([a_home], [], 40)
 
     relayed = call(
@@ -528,7 +627,7 @@
 
     middle = matrices([], [(plus, RELAY), (minus, RELAY)], 10)
 
-    local, totals, f_home, f_mate, f_plus, f_minus, f_cross = call(
+    local, totals, f_home, f_mate, f_plus, f_minus, cross = call(
         solve_kernel,
         [
             ((8, NLON), F32, vmem()),
@@ -537,9 +636,9 @@
             strip(OFFCAP),
             strip(2 * OFFCAP),
             strip(2 * OFFCAP),
-            strip(OFFCAP),
-        ],
-        [smem()] * 3 + [hbm()] + [free()] * 4,
+            parcel(CROSS),
+        ],
+        [smem()] * 3 + [hbm()] + [free()] * 5,
         [
             pltpu.VMEM(helm_coef.shape, F32),
             pltpu.VMEM((6, HALO, 16, BLK), BF16),
@@ -552,46 +651,77 @@
             pltpu.VMEM((SLOTS * 4, BLK), F32),
             pltpu.VMEM((SLOTS * 4, BLK), F32),
             pltpu.VMEM((NBLK, BLK), F32),
-            pltpu.SemaphoreType.DMA((8,)),
+            pltpu.SemaphoreType.DMA((9,)),
             pltpu.SemaphoreType.DMA,
         ],
         2,
         24,
-    )(me, slots, middle[3], kept(helm_coef), own, plus, minus, mate)
+    )(me, slots, middle[3], kept(helm_coef), own, plus, minus, mate, cross)
     above = lax.all_to_all(totals, "lev", 0, 0)
     f_plus = moved(f_plus, 2)
     f_minus = moved(f_minus, -2)
-    f_cross = crossed(f_cross)
-
-    late = matrices(
-        [],
-        [(cross, 0), (mate, HALO + LOWS + 1), (mate, OWN + HALO), (mate, OWN + RELAY + HALO)],
-        4,
-    )
+    cross = crossed(cross)
 
     def lists(found):
         mats, entry_slot, entry_win, entry_count = found
         return entry_slot, entry_win, entry_count, kept(mats)
 
     listed = [smem()] * 3 + [hbm()]
+    *late, begun = call(
+        late_kernel,
+        [
+            ((2 * LATE, WIN, BLK), BF16, hbm(), pltpu.HBM),
+            ((2 * LATE + 8,), jnp.int32, smem()),
+            ((2 * LATE + 8,), jnp.int32, smem()),
+            ((1,), jnp.int32, smem()),
+            ((16, CELLS + WIN), F32, vmem()),
+        ],
+        [free()] + listed + [vmem()] * 2,
+        [
+            pltpu.VMEM((3, ROUTE, 16, BLK), BF16),
+            pltpu.VMEM((STEN, LATE, BLK), F32),
+            pltpu.VMEM((STEN, 2 * LATE, BLK), F32),
+            pltpu.VMEM((1, BLK), jnp.int32),
+            pltpu.SMEM((1, BLK), jnp.int32),
+            pltpu.VMEM((HOME * 4 + 8, BLK), F32),
+            pltpu.VMEM((RING, PACK, WIN, BLK), BF16),
+            pltpu.VMEM((RING, PACK, WIN, BLK), BF16),
+            pltpu.SemaphoreType.DMA((3,)),
+            pltpu.SemaphoreType.DMA((RING,)),
+            pltpu.SemaphoreType.DMA((RING,)),
+            pltpu.SemaphoreType.DMA,
+        ],
+        4,
+        24,
+    )(mate, *lists(first), b_home, f_home)
+
     return call(
         spread_kernel,
         [((4, 4, CELLS), F32, vmem())],
-        [smem()] * 2 + [hbm()] + listed * 3 + [free()] * 5 + [vmem()] * 7,
+        [smem(), hbm()] + listed * 2 + [free()] * 2 + [vmem(), free()] + [vmem()] * 6,
         [
             pltpu.SMEM((4,), F32),
-            pltpu.VMEM((SLOTS, 16, BLK), BF16),
-            pltpu.VMEM((SLOTS * 4 + 8, BLK), F32),
+            pltpu.VMEM((SLOTS - HOME, 16, BLK), BF16),
+            pltpu.VMEM(((SLOTS - HOME) * 4 + 8, BLK), F32),
             pltpu.VMEM((16, CELLS + WIN), F32),
-            pltpu.VMEM((3, RING, PACK, WIN, BLK), BF16),
+            pltpu.VMEM((2, RING, PACK, WIN, BLK), BF16),
+            pltpu.VMEM((ROUTE, 16, BLK), BF16),
+            pltpu.VMEM((STEN, OFFCAP, BLK), F32),
+            pltpu.VMEM((STEN, 2 * OFFCAP, BLK), F32),
+            pltpu.VMEM((1, BLK), jnp.int32),
+            pltpu.SMEM((1, BLK), jnp.int32),
+            pltpu.SMEM((2 * OFFCAP + 8,), jnp.int32),
+            pltpu.SMEM((2 * OFFCAP + 8,), jnp.int32),
+            pltpu.VMEM((PACK, WIN, BLK), BF16),
             pltpu.SemaphoreType.DMA((GROUPS + 2,)),
-            pltpu.SemaphoreType.DMA((3, RING)),
+            pltpu.SemaphoreType.DMA((2, RING)),
+            pltpu.SemaphoreType.DMA,
         ],
         4,
         24,
     )(
-        me, lev, kept(geo_coef), *lists(first), *lists(middle), *lists(late),
-        b_home, plus, minus, cross, mate, f_home, f_mate, f_plus, f_minus, f_cross, local, above,
+        lev, kept(geo_coef), *lists(middle), *lists(late),
+        plus, minus, cross, mate, f_mate, f_plus, f_minus, begun, local, above,
     )[0]
 
 

time: 75.5 us -> 70.4 us (0.932)
  the two profiles are of different devices: /device:TPU:205 before, /device:TPU:203 now
where the time goes in v5:
time: 70.4 us; the launch traced here: 69.9 us
  Pallas kernels  32.8 us (47%)
  starting transfers between devices  30.9 us (44%)
  waiting for transfers between devices  6.19 us (9%)
    ppermute x4, starting transfers between devices, moved(): lax.ppermute(parcel, 'tile', [(i, i + by) for i in range(peers) if 0 <= i...  10.6 us
    ppermute x1, starting transfers between devices, crossed(): lax.ppermute(parcel, 'tile', [(i, j) for i, j in pairs if 0 <= j < peers])  9.52 us
    pallas_call x1, Pallas kernels, body(): call(spread_kernel, [((4, 4, CELLS), F32, vmem())], [smem(), hbm()] + lis...  8.63 us
    pallas_call x2, Pallas kernels, matrices(): call(lambda *refs: matrix_kernel(count, len(home), [at for _, at in parts...  8.11 us
    pallas_call x1, Pallas kernels, body(): call(late_kernel, [((2 * LATE, WIN, BLK), BF16, hbm(), pltpu.HBM), ((2 *...  7.34 us
    all_to_all x1, starting transfers between devices, body(): above = lax.all_to_all(totals, 'lev', 0, 0)  7 us
    ppermute x4, waiting for transfers between devices, moved(): lax.ppermute(parcel, 'tile', [(i, i + by) for i in range(peers) if 0 <= i...  6.18 us
    pallas_call x1, Pallas kernels, body(): call(solve_kernel, [((8, NLON), F32, vmem()), ((peers, NBLK, BLK), BF16,...  4.99 us
  transfers between devices with their start and end apart: 7, of which 2 were waited for; matrix products, arithmetic and copies ran while one was open for 0% of the time, Pallas kernels for 22%

profile of v5, /device:TPU:203, one launch (start us, length us, event | category | flops | bytes accessed | tf_op | source)
XLA Modules:
  0.0 69.9 jit_solution(820643041947129181)
XLA Ops:
  0.0 2.7 %shard_map.73 = (s32[64]{0:T(128)S(1)}, bf16[25,32,128]{2,1,0:T(8,128)(2,1)S(1)}, bf16[32,16,128]{2,1,0:T(8,128)(2,1)S(1)}, bf16[90,16,128]{2,1,0:T(8,128)(2,1)S...) custom-call(s32[1]{0:T(128)} %bitcast.1.me, ...), custom_call_target="tpu_custom_call" | custom-call | flops 1000000 | bytes 3000000 | tf_op jit(solution)/shard_map/pallas_call | solution.py:587
  2.8 3.1 %collective-permute-start = (bf16[114,16,128]{2,1,0:T(8,128)(2,1)S(1)}, bf16[114,16,128]{2,1,0:T(8,128)(2,1)S(1)}, u32[]{:S(2)}, u32[]{:S(2)}) collective-permute-start(bf16[114,16,128]{2,1,0:T(8,128)(2,1)S(1)} %get-tuple-element.32), channel_id=1, source_target_pairs={{0,16},{8,24},{16,32},{24,40},{32,48},{40,56},{48,64},{56,72},{64,... | collective-permute-start | bytes 1400840 | tf_op jit(solution)/shard_map/ppermute | solution.py:535
  5.9 2.2 %collective-permute-start.1 = (bf16[114,16,128]{2,1,0:T(8,128)(2,1)S(1)}, bf16[114,16,128]{2,1,0:T(8,128)(2,1)S(1)}, u32[]{:S(2)}, u32[]{:S(2)}) collective-permute-start(bf16[114,16,128]{2,1,0:T(8,128)(2,1)S(1)} %get-tuple-element.33), channel_id=1, source_target_pairs={{16,0},{24,8},{32,16},{40,24},{48,32},{56,40},{64,48},{72,56},{80,... | collective-permute-start | bytes 1400840 | tf_op jit(solution)/shard_map/ppermute | solution.py:535
  8.1 4.8 %shard_map.75 = (bf16[64,256,128]{2,1,0:T(8,128)(2,1)}, s32[72]{0:T(128)S(1)}, s32[72]{0:T(128)S(1)}, s32[1]{0:T(128)}) custom-call(bf16[25,32,128]{2,1,0:T(8,128)(2,1)S(1)} %get-tuple-element.38.refs_0_), custom_call_target="tpu_custom_call" | custom-call | flops 40000000 | bytes 120000000 | tf_op jit(solution)/shard_map/pallas_call | solution.py:551
  12.8 3.4 %collective-permute-done.refs_0_.plus = bf16[114,16,128]{2,1,0:T(8,128)(2,1)S(1)} collective-permute-done((bf16[114,16,128]{2,1,0:T(8,128)(2,1)S(1)}, bf16[114,16,128]{2,1,0:T(8,128)(2,1)S(1)}, u32[]{:S(2)}, u32[]{:S(2)}) %collective-permute-start) | collective-permute-done | bytes 466976 | tf_op jit(solution)/shard_map/ppermute | solution.py:535
  16.2 2.8 %collective-permute-done.1.refs_1_.minus = bf16[114,16,128]{2,1,0:T(8,128)(2,1)S(1)} collective-permute-done((bf16[114,16,128]{2,1,0:T(8,128)(2,1)S(1)}, bf16[114,16,128]{2,1,0:T(8,128)(2,1)S(1)}, u32[]{:S(2)}, u32[]{:S(2)}) %collective-permute-start.1) | collective-permute-done | bytes 466976 | tf_op jit(solution)/shard_map/ppermute | solution.py:535
  19.0 0.9 %shard_map.76 = bf16[236,16,128]{2,1,0:T(8,128)(2,1)S(1)} custom-call(s32[1]{0:T(128)} %get-tuple-element.39._.count1, bf16[90,16,128]{2,1,0:T(8,128)(2,1)S(1)} %get-tuple-element.40.own, bf16[114,16,128]{2,1,0:T(8,128)(2,1)S(1)} %collective-permute-done.refs_0_.plus, bf16[114,16,128]{2,1,0:T(8,128)(2,1)S(1)} %collective-permute-done.1.refs_1_.minus), custom_call_target="tpu_custom_call" | custom-call | flops 1000000 | bytes 3000000 | tf_op jit(solution)/shard_map/pallas_call | solution.py:618
  20.0 3.8 %collective-permute-start.2 = (bf16[236,16,128]{2,1,0:T(8,128)(2,1)S(1)}, bf16[236,16,128]{2,1,0:T(8,128)(2,1)S(1)}, u32[]{:S(2)}, u32[]{:S(2)}) collective-permute-start(bf16[236,16,128]{2,1,0:T(8,128)(2,1)S(1)} %shard_map.76), channel_id=1, source_target_pairs={{0,8},{8,0},{16,24},{24,16},{32,40},{40,32},{48,56},{56,48},{64,72... | collective-permute-start | bytes 2899976 | tf_op jit(solution)/shard_map/ppermute | solution.py:539
  23.7 3.3 %shard_map.74 = (bf16[64,256,128]{2,1,0:T(8,128)(2,1)}, s32[72]{0:T(128)S(1)}, s32[72]{0:T(128)S(1)}, s32[1]{0:T(128)}) custom-call(bf16[114,16,128]{2,1,0:T(8,128)(2,1)S(1)} %collective-permute-done.refs_0_.plus, bf16[114,16,128]{2,1,0:T(8,128)(2,1)S(1)} %collective-permute-done.1.refs_1_.minus), custom_call_target="tpu_custom_call" | custom-call | flops 10000000 | bytes 30000000 | tf_op jit(solution)/shard_map/pallas_call | solution.py:551
  27.1 0.0 collective-permute-done.2.mate
  27.1 5.0 %shard_map.77 = (f32[8,4096]{1,0:T(8,128)S(1)}, bf16[8,64,128]{2,1,0:T(8,128)(2,1)}, bf16[128,128]{1,0:T(8,128)(2,1)S(1)}, bf16[64,128]{1,0:T(8,128)(2,1)S(1)}, ...) custom-call(s32[1]{0:T(128)} %bitcast.1.me, ...), custom_call_target="tpu_custom_call" | custom-call | flops 2000000 | bytes 6000000 | tf_op jit(solution)/shard_map/pallas_call | solution.py:630
  32.1 7.0 %all-to-all-start = ((bf16[8,64,128]{2,1,0:T(8,128)(2,1)}), bf16[8,64,128]{2,1,0:T(8,128)(2,1)S(1)}, u32[]{:S(2)}, u32[]{:S(2)}) async-start(bf16[8,64,128]{2,1,0:T(8,128)(2,1)} %get-tuple-element.58), calls=%async_computation | async-start | bytes 262144 | tf_op jit(solution)/shard_map/all_to_all | solution.py:660
  39.1 9.5 %collective-permute-start.3 = (bf16[45,16,128]{2,1,0:T(8,128)(2,1)S(1)}, bf16[45,16,128]{2,1,0:T(8,128)(2,1)S(1)}, u32[]{:S(2)}, u32[]{:S(2)}) collective-permute-start(bf16[45,16,128]{2,1,0:T(8,128)(2,1)S(1)} %get-tuple-element.52), channel_id=1, source_target_pairs={{8,32},{24,48},{32,8},{40,64},{48,24},{56,80},{64,40},{72,96},{80,... | collective-permute-start | bytes 552968 | tf_op jit(solution)/shard_map/ppermute | solution.py:545
  48.6 1.9 %collective-permute-start.4 = (bf16[128,128]{1,0:T(8,128)(2,1)S(1)}, bf16[128,128]{1,0:T(8,128)(2,1)S(1)}, u32[]{:S(2)}, u32[]{:S(2)}) collective-permute-start(bf16[128,128]{1,0:T(8,128)(2,1)S(1)} %get-tuple-element.54), channel_id=1, source_target_pairs={{0,16},{8,24},{16,32},{24,40},{32,48},{40,56},{48,64},{56,72},{64,... | collective-permute-start | bytes 98312 | tf_op jit(solution)/shard_map/ppermute | solution.py:535
  50.6 3.4 %collective-permute-start.5 = (bf16[128,128]{1,0:T(8,128)(2,1)S(1)}, bf16[128,128]{1,0:T(8,128)(2,1)S(1)}, u32[]{:S(2)}, u32[]{:S(2)}) collective-permute-start(bf16[128,128]{1,0:T(8,128)(2,1)S(1)} %get-tuple-element.55), channel_id=1, source_target_pairs={{16,0},{24,8},{32,16},{40,24},{48,32},{56,40},{64,48},{72,56},{80,... | collective-permute-start | bytes 98312 | tf_op jit(solution)/shard_map/ppermute | solution.py:535
  53.9 7.3 %shard_map.78 = (bf16[96,256,128]{2,1,0:T(8,128)(2,1)}, s32[104]{0:T(128)S(1)}, s32[104]{0:T(128)S(1)}, s32[1]{0:T(128)}, f32[16,8448]{1,0:T(8,128)S(1)}) custom-call(bf16[236,16,128]{2,1,0:T(8,128)(2,1)S(1)} %collective-permute-done.2.mate, s32[72]{0:T(128)S(1)} %get-tuple-element.41.slot1, s32[72]{0:T(128)S(1)} %get-tuple-element.42.win1, ...), custom_call_target="tpu_custom_call" | custom-call | flops 4000000 | bytes 12000000 | tf_op jit(solution)/shard_map/pallas_call | solution.py:670
  61.3 0.0 collective-permute-done.4.f_plus
  61.3 0.0 collective-permute-done.5.f_minus
  61.3 0.0 collective-permute-done.3.cross
  61.3 0.0 all-to-all-done.above
  61.3 8.6 %shard_map.79 = f32[4,4,8192]{2,1,0:T(4,128)} custom-call(s32[1]{0:T(128)} %bitcast.lev, f32[4]{0:T(128)} %geo_in.1, s32[72]{0:T(128)S(1)} %get-tuple-element.34.slot2, s32[72]{0:T(128)S(1)} %get-tuple-element.35.win2, s32[1]{0:T(128)} %get-tuple-element.36._.count2, bf16[64,256,128]{2,1,0:T(8,128)(2,1)} %get-tuple-element.37.mats2, ...), custom_call_target="tpu_custom_call" | custom-call | flops 4000000 | bytes 12000000 | tf_op jit(solution)/shard_map/pallas_call | solution.py:698
Async XLA Ops:
  2.8 13.5 %collective-permute-start = (bf16[114,16,128]{2,1,0:T(8,128)(2,1)S(1)}, bf16[114,16,128]{2,1,0:T(8,128)(2,1)S(1)}, u32[]{:S(2)}, u32[]{:S(2)}) collective-permute-start(bf16[114,16,128]{2,1,0:T(8,128)(2,1)S(1)} %get-tuple-element.32), channel_id=1, source_target_pairs={{0,16},{8,24},{16,32},{24,40},{32,48},{40,56},{48,64},{56,72},{64,... | collective-permute-start | bytes 1400840 | tf_op jit(solution)/shard_map/ppermute | solution.py:535
  5.9 13.1 %collective-permute-start.1 = (bf16[114,16,128]{2,1,0:T(8,128)(2,1)S(1)}, bf16[114,16,128]{2,1,0:T(8,128)(2,1)S(1)}, u32[]{:S(2)}, u32[]{:S(2)}) collective-permute-start(bf16[114,16,128]{2,1,0:T(8,128)(2,1)S(1)} %get-tuple-element.33), channel_id=1, source_target_pairs={{16,0},{24,8},{32,16},{40,24},{48,32},{56,40},{64,48},{72,56},{80,... | collective-permute-start | bytes 1400840 | tf_op jit(solution)/shard_map/ppermute | solution.py:535
  20.0 7.1 %collective-permute-start.2 = (bf16[236,16,128]{2,1,0:T(8,128)(2,1)S(1)}, bf16[236,16,128]{2,1,0:T(8,128)(2,1)S(1)}, u32[]{:S(2)}, u32[]{:S(2)}) collective-permute-start(bf16[236,16,128]{2,1,0:T(8,128)(2,1)S(1)} %shard_map.76), channel_id=1, source_target_pairs={{0,8},{8,0},{16,24},{24,16},{32,40},{40,32},{48,56},{56,48},{64,72... | collective-permute-start | bytes 2899976 | tf_op jit(solution)/shard_map/ppermute | solution.py:539
  32.1 29.2 %all-to-all-start = ((bf16[8,64,128]{2,1,0:T(8,128)(2,1)}), bf16[8,64,128]{2,1,0:T(8,128)(2,1)S(1)}, u32[]{:S(2)}, u32[]{:S(2)}) async-start(bf16[8,64,128]{2,1,0:T(8,128)(2,1)} %get-tuple-element.58), calls=%async_computation | async-start | bytes 262144 | tf_op jit(solution)/shard_map/all_to_all | solution.py:660
  39.1 22.2 %collective-permute-start.3 = (bf16[45,16,128]{2,1,0:T(8,128)(2,1)S(1)}, bf16[45,16,128]{2,1,0:T(8,128)(2,1)S(1)}, u32[]{:S(2)}, u32[]{:S(2)}) collective-permute-start(bf16[45,16,128]{2,1,0:T(8,128)(2,1)S(1)} %get-tuple-element.52), channel_id=1, source_target_pairs={{8,32},{24,48},{32,8},{40,64},{48,24},{56,80},{64,40},{72,96},{80,... | collective-permute-start | bytes 552968 | tf_op jit(solution)/shard_map/ppermute | solution.py:545
  48.6 12.7 %collective-permute-start.4 = (bf16[128,128]{1,0:T(8,128)(2,1)S(1)}, bf16[128,128]{1,0:T(8,128)(2,1)S(1)}, u32[]{:S(2)}, u32[]{:S(2)}) collective-permute-start(bf16[128,128]{1,0:T(8,128)(2,1)S(1)} %get-tuple-element.54), channel_id=1, source_target_pairs={{0,16},{8,24},{16,32},{24,40},{32,48},{40,56},{48,64},{56,72},{64,... | collective-permute-start | bytes 98312 | tf_op jit(solution)/shard_map/ppermute | solution.py:535
  50.6 10.7 %collective-permute-start.5 = (bf16[128,128]{1,0:T(8,128)(2,1)S(1)}, bf16[128,128]{1,0:T(8,128)(2,1)S(1)}, u32[]{:S(2)}, u32[]{:S(2)}) collective-permute-start(bf16[128,128]{1,0:T(8,128)(2,1)S(1)} %get-tuple-element.55), channel_id=1, source_target_pairs={{16,0},{24,8},{32,16},{40,24},{48,32},{56,40},{64,48},{72,56},{80,... | collective-permute-start | bytes 98312 | tf_op jit(solution)/shard_map/ppermute | solution.py:535

commit v6 on v3

v6 whole, which is shorter than its diff:
```python
import jax
import jax.numpy as jnp
from jax import lax
from jax.experimental import pallas as pl
from jax.experimental.pallas import tpu as pltpu
from jax.sharding import PartitionSpec as P

NLON = 4096
BLK = 128
WIN = 256
SWEEPS = 4
REACH = 3
HOME = 32
OFFCAP = 16

F32 = jnp.float32
BF16 = jnp.bfloat16
STEN = 12
NBLK = 64
CELLS = 8192
NWIN = CELLS // WIN
OFFSETS = (-3, -2, -1, 1, 2, 3)
SLOTS = HOME + OFFCAP * len(OFFSETS)
HALO = NLON // BLK
ROUTE = 2 * STEN + 1
LOAD = ROUTE + OFFCAP
LOWS = HALO // 2
MATE = HALO + LOWS + 1
MATE_PLUS = MATE + LOAD
MATE_MINUS = MATE_PLUS + LOAD
RELAY_PLUS = MATE_MINUS + LOAD
RELAY_MINUS = RELAY_PLUS + HALO
OWN = RELAY_MINUS + HALO
NEAR = HOME + OFFCAP
FAR = 5 * OFFCAP
CROSS = LOAD + 4
PAIR = 2 * LOAD + 8
PACK = 4
REMAINDER = 1e-6


def vmem():
    return pl.BlockSpec(memory_space=pltpu.VMEM)


def smem():
    return pl.BlockSpec(memory_space=pltpu.SMEM)


def free():
    return pl.BlockSpec(memory_space=pl.ANY)


def hbm():
    return pl.BlockSpec(memory_space=pltpu.HBM)


def kept(array):
    return pltpu.with_memory_space_constraint(array, pltpu.HBM)


def lanes(i):
    return slice(i * BLK, (i + 1) * BLK)


def base_of(by):
    return 0 if by == 0 else HOME + OFFCAP * OFFSETS.index(by)


def either(core, first, second):
    return pl.multiple_of(jnp.where(core == 0, base_of(first), base_of(second)), OFFCAP)


def launch(copies):
    copies = [pltpu.make_async_copy(*copy) for copy in copies]
    for copy in copies:
        copy.start()
    return copies


def finish(copies):
    for copy in copies:
        copy.wait()


def call(kernel, outs, ins, scratch, cost, limit, aliases=None):
    return pl.pallas_call(
        kernel,
        out_shape=[(out[3] if out[3:] else jax.ShapeDtypeStruct)(out[0], out[1]) for out in outs],
        out_specs=[out[2] for out in outs],
        in_specs=ins,
        scratch_shapes=scratch,
        input_output_aliases=aliases or {},
        compiler_params=pltpu.CompilerParams(vmem_limit_bytes=limit << 20),
        cost_estimate=pl.CostEstimate(flops=cost * 1000000, bytes_accessed=cost * 3000000, transcendentals=0),
    )


def halo_pieces(first, helm):
    for i in range(HALO):
        coef = jnp.concatenate([helm[:, lanes(i)], helm[:, lanes(HALO + i)]], axis=0)
        side = [first[:, lanes(i)].astype(F32), first[:, lanes(HALO + i)].astype(F32)]
        yield i, coef, jnp.concatenate(side + [coef], axis=0).astype(BF16)


def halo_kernel(adj_in, helm_in, out, first, helm, sems):
    finish(launch([(adj_in.at[0], first, sems.at[0]), (helm_in, helm, sems.at[1])]))
    for i, _, piece in halo_pieces(first, helm):
        out[i] = piece


def pack_kernel(
    me, dest_in, win_in, adj_in, helm_in, cell_in, weight_in,
    slots, a_home, b_home, own, plus, minus, cross,
    dest, win, adj, helm, cell, weight, count, a_all, b_all, sems,
):
    pairs = ((dest_in, dest), (win_in, win), (adj_in, adj), (helm_in, helm), (cell_in, cell), (weight_in, weight))
    copies = launch([(a, b, sems.at[i]) for i, (a, b) in enumerate(pairs)])
    core = lax.rem(me[0], 2)
    for by in range(-REACH, REACH + 1):
        count[by + REACH] = base_of(by)
    a_all[...] = jnp.zeros_like(a_all)
    b_all[...] = jnp.zeros_like(b_all)
    finish(copies)
    lane = lax.broadcasted_iota(jnp.int32, (16, BLK), 1)
    table = jnp.zeros((16, BLK), jnp.int32)
    for b in range(NBLK):
        route = dest[b] - me[0] + REACH
        slot = count[route]
        count[route] = slot + 1
        slots[b] = slot
        table = jnp.where(lane == b, slot, table)
        a_all[pl.ds(slot, STEN, stride=SLOTS), :] = weight[:, lanes(b)].astype(F32)
        a_all[pl.ds(STEN * SLOTS + slot, STEN, stride=SLOTS), :] = cell[:, lanes(b)].astype(F32)
        a_all[pl.ds(2 * STEN * SLOTS + slot, 1), :] = jnp.full((1, BLK), win[b] + 1, jnp.int32).astype(F32)
        b_all[slot] = jnp.concatenate([adj[f, :, lanes(b)].astype(F32) for f in range(4)], axis=0).astype(BF16)
    for r in range(ROUTE):
        a_home[r] = a_all[r * SLOTS : r * SLOTS + HOME, :].astype(BF16)
    b_home[...] = b_all[:HOME]
    loads = (
        (own, MATE, either(core, 1, -1)),
        (own, MATE_PLUS, either(core, 3, 1)),
        (own, MATE_MINUS, either(core, -1, -3)),
        (plus, 0, either(core, 2, 2)),
        (minus, 0, either(core, -2, -2)),
        (cross, 0, either(core, -3, 3)),
    )
    for parcel, at, base in loads:
        for r in range(ROUTE):
            parcel[at + r] = a_all[pl.ds(r * SLOTS + base, OFFCAP), :].astype(BF16)
        parcel[at + ROUTE : at + LOAD] = b_all[pl.ds(base, OFFCAP)]
    rest = []
    for i, coef, piece in halo_pieces(adj.at[0], helm):
        rest.append(coef - coef.astype(BF16).astype(F32))
        own[i] = piece
    for i in range(LOWS):
        own[HALO + i] = jnp.concatenate(rest[2 * i : 2 * i + 2], axis=0).astype(BF16)
    own[HALO + LOWS] = table.astype(F32).astype(BF16)
    own[RELAY_PLUS:] = jnp.zeros((2 * HALO, 16, BLK), BF16)


def relay_kernel(_, plus, minus, out, sems):
    finish(
        launch(
            [
                (plus, out.at[pl.ds(RELAY_PLUS, HALO)], sems.at[0]),
                (minus, out.at[pl.ds(RELAY_MINUS, HALO)], sems.at[1]),
            ]
        )
    )


def solve_kernel(
    me, slots, helm_in, own, plus, minus, mate, plus_in, minus_in, cross_in,
    local, totals, f_home, f_mate, f_plus, f_minus, cross,
    helm, halo, lows, rhs, coef, result, table, table_s, mine_all, mate_all, t_all, sems, table_sem,
):
    core = lax.rem(me[0], 2)
    tables = launch([(mate.at[pl.ds(HALO, LOWS + 1)], lows, sems.at[7])])
    forward = (
        (plus_in, f_plus.at[pl.ds(0, LOAD)]),
        (mate.at[pl.ds(MATE_PLUS, LOAD)], f_plus.at[pl.ds(LOAD, LOAD)]),
        (minus_in, f_minus.at[pl.ds(0, LOAD)]),
        (mate.at[pl.ds(MATE_MINUS, LOAD)], f_minus.at[pl.ds(LOAD, LOAD)]),
        (cross_in, cross.at[pl.ds(0, LOAD)]),
    )
    pairs = (
        (helm_in, helm),
        (plus, halo.at[core]),
        (mate.at[pl.ds(RELAY_PLUS, HALO)], halo.at[1 - core]),
        (own, halo.at[2 + core]),
        (mate.at[pl.ds(0, HALO)], halo.at[3 - core]),
        (minus, halo.at[4 + core]),
        (mate.at[pl.ds(RELAY_MINUS, HALO)], halo.at[5 - core]),
    )
    copies = launch([(a, b, sems.at[i]) for i, (a, b) in enumerate(pairs)])
    passed = launch([(a, b, sems.at[8 + i]) for i, (a, b) in enumerate(forward)])
    mine_all[...] = jnp.zeros_like(mine_all)
    mate_all[...] = jnp.zeros_like(mate_all)
    finish(tables)
    table[...] = lows[LOWS].astype(F32)[:1].astype(jnp.int32)
    tables = launch([(table, table_s, table_sem)])
    finish(copies)
    for band in range(6):
        for i in range(HALO):
            tile = halo[band, i].astype(F32)
            rhs[band, :, lanes(i)] = tile[:8]
            coef[band, :, lanes(i)] = tile[8:]
    for i in range(LOWS):
        tile = lows[i].astype(F32)
        coef[3 - core, :, lanes(2 * i)] += tile[:8]
        coef[3 - core, :, lanes(2 * i + 1)] += tile[8:]
    coef[2 + core] = jnp.concatenate([helm[:, :NLON], helm[:, NLON:]], axis=0)
    right = [rhs[band] for band in range(6)]
    factor = [coef[band] for band in range(6)]
    scale = [1.0 / (1.0 + 4.0 * c) for c in factor]
    solved = [r * s for r, s in zip(right, scale)]
    upper = lax.broadcasted_iota(jnp.int32, (8, NLON), 0) < 4
    for wanted in ((0, 1, 2, 3, 4, 5), (1, 2, 3, 4), (1, 2, 3, 4), (2, 3)):
        shifted = [c * s for c, s in zip(factor, solved)]
        turned = [pltpu.roll(p, 4, 0) for p in shifted]
        fresh = list(solved)
        for band in wanted:
            p = shifted[band]
            north = turned[max(band - 1, 0)]
            south = turned[min(band + 1, 5)]
            total = turned[band] + jnp.where(upper, north, south)
            total = total + pltpu.roll(p, 1, 1) + pltpu.roll(p, NLON - 1, 1)
            fresh[band] = (right[band] + total) * scale[band]
        solved = fresh
    result[0] = solved[2]
    result[1] = solved[3]
    mine = result[core]
    other = result[1 - core]
    finish(tables)
    for r in range(2):
        sums = mine[4 * r : 4 * r + 1]
        local[4 * r : 4 * r + 1, :] = sums
        for level in range(1, 4):
            sums = sums + mine[4 * r + level : 4 * r + level + 1]
            local[4 * r + level : 4 * r + level + 1, :] = sums
        for i in range(HALO):
            b = HALO * r + i
            t_all[b : b + 1, :] = sums[:, lanes(i)]
            mine_all[pl.ds(slots[b] * 4, 4), :] = mine[4 * r : 4 * r + 4, lanes(i)]
            mate_all[pl.ds(table_s[0, b] * 4, 4), :] = other[4 * r : 4 * r + 4, lanes(i)]
    totals_here = t_all[...].astype(BF16)
    for i in range(totals.shape[0]):
        totals[i] = totals_here

    def part(source, first, second):
        return source[pl.ds(either(core, first, second) * 4, OFFCAP * 4), :].astype(BF16)

    f_home[...] = mine_all[: HOME * 4].astype(BF16)
    f_mate[...] = part(mate_all, -1, 1)
    sent = (
        (f_plus, 2 * LOAD, part(mine_all, 2, 2)),
        (f_plus, 2 * LOAD + 4, part(mate_all, 1, 3)),
        (f_minus, 2 * LOAD, part(mine_all, -2, -2)),
        (f_minus, 2 * LOAD + 4, part(mate_all, -3, -1)),
        (cross, LOAD, part(mine_all, -3, 3)),
    )
    for parcel, at, piece in sent:
        for i in range(4):
            parcel[at + i] = piece[16 * i : 16 * i + 16]
    finish(passed)


def merge(load, cells, merged, count, base):
    w = [load(k) for k in range(STEN)]
    c = [load(STEN + k) for k in range(STEN)]
    total = list(w)
    for k in range(STEN):
        for m in range(k):
            same = c[k] == c[m]
            total[k] = total[k] + jnp.where(same, w[m], 0.0)
            total[m] = total[m] + jnp.where(same, w[k], 0.0)
    lost = jnp.zeros((8, BLK), F32)
    held = jnp.zeros((8, BLK), F32)
    for k in range(STEN):
        high = total[k].astype(BF16).astype(F32)
        low = total[k] - high
        cells[k, base : base + 8, :] = c[k]
        merged[k, base : base + 8, :] = high
        merged[k, count + base : count + base + 8, :] = low
        lost = lost + low * low
        held = held + w[k] * w[k]
    more = jnp.sum(lost, axis=1, keepdims=True) > REMAINDER * jnp.sum(held, axis=1, keepdims=True)
    mark = load(2 * STEN)
    mark = jnp.where(mark > 0.0, mark + jnp.where(more, 64.0, 0.0), 0.0)
    lane = lax.broadcasted_iota(jnp.int32, (8, BLK), 1)
    row = lax.broadcasted_iota(jnp.int32, (8, BLK), 0)
    return jnp.where(lane == row + base, mark, 0.0)


def merge_all(groups, cells, merged, count, meta):
    marks = jnp.zeros((8, BLK), F32)
    for i, group in enumerate(groups):
        rows = group()
        for half in (0, 8):
            marks = marks + merge(lambda r: rows[r][half : half + 8], cells, merged, count, 16 * i + half)
    meta[...] = jnp.sum(marks, axis=0, keepdims=True).astype(jnp.int32)


def enlist(meta_s, count, entry_slot, entry_win):
    def eight(i, n):
        for j in range(8):
            slot = i * 8 + j
            mark = meta_s[0, slot]
            window = (mark & 63) - 1
            entry_slot[n + 1] = slot
            entry_win[n + 1] = window
            n = n + (mark > 0).astype(jnp.int32)
            entry_slot[n + 1] = slot + count
            entry_win[n + 1] = window
            n = n + (mark >= 64).astype(jnp.int32)
        return n

    n = lax.fori_loop(0, count // 8, eight, jnp.int32(0))
    for at in [0] + [n + 1 + j for j in range(PACK)]:
        entry_slot[at] = 0
        entry_win[at] = NWIN
    return n


def spread(parts, count, cells, merged, meta, meta_s, entry_slot, entry_win, values, firsts, mats, total, meta_sem, ready):
    merge_all(parts, cells, merged, count, meta)
    finish(launch([(meta, meta_s, meta_sem)]))
    n = enlist(meta_s, count, entry_slot, entry_win)
    ready()
    iota = lax.broadcasted_iota(jnp.int32, (16, BLK), 0).astype(F32)
    first_rows = lax.broadcasted_iota(jnp.int32, (8, BLK), 0) < 4
    mats[PACK - 1] = jnp.zeros((WIN, BLK), BF16)

    def multiply(at, mat):
        slot = lax.rem(entry_slot[at], count)
        tile = values[slot].astype(F32)
        head = jnp.where(first_rows, firsts[pl.ds(slot * 4, 8), :], tile[:8])
        left = jnp.concatenate([head, tile[8:]], axis=0).astype(BF16)
        return lax.dot_general(left, mat[...], (((1,), (1,)), ((), ())), preferred_element_type=F32)

    def build(at, mat):
        entry = entry_slot[at]
        slot = lax.rem(entry, count)
        c = [jnp.broadcast_to(cells[k, pl.ds(slot, 1), :], (16, BLK)).astype(BF16) for k in range(STEN)]
        w = [jnp.broadcast_to(merged[k, pl.ds(entry, 1), :], (16, BLK)).astype(BF16) for k in range(STEN)]
        for i in range(WIN // 16):
            here = (iota + 16.0 * i).astype(BF16)
            m = jnp.zeros((16, BLK), BF16)
            for k in range(STEN):
                m = jnp.where(c[k] == here, w[k], m)
            mat[16 * i : 16 * i + 16, :] = m

    def add(at, product):
        start = pl.multiple_of(entry_win[at] * WIN, WIN)
        total[:, pl.ds(start, WIN)] += product

    def step(group, carry):
        for j in range(PACK):
            at = group * PACK + j
            product = multiply(at, mats.at[(j - 1) % PACK])
            build(at + 1, mats.at[j])
            add(at, product)
        return carry

    groups = (n + PACK - 1) // PACK
    lax.fori_loop(0, groups, step, 0)
    add(groups * PACK, multiply(groups * PACK, mats.at[PACK - 1]))


def spread_scratch(count):
    return [
        pltpu.VMEM((STEN, count, BLK), F32),
        pltpu.VMEM((STEN, 2 * count, BLK), F32),
        pltpu.VMEM((1, BLK), jnp.int32),
        pltpu.SMEM((1, BLK), jnp.int32),
        pltpu.SMEM((2 * count + 8,), jnp.int32),
        pltpu.SMEM((2 * count + 8,), jnp.int32),
        pltpu.VMEM((count, 16, BLK), BF16),
        pltpu.VMEM((count * 4 + 8, BLK), F32),
        pltpu.VMEM((PACK, WIN, BLK), BF16),
    ]


def arrival(copy, tiles):
    def rows():
        copy.wait()
        return [tiles[r].astype(F32) for r in range(ROUTE)]

    return rows


def near_kernel(
    mate, a_home, b_home, f_home, f_mate, total,
    a_in, cells, merged, meta, meta_s, entry_slot, entry_win, values, firsts, mats, sems, meta_sem,
):
    routes = launch([(mate.at[pl.ds(MATE, ROUTE)], a_in, sems.at[0])])
    copies = launch([(mate.at[pl.ds(MATE + ROUTE, OFFCAP)], values.at[pl.ds(HOME, OFFCAP)], sems.at[1])])
    total[...] = jnp.zeros_like(total)
    values[:HOME] = b_home[...]
    firsts[: HOME * 4, :] = f_home[...].astype(F32)
    firsts[HOME * 4 : NEAR * 4, :] = f_mate[...].astype(F32)
    firsts[NEAR * 4 :, :] = jnp.zeros((8, BLK), F32)

    def own_rows(at):
        return lambda: [a_home[r, at : at + 16, :].astype(F32) for r in range(ROUTE)]

    parts = [own_rows(at) for at in range(0, HOME, 16)] + [arrival(routes[0], a_in)]
    spread(
        parts, NEAR, cells, merged, meta, meta_s, entry_slot, entry_win, values, firsts, mats, total, meta_sem,
        lambda: finish(copies),
    )


def far_kernel(
    lev, geo_in, plus, minus, cross, begun, local, above,
    out, geo, total, a_in, cells, merged, meta, meta_s, entry_slot, entry_win, values, firsts, mats, sems, meta_sem,
):
    parts = (
        (plus, 0, 2 * LOAD),
        (plus, LOAD, 2 * LOAD + 4),
        (minus, 0, 2 * LOAD),
        (minus, LOAD, 2 * LOAD + 4),
        (cross, 0, LOAD),
    )
    count = len(parts)
    routes = launch([(p.at[pl.ds(at, ROUTE)], a_in.at[i], sems.at[i]) for i, (p, at, _) in enumerate(parts)])
    pairs = [
        (p.at[pl.ds(at + ROUTE, OFFCAP)], values.at[pl.ds(OFFCAP * i, OFFCAP)]) for i, (p, at, _) in enumerate(parts)
    ]
    pairs += [(geo_in, geo)]
    copies = launch([(a, b, sems.at[count + i]) for i, (a, b) in enumerate(pairs)])
    total[...] = begun[...]
    for i, (p, _, at) in enumerate(parts):
        for j in range(4):
            row = OFFCAP * 4 * i + 16 * j
            firsts[row : row + 16, :] = p[at + j].astype(F32)
    firsts[FAR * 4 :, :] = jnp.zeros((8, BLK), F32)
    spread(
        [arrival(copy, a_in.at[i]) for i, copy in enumerate(routes)],
        FAR, cells, merged, meta, meta_s, entry_slot, entry_win, values, firsts, mats, total, meta_sem,
        lambda: finish(copies),
    )

    sums = jnp.zeros((NBLK, BLK), F32)
    for peer in range(above.shape[0]):
        sums = sums + jnp.where(peer < lev[0], above[peer].astype(F32), 0.0)
    level = lax.broadcasted_iota(jnp.int32, (4, BLK), 0)
    factor = jnp.zeros((4, BLK), F32)
    for i in range(4):
        factor = jnp.where(level == i, geo[i], factor)
    for f in (0, 1, 3):
        out[f] = total[4 * f : 4 * f + 4, :CELLS]
    for b in range(NBLK):
        r = b // HALO
        term = factor * (local[4 * r : 4 * r + 4, lanes(b % HALO)] + sums[b : b + 1])
        out[2, :, lanes(b)] = total[8:12, lanes(b)] + term


def moved(parcel, by):
    peers = lax.axis_size("tile")
    return lax.ppermute(parcel, "tile", [(i, i + by) for i in range(peers) if 0 <= i + by < peers])


def swapped(parcel):
    return lax.ppermute(parcel, "tile", [(i, i ^ 1) for i in range(lax.axis_size("tile"))])


def crossed(parcel):
    peers = lax.axis_size("tile")
    pairs = [(i, i + (3 if i % 2 else -3)) for i in range(peers)]
    return lax.ppermute(parcel, "tile", [(i, j) for i, j in pairs if 0 <= j < peers])


def body(adj_in, helm_coef, geo_coef, dest_tile, src_window, src_cell, interp_w):
    me = lax.axis_index("tile").astype(jnp.int32)[None]
    lev = lax.axis_index("lev").astype(jnp.int32)[None]
    peers = lax.axis_size("lev")

    def parcel(entries):
        return ((entries, 16, BLK), BF16, vmem())

    def strip(blocks):
        return ((blocks * 4, BLK), BF16, vmem())

    halo = call(
        halo_kernel,
        [parcel(HALO)],
        [hbm()] * 2,
        [pltpu.VMEM(adj_in.shape[1:], BF16), pltpu.VMEM(helm_coef.shape, F32), pltpu.SemaphoreType.DMA((2,))],
        1,
        16,
    )(kept(adj_in), kept(helm_coef))[0]
    plus = moved(halo, 2)
    minus = moved(halo, -2)

    slots, a_home, b_home, own, same_plus, same_minus, cross = call(
        pack_kernel,
        [
            ((NBLK,), jnp.int32, smem()),
            ((ROUTE, HOME, BLK), BF16, vmem()),
            parcel(HOME),
            parcel(OWN),
            parcel(LOAD),
            parcel(LOAD),
            parcel(LOAD),
        ],
        [smem()] + [hbm()] * 6,
        [
            pltpu.SMEM((NBLK,), jnp.int32),
            pltpu.SMEM((NBLK,), jnp.int32),
            pltpu.VMEM(adj_in.shape, BF16),
            pltpu.VMEM(helm_coef.shape, F32),
            pltpu.VMEM(src_cell.shape, jnp.int32),
            pltpu.VMEM(interp_w.shape, BF16),
            pltpu.SMEM((2 * REACH + 1,), jnp.int32),
            pltpu.VMEM((ROUTE * SLOTS, BLK), F32),
            pltpu.VMEM((SLOTS, 16, BLK), BF16),
            pltpu.SemaphoreType.DMA((6,)),
        ],
        20,
        24,
    )(me, *map(kept, (dest_tile[:, 0], src_window, adj_in, helm_coef, src_cell, interp_w)))

    relayed = call(
        relay_kernel,
        [((OWN, 16, BLK), BF16, free())],
        [free()] * 3,
        [pltpu.SemaphoreType.DMA((2,))],
        1,
        16,
        {0: 0},
    )(own, plus, minus)[0]
    mate = swapped(relayed)

    local, totals, f_home, f_mate, f_plus, f_minus, cross = call(
        solve_kernel,
        [
            ((8, NLON), F32, vmem()),
            ((peers, NBLK, BLK), BF16, vmem()),
            strip(HOME),
            strip(OFFCAP),
            parcel(PAIR),
            parcel(PAIR),
            parcel(CROSS),
        ],
        [smem()] * 2 + [hbm()] + [free()] * 7,
        [
            pltpu.VMEM(helm_coef.shape, F32),
            pltpu.VMEM((6, HALO, 16, BLK), BF16),
            pltpu.VMEM((LOWS + 1, 16, BLK), BF16),
            pltpu.VMEM((6, 8, NLON), F32),
            pltpu.VMEM((6, 8, NLON), F32),
            pltpu.VMEM((2, 8, NLON), F32),
            pltpu.VMEM((1, BLK), jnp.int32),
            pltpu.SMEM((1, BLK), jnp.int32),
            pltpu.VMEM((SLOTS * 4, BLK), F32),
            pltpu.VMEM((SLOTS * 4, BLK), F32),
            pltpu.VMEM((NBLK, BLK), F32),
            pltpu.SemaphoreType.DMA((13,)),
            pltpu.SemaphoreType.DMA,
        ],
        2,
        24,
    )(me, slots, kept(helm_coef), halo, plus, minus, mate, same_plus, same_minus, cross)
    f_plus = moved(f_plus, 2)
    f_minus = moved(f_minus, -2)
    cross = crossed(cross)
    above = lax.all_to_all(totals, "lev", 0, 0)

    begun = call(
        near_kernel,
        [((16, CELLS + WIN), F32, vmem())],
        [free()] + [vmem()] * 4,
        [pltpu.VMEM((ROUTE, 16, BLK), BF16)]
        + spread_scratch(NEAR)
        + [pltpu.SemaphoreType.DMA((2,)), pltpu.SemaphoreType.DMA],
        8,
        16,
    )(mate, a_home, b_home, f_home, f_mate)[0]

    return call(
        far_kernel,
        [((4, 4, CELLS), F32, vmem())],
        [smem(), hbm()] + [vmem()] * 6,
        [
            pltpu.SMEM((4,), F32),
            pltpu.VMEM((16, CELLS + WIN), F32),
            pltpu.VMEM((5, ROUTE, 16, BLK), BF16),
        ]
        + spread_scratch(FAR)
        + [pltpu.SemaphoreType.DMA((11,)), pltpu.SemaphoreType.DMA],
        4,
        16,
    )(lev, kept(geo_coef), f_plus, f_minus, cross, begun, local, above)[0]


def solution(mesh):
    placed = (
        P(None, "lev", "tile"),
        P("lev", "tile"),
        P("lev"),
        P("tile", None),
        P("tile"),
        P(None, "tile"),
        P(None, "tile"),
    )
    return jax.shard_map(
        body, mesh=mesh, in_specs=placed, out_specs=P(None, "lev", "tile"), check_vma=False
    )
```

time: 85.3 us -> 61.9 us (0.73)
  the two profiles are of different devices: /device:TPU:207 before, /device:TPU:333 now
where the time goes in v6:
time: 61.9 us; the launch traced here: 61.5 us
  starting transfers between devices  32.1 us (52%)
  Pallas kernels  27.1 us (44%)
  waiting for transfers between devices  2.16 us (3%)
    ppermute x4, starting transfers between devices, moved(): lax.ppermute(parcel, 'tile', [(i, i + by) for i in range(peers) if 0 <= i...  11.6 us
    pallas_call x1, Pallas kernels, body(): call(far_kernel, [((4, 4, CELLS), F32, vmem())], [smem(), hbm()] + [vmem(...  10 us
    ppermute x1, starting transfers between devices, crossed(): lax.ppermute(parcel, 'tile', [(i, j) for i, j in pairs if 0 <= j < peers])  9.84 us
    pallas_call x1, Pallas kernels, body(): call(near_kernel, [((16, CELLS + WIN), F32, vmem())], [free()] + [vmem()]...  7.47 us
    all_to_all x1, starting transfers between devices, body(): above = lax.all_to_all(totals, 'lev', 0, 0)  7 us
    pallas_call x1, Pallas kernels, body(): call(solve_kernel, [((8, NLON), F32, vmem()), ((peers, NBLK, BLK), BF16,...  5.4 us
    ppermute x1, starting transfers between devices, swapped(): lax.ppermute(parcel, 'tile', [(i, i ^ 1) for i in range(lax.axis_size('ti...  3.71 us
    pallas_call x1, Pallas kernels, body(): call(pack_kernel, [((NBLK,), jnp.int32, smem()), ((ROUTE, HOME, BLK), BF1...  2.82 us
  transfers between devices with their start and end apart: 7, of which 1 were waited for; matrix products, arithmetic and copies ran while one was open for 0% of the time, Pallas kernels for 17%

profile of v6, /device:TPU:333, one launch (start us, length us, event | category | flops | bytes accessed | tf_op | source)
XLA Modules:
  0.0 61.5 jit_solution(13671551885222453893)
XLA Ops:
  0.0 1.0 %shard_map.74.own = bf16[32,16,128]{2,1,0:T(8,128)(2,1)S(1)} custom-call(bf16[4,4,8192]{2,1,0:T(4,128)(2,1)} %adj_in.3, f32[4,8192]{1,0:T(4,128)} %helm_in.5), custom_call_target="tpu_custom_call" | custom-call | flops 1000000 | bytes 3000000 | tf_op jit(solution)/shard_map/pallas_call | solution.py:486
  1.0 2.2 %collective-permute-start.1 = (bf16[32,16,128]{2,1,0:T(8,128)(2,1)S(1)}, bf16[32,16,128]{2,1,0:T(8,128)(2,1)S(1)}, u32[]{:S(2)}, u32[]{:S(2)}) collective-permute-start(bf16[32,16,128]{2,1,0:T(8,128)(2,1)S(1)} %shard_map.74.own), channel_id=1, source_target_pairs={{16,0},{24,8},{32,16},{40,24},{48,32},{56,40},{64,48},{72,56},{80,... | collective-permute-start | bytes 393224 | tf_op jit(solution)/shard_map/ppermute | solution.py:462
  3.2 3.1 %collective-permute-start = (bf16[32,16,128]{2,1,0:T(8,128)(2,1)S(1)}, bf16[32,16,128]{2,1,0:T(8,128)(2,1)S(1)}, u32[]{:S(2)}, u32[]{:S(2)}) collective-permute-start(bf16[32,16,128]{2,1,0:T(8,128)(2,1)S(1)} %shard_map.74.own), channel_id=1, source_target_pairs={{0,16},{8,24},{16,32},{24,40},{32,48},{40,56},{48,64},{56,72},{64,... | collective-permute-start | bytes 393224 | tf_op jit(solution)/shard_map/ppermute | solution.py:462
  6.3 2.8 %shard_map.73 = (s32[64]{0:T(128)S(1)}, bf16[25,32,128]{2,1,0:T(8,128)(2,1)S(1)}, bf16[32,16,128]{2,1,0:T(8,128)(2,1)S(1)}, bf16[236,16,128]{2,1,0:T(8,128)(2,1)...) custom-call(s32[1]{0:T(128)} %bitcast.1.me, ...), custom_call_target="tpu_custom_call" | custom-call | flops 20000000 | bytes 60000000 | tf_op jit(solution)/shard_map/pallas_call | solution.py:497
  9.1 0.0 collective-permute-done.1.minus
  9.1 0.0 collective-permute-done.plus
  9.1 0.4 shard_map.75
  9.5 3.7 %collective-permute-start.2 = (bf16[236,16,128]{2,1,0:T(8,128)(2,1)S(1)}, bf16[236,16,128]{2,1,0:T(8,128)(2,1)S(1)}, u32[]{:S(2)}, u32[]{:S(2)}) collective-permute-start(bf16[236,16,128]{2,1,0:T(8,128)(2,1)S(1)} %shard_map.75), channel_id=1, source_target_pairs={{0,8},{8,0},{16,24},{24,16},{32,40},{40,32},{48,56},{56,48},{64,72... | collective-permute-start | bytes 2899976 | tf_op jit(solution)/shard_map/ppermute | solution.py:466
  13.2 2.1 %collective-permute-done.2.mate = bf16[236,16,128]{2,1,0:T(8,128)(2,1)S(1)} collective-permute-done((bf16[236,16,128]{2,1,0:T(8,128)(2,1)S(1)}, bf16[236,16,128]{2,1,0:T(8,128)(2,1)S(1)}, u32[]{:S(2)}, u32[]{:S(2)}) %collective-permute-start.2) | collective-permute-done | bytes 966688 | tf_op jit(solution)/shard_map/ppermute | solution.py:466
  15.4 5.4 %shard_map.76 = (f32[8,4096]{1,0:T(8,128)S(1)}, bf16[8,64,128]{2,1,0:T(8,128)(2,1)}, bf16[128,128]{1,0:T(8,128)(2,1)S(1)}, bf16[64,128]{1,0:T(8,128)(2,1)S(1)}, ...) custom-call(s32[1]{0:T(128)} %bitcast.1.me, ...), custom_call_target="tpu_custom_call" | custom-call | flops 2000000 | bytes 6000000 | tf_op jit(solution)/shard_map/pallas_call | solution.py:536
  20.8 4.4 %collective-permute-start.3 = (bf16[90,16,128]{2,1,0:T(8,128)(2,1)}, bf16[90,16,128]{2,1,0:T(8,128)(2,1)S(1)}, u32[]{:S(2)}, u32[]{:S(2)}) collective-permute-start(bf16[90,16,128]{2,1,0:T(8,128)(2,1)} %get-tuple-element.24), channel_id=1, source_target_pairs={{0,16},{8,24},{16,32},{24,40},{32,48},{40,56},{48,64},{56,72},{64,... | collective-permute-start | bytes 1105928 | tf_op jit(solution)/shard_map/ppermute | solution.py:462
  25.2 1.9 %collective-permute-start.4 = (bf16[90,16,128]{2,1,0:T(8,128)(2,1)S(1)}, bf16[90,16,128]{2,1,0:T(8,128)(2,1)S(1)}, u32[]{:S(2)}, u32[]{:S(2)}) collective-permute-start(bf16[90,16,128]{2,1,0:T(8,128)(2,1)S(1)} %get-tuple-element.25), channel_id=1, source_target_pairs={{16,0},{24,8},{32,16},{40,24},{48,32},{56,40},{64,48},{72,56},{80,... | collective-permute-start | bytes 1105928 | tf_op jit(solution)/shard_map/ppermute | solution.py:462
  27.1 7.0 %all-to-all-start = ((bf16[8,64,128]{2,1,0:T(8,128)(2,1)}), bf16[8,64,128]{2,1,0:T(8,128)(2,1)S(1)}, u32[]{:S(2)}, u32[]{:S(2)}) async-start(bf16[8,64,128]{2,1,0:T(8,128)(2,1)} %get-tuple-element.32), calls=%async_computation | async-start | bytes 262144 | tf_op jit(solution)/shard_map/all_to_all | solution.py:569
  34.1 9.8 %collective-permute-start.5 = (bf16[45,16,128]{2,1,0:T(8,128)(2,1)}, bf16[45,16,128]{2,1,0:T(8,128)(2,1)S(1)}, u32[]{:S(2)}, u32[]{:S(2)}) collective-permute-start(bf16[45,16,128]{2,1,0:T(8,128)(2,1)} %get-tuple-element.26), channel_id=1, source_target_pairs={{8,32},{24,48},{32,8},{40,64},{48,24},{56,80},{64,40},{72,96},{80,... | collective-permute-start | bytes 552968 | tf_op jit(solution)/shard_map/ppermute | solution.py:472
  43.9 7.5 %shard_map.77.begun = f32[16,8448]{1,0:T(8,128)S(1)} custom-call(bf16[236,16,128]{2,1,0:T(8,128)(2,1)S(1)} %collective-permute-done.2.mate, bf16[25,32,128]{2,1,0:T(8,128)(2,1)S(1)} %get-tuple-element.27.a_home, bf16[32,16,128]{2,1,0:T(8,128)(2,1)S(1)} %get-tuple-element.28.b_home, bf16[128,128]{1,0:T(8,128)(2,1)S(1)} %get-tuple-element.29.f_home, ...), custom_call_target="tpu_custom_call" | custom-call | flops 8000000 | bytes 24000000 | tf_op jit(solution)/shard_map/pallas_call | solution.py:571
  51.4 0.0 collective-permute-done.5.cross
  51.4 0.0 all-to-all-done.above
  51.4 0.0 collective-permute-done.3.plus
  51.4 0.0 collective-permute-done.4.minus
  51.5 10.0 %shard_map.78 = f32[4,4,8192]{2,1,0:T(4,128)} custom-call(s32[1]{0:T(128)} %bitcast.lev, f32[4]{0:T(128)} %geo_in.1, bf16[90,16,128]{2,1,0:T(8,128)(2,1)S(1)} %collective-permute-done.3.plus, bf16[90,16,128]{2,1,0:T(8,128)(2,1)S(1)} %collective-permute-done.4.minus, bf16[45,16,128]{2,1,0:T(8,128)(2,1)S(1)} %collective-permute-done.5.cross, ...), custom_call_target="tpu_custom_call" | custom-call | flops 4000000 | bytes 12000000 | tf_op jit(solution)/shard_map/pallas_call | solution.py:582
Async XLA Ops:
  1.0 8.1 %collective-permute-start.1 = (bf16[32,16,128]{2,1,0:T(8,128)(2,1)S(1)}, bf16[32,16,128]{2,1,0:T(8,128)(2,1)S(1)}, u32[]{:S(2)}, u32[]{:S(2)}) collective-permute-start(bf16[32,16,128]{2,1,0:T(8,128)(2,1)S(1)} %shard_map.74.own), channel_id=1, source_target_pairs={{16,0},{24,8},{32,16},{40,24},{48,32},{56,40},{64,48},{72,56},{80,... | collective-permute-start | bytes 393224 | tf_op jit(solution)/shard_map/ppermute | solution.py:462
  3.2 6.0 %collective-permute-start = (bf16[32,16,128]{2,1,0:T(8,128)(2,1)S(1)}, bf16[32,16,128]{2,1,0:T(8,128)(2,1)S(1)}, u32[]{:S(2)}, u32[]{:S(2)}) collective-permute-start(bf16[32,16,128]{2,1,0:T(8,128)(2,1)S(1)} %shard_map.74.own), channel_id=1, source_target_pairs={{0,16},{8,24},{16,32},{24,40},{32,48},{40,56},{48,64},{56,72},{64,... | collective-permute-start | bytes 393224 | tf_op jit(solution)/shard_map/ppermute | solution.py:462
  9.5 5.9 %collective-permute-start.2 = (bf16[236,16,128]{2,1,0:T(8,128)(2,1)S(1)}, bf16[236,16,128]{2,1,0:T(8,128)(2,1)S(1)}, u32[]{:S(2)}, u32[]{:S(2)}) collective-permute-start(bf16[236,16,128]{2,1,0:T(8,128)(2,1)S(1)} %shard_map.75), channel_id=1, source_target_pairs={{0,8},{8,0},{16,24},{24,16},{32,40},{40,32},{48,56},{56,48},{64,72... | collective-permute-start | bytes 2899976 | tf_op jit(solution)/shard_map/ppermute | solution.py:466
  20.8 30.6 %collective-permute-start.3 = (bf16[90,16,128]{2,1,0:T(8,128)(2,1)}, bf16[90,16,128]{2,1,0:T(8,128)(2,1)S(1)}, u32[]{:S(2)}, u32[]{:S(2)}) collective-permute-start(bf16[90,16,128]{2,1,0:T(8,128)(2,1)} %get-tuple-element.24), channel_id=1, source_target_pairs={{0,16},{8,24},{16,32},{24,40},{32,48},{40,56},{48,64},{56,72},{64,... | collective-permute-start | bytes 1105928 | tf_op jit(solution)/shard_map/ppermute | solution.py:462
  25.2 26.3 %collective-permute-start.4 = (bf16[90,16,128]{2,1,0:T(8,128)(2,1)S(1)}, bf16[90,16,128]{2,1,0:T(8,128)(2,1)S(1)}, u32[]{:S(2)}, u32[]{:S(2)}) collective-permute-start(bf16[90,16,128]{2,1,0:T(8,128)(2,1)S(1)} %get-tuple-element.25), channel_id=1, source_target_pairs={{16,0},{24,8},{32,16},{40,24},{48,32},{56,40},{64,48},{72,56},{80,... | collective-permute-start | bytes 1105928 | tf_op jit(solution)/shard_map/ppermute | solution.py:462
  27.1 24.3 %all-to-all-start = ((bf16[8,64,128]{2,1,0:T(8,128)(2,1)}), bf16[8,64,128]{2,1,0:T(8,128)(2,1)S(1)}, u32[]{:S(2)}, u32[]{:S(2)}) async-start(bf16[8,64,128]{2,1,0:T(8,128)(2,1)} %get-tuple-element.32), calls=%async_computation | async-start | bytes 262144 | tf_op jit(solution)/shard_map/all_to_all | solution.py:569
  34.1 17.3 %collective-permute-start.5 = (bf16[45,16,128]{2,1,0:T(8,128)(2,1)}, bf16[45,16,128]{2,1,0:T(8,128)(2,1)S(1)}, u32[]{:S(2)}, u32[]{:S(2)}) collective-permute-start(bf16[45,16,128]{2,1,0:T(8,128)(2,1)} %get-tuple-element.26), channel_id=1, source_target_pairs={{8,32},{24,48},{32,8},{40,64},{48,24},{56,80},{64,40},{72,96},{80,... | collective-permute-start | bytes 552968 | tf_op jit(solution)/shard_map/ppermute | solution.py:472

commit v7 on v6

--- a/solution.py
+++ b/solution.py
@@ -35,7 +35,7 @@
 FAR = 5 * OFFCAP
 CROSS = LOAD + 4
 PAIR = 2 * LOAD + 8
-PACK = 4
+PACK = 8
 REMAINDER = 1e-6
 
 
@@ -308,64 +308,64 @@
             slot = i * 8 + j
             mark = meta_s[0, slot]
             window = (mark & 63) - 1
-            entry_slot[n + 1] = slot
-            entry_win[n + 1] = window
+            entry_slot[n] = slot
+            entry_win[n] = window
             n = n + (mark > 0).astype(jnp.int32)
-            entry_slot[n + 1] = slot + count
-            entry_win[n + 1] = window
+            entry_slot[n] = slot + count
+            entry_win[n] = window
             n = n + (mark >= 64).astype(jnp.int32)
         return n
 
     n = lax.fori_loop(0, count // 8, eight, jnp.int32(0))
-    for at in [0] + [n + 1 + j for j in range(PACK)]:
-        entry_slot[at] = 0
-        entry_win[at] = NWIN
+    for j in range(PACK):
+        entry_slot[n + j] = 0
+        entry_win[n + j] = NWIN
     return n
 
 
-def spread(parts, count, cells, merged, meta, meta_s, entry_slot, entry_win, values, firsts, mats, total, meta_sem, ready):
+def spread(parts, count, cells, merged, meta, meta_s, entry_slot, entry_win, values, firsts, total, meta_sem, ready):
     merge_all(parts, cells, merged, count, meta)
     finish(launch([(meta, meta_s, meta_sem)]))
     n = enlist(meta_s, count, entry_slot, entry_win)
     ready()
     iota = lax.broadcasted_iota(jnp.int32, (16, BLK), 0).astype(F32)
     first_rows = lax.broadcasted_iota(jnp.int32, (8, BLK), 0) < 4
-    mats[PACK - 1] = jnp.zeros((WIN, BLK), BF16)
 
     def multiply(at, mat):
         slot = lax.rem(entry_slot[at], count)
         tile = values[slot].astype(F32)
         head = jnp.where(first_rows, firsts[pl.ds(slot * 4, 8), :], tile[:8])
         left = jnp.concatenate([head, tile[8:]], axis=0).astype(BF16)
-        return lax.dot_general(left, mat[...], (((1,), (1,)), ((), ())), preferred_element_type=F32)
-
-    def build(at, mat):
+        return lax.dot_general(left, mat, (((1,), (1,)), ((), ())), preferred_element_type=F32)
+
+    def build(at):
         entry = entry_slot[at]
         slot = lax.rem(entry, count)
         c = [jnp.broadcast_to(cells[k, pl.ds(slot, 1), :], (16, BLK)).astype(BF16) for k in range(STEN)]
         w = [jnp.broadcast_to(merged[k, pl.ds(entry, 1), :], (16, BLK)).astype(BF16) for k in range(STEN)]
+        tiles = []
         for i in range(WIN // 16):
             here = (iota + 16.0 * i).astype(BF16)
             m = jnp.zeros((16, BLK), BF16)
             for k in range(STEN):
                 m = jnp.where(c[k] == here, w[k], m)
-            mat[16 * i : 16 * i + 16, :] = m
+            tiles.append(m)
+        return jnp.concatenate(tiles, axis=0)
 
     def add(at, product):
         start = pl.multiple_of(entry_win[at] * WIN, WIN)
         total[:, pl.ds(start, WIN)] += product
 
     def step(group, carry):
+        products = []
         for j in range(PACK):
             at = group * PACK + j
-            product = multiply(at, mats.at[(j - 1) % PACK])
-            build(at + 1, mats.at[j])
+            products.append((at, multiply(at, build(at))))
+        for at, product in products:
             add(at, product)
         return carry
 
-    groups = (n + PACK - 1) // PACK
-    lax.fori_loop(0, groups, step, 0)
-    add(groups * PACK, multiply(groups * PACK, mats.at[PACK - 1]))
+    lax.fori_loop(0, (n + PACK - 1) // PACK, step, 0)
 
 
 def spread_scratch(count):
@@ -374,11 +374,10 @@
         pltpu.VMEM((STEN, 2 * count, BLK), F32),
         pltpu.VMEM((1, BLK), jnp.int32),
         pltpu.SMEM((1, BLK), jnp.int32),
-        pltpu.SMEM((2 * count + 8,), jnp.int32),
-        pltpu.SMEM((2 * count + 8,), jnp.int32),
+        pltpu.SMEM((2 * count + PACK,), jnp.int32),
+        pltpu.SMEM((2 * count + PACK,), jnp.int32),
         pltpu.VMEM((count, 16, BLK), BF16),
         pltpu.VMEM((count * 4 + 8, BLK), F32),
-        pltpu.VMEM((PACK, WIN, BLK), BF16),
     ]
 
 
@@ -392,7 +391,7 @@
 
 def near_kernel(
     mate, a_home, b_home, f_home, f_mate, total,
-    a_in, cells, merged, meta, meta_s, entry_slot, entry_win, values, firsts, mats, sems, meta_sem,
+    a_in, cells, merged, meta, meta_s, entry_slot, entry_win, values, firsts, sems, meta_sem,
 ):
     routes = launch([(mate.at[pl.ds(MATE, ROUTE)], a_in, sems.at[0])])
     copies = launch([(mate.at[pl.ds(MATE + ROUTE, OFFCAP)], values.at[pl.ds(HOME, OFFCAP)], sems.at[1])])
@@ -407,14 +406,14 @@
 
     parts = [own_rows(at) for at in range(0, HOME, 16)] + [arrival(routes[0], a_in)]
     spread(
-        parts, NEAR, cells, merged, meta, meta_s, entry_slot, entry_win, values, firsts, mats, total, meta_sem,
+        parts, NEAR, cells, merged, meta, meta_s, entry_slot, entry_win, values, firsts, total, meta_sem,
         lambda: finish(copies),
     )
 
 
 def far_kernel(
     lev, geo_in, plus, minus, cross, begun, local, above,
-    out, geo, total, a_in, cells, merged, meta, meta_s, entry_slot, entry_win, values, firsts, mats, sems, meta_sem,
+    out, geo, total, a_in, cells, merged, meta, meta_s, entry_slot, entry_win, values, firsts, sems, meta_sem,
 ):
     parts = (
         (plus, 0, 2 * LOAD),
@@ -438,7 +437,7 @@
     firsts[FAR * 4 :, :] = jnp.zeros((8, BLK), F32)
     spread(
         [arrival(copy, a_in.at[i]) for i, copy in enumerate(routes)],
-        FAR, cells, merged, meta, meta_s, entry_slot, entry_win, values, firsts, mats, total, meta_sem,
+        FAR, cells, merged, meta, meta_s, entry_slot, entry_win, values, firsts, total, meta_sem,
         lambda: finish(copies),
     )
 

time: 61.9 us -> 58.8 us (0.950)
  the two profiles are of different devices: /device:TPU:333 before, /device:TPU:264 now
where the time goes in v7:
time: 58.8 us; the launch traced here: 57.9 us
  starting transfers between devices  26.4 us (45%)
  Pallas kernels  18.7 us (32%)
  waiting for transfers between devices  12.6 us (21%)
    ppermute x4, starting transfers between devices, moved(): lax.ppermute(parcel, 'tile', [(i, i + by) for i in range(peers) if 0 <= i...  15 us
    all_to_all x1, starting transfers between devices, body(): above = lax.all_to_all(totals, 'lev', 0, 0)  7.56 us
    pallas_call x1, Pallas kernels, body(): call(solve_kernel, [((8, NLON), F32, vmem()), ((peers, NBLK, BLK), BF16,...  5.39 us
    pallas_call x1, Pallas kernels, body(): call(far_kernel, [((4, 4, CELLS), F32, vmem())], [smem(), hbm()] + [vmem(...  5.32 us
    ppermute x4, waiting for transfers between devices, moved(): lax.ppermute(parcel, 'tile', [(i, i + by) for i in range(peers) if 0 <= i...  5.26 us
    ppermute x1, waiting for transfers between devices, crossed(): lax.ppermute(parcel, 'tile', [(i, j) for i, j in pairs if 0 <= j < peers])  4.85 us
    pallas_call x1, Pallas kernels, body(): call(near_kernel, [((16, CELLS + WIN), F32, vmem())], [free()] + [vmem()]...  3.9 us
    pallas_call x1, Pallas kernels, body(): call(pack_kernel, [((NBLK,), jnp.int32, smem()), ((ROUTE, HOME, BLK), BF1...  2.82 us
  transfers between devices with their start and end apart: 7, of which 3 were waited for; matrix products, arithmetic and copies ran while one was open for 0% of the time, Pallas kernels for 12%

profile of v7, /device:TPU:264, one launch (start us, length us, event | category | flops | bytes accessed | tf_op | source)
XLA Modules:
  0.0 57.9 jit_solution(7591926399734708972)
XLA Ops:
  0.0 1.0 %shard_map.74.own = bf16[32,16,128]{2,1,0:T(8,128)(2,1)S(1)} custom-call(bf16[4,4,8192]{2,1,0:T(4,128)(2,1)} %adj_in.3, f32[4,8192]{1,0:T(4,128)} %helm_in.5), custom_call_target="tpu_custom_call" | custom-call | flops 1000000 | bytes 3000000 | tf_op jit(solution)/shard_map/pallas_call | solution.py:485
  1.0 3.8 %collective-permute-start.1 = (bf16[32,16,128]{2,1,0:T(8,128)(2,1)S(1)}, bf16[32,16,128]{2,1,0:T(8,128)(2,1)S(1)}, u32[]{:S(2)}, u32[]{:S(2)}) collective-permute-start(bf16[32,16,128]{2,1,0:T(8,128)(2,1)S(1)} %shard_map.74.own), channel_id=1, source_target_pairs={{16,0},{24,8},{32,16},{40,24},{48,32},{56,40},{64,48},{72,56},{80,... | collective-permute-start | bytes 393224 | tf_op jit(solution)/shard_map/ppermute | solution.py:461
  4.8 2.1 %collective-permute-start = (bf16[32,16,128]{2,1,0:T(8,128)(2,1)S(1)}, bf16[32,16,128]{2,1,0:T(8,128)(2,1)S(1)}, u32[]{:S(2)}, u32[]{:S(2)}) collective-permute-start(bf16[32,16,128]{2,1,0:T(8,128)(2,1)S(1)} %shard_map.74.own), channel_id=1, source_target_pairs={{0,16},{8,24},{16,32},{24,40},{32,48},{40,56},{48,64},{56,72},{64,... | collective-permute-start | bytes 393224 | tf_op jit(solution)/shard_map/ppermute | solution.py:461
  6.9 2.8 %shard_map.73 = (s32[64]{0:T(128)S(1)}, bf16[25,32,128]{2,1,0:T(8,128)(2,1)S(1)}, bf16[32,16,128]{2,1,0:T(8,128)(2,1)S(1)}, bf16[236,16,128]{2,1,0:T(8,128)(2,1)...) custom-call(s32[1]{0:T(128)} %bitcast.1.me, ...), custom_call_target="tpu_custom_call" | custom-call | flops 20000000 | bytes 60000000 | tf_op jit(solution)/shard_map/pallas_call | solution.py:496
  9.7 0.0 collective-permute-done.1.minus
  9.7 5.2 %collective-permute-done.plus = bf16[32,16,128]{2,1,0:T(8,128)(2,1)S(1)} collective-permute-done((bf16[32,16,128]{2,1,0:T(8,128)(2,1)S(1)}, bf16[32,16,128]{2,1,0:T(8,128)(2,1)S(1)}, u32[]{:S(2)}, u32[]{:S(2)}) %collective-permute-start) | collective-permute-done | bytes 131104 | tf_op jit(solution)/shard_map/ppermute | solution.py:461
  14.9 0.3 shard_map.75
  15.3 1.9 %collective-permute-start.2 = (bf16[236,16,128]{2,1,0:T(8,128)(2,1)S(1)}, bf16[236,16,128]{2,1,0:T(8,128)(2,1)S(1)}, u32[]{:S(2)}, u32[]{:S(2)}) collective-permute-start(bf16[236,16,128]{2,1,0:T(8,128)(2,1)S(1)} %shard_map.75), channel_id=1, source_target_pairs={{0,8},{8,0},{16,24},{24,16},{32,40},{40,32},{48,56},{56,48},{64,72... | collective-permute-start | bytes 2899976 | tf_op jit(solution)/shard_map/ppermute | solution.py:465
  17.2 2.5 %collective-permute-done.2.mate = bf16[236,16,128]{2,1,0:T(8,128)(2,1)S(1)} collective-permute-done((bf16[236,16,128]{2,1,0:T(8,128)(2,1)S(1)}, bf16[236,16,128]{2,1,0:T(8,128)(2,1)S(1)}, u32[]{:S(2)}, u32[]{:S(2)}) %collective-permute-start.2) | collective-permute-done | bytes 966688 | tf_op jit(solution)/shard_map/ppermute | solution.py:465
  19.7 5.4 %shard_map.76 = (f32[8,4096]{1,0:T(8,128)S(1)}, bf16[8,64,128]{2,1,0:T(8,128)(2,1)}, bf16[128,128]{1,0:T(8,128)(2,1)S(1)}, bf16[64,128]{1,0:T(8,128)(2,1)S(1)}, ...) custom-call(s32[1]{0:T(128)} %bitcast.1.me, ...), custom_call_target="tpu_custom_call" | custom-call | flops 2000000 | bytes 6000000 | tf_op jit(solution)/shard_map/pallas_call | solution.py:535
  25.1 1.9 %collective-permute-start.3 = (bf16[90,16,128]{2,1,0:T(8,128)(2,1)}, bf16[90,16,128]{2,1,0:T(8,128)(2,1)S(1)}, u32[]{:S(2)}, u32[]{:S(2)}) collective-permute-start(bf16[90,16,128]{2,1,0:T(8,128)(2,1)} %get-tuple-element.24), channel_id=1, source_target_pairs={{0,16},{8,24},{16,32},{24,40},{32,48},{40,56},{48,64},{56,72},{64,... | collective-permute-start | bytes 1105928 | tf_op jit(solution)/shard_map/ppermute | solution.py:461
  27.1 7.2 %collective-permute-start.4 = (bf16[90,16,128]{2,1,0:T(8,128)(2,1)S(1)}, bf16[90,16,128]{2,1,0:T(8,128)(2,1)S(1)}, u32[]{:S(2)}, u32[]{:S(2)}) collective-permute-start(bf16[90,16,128]{2,1,0:T(8,128)(2,1)S(1)} %get-tuple-element.25), channel_id=1, source_target_pairs={{16,0},{24,8},{32,16},{40,24},{48,32},{56,40},{64,48},{72,56},{80,... | collective-permute-start | bytes 1105928 | tf_op jit(solution)/shard_map/ppermute | solution.py:461
  34.3 7.6 %all-to-all-start = ((bf16[8,64,128]{2,1,0:T(8,128)(2,1)}), bf16[8,64,128]{2,1,0:T(8,128)(2,1)S(1)}, u32[]{:S(2)}, u32[]{:S(2)}) async-start(bf16[8,64,128]{2,1,0:T(8,128)(2,1)} %get-tuple-element.32), calls=%async_computation | async-start | bytes 262144 | tf_op jit(solution)/shard_map/all_to_all | solution.py:568
  41.9 1.9 %collective-permute-start.5 = (bf16[45,16,128]{2,1,0:T(8,128)(2,1)}, bf16[45,16,128]{2,1,0:T(8,128)(2,1)S(1)}, u32[]{:S(2)}, u32[]{:S(2)}) collective-permute-start(bf16[45,16,128]{2,1,0:T(8,128)(2,1)} %get-tuple-element.26), channel_id=1, source_target_pairs={{8,32},{24,48},{32,8},{40,64},{48,24},{56,80},{64,40},{72,96},{80,... | collective-permute-start | bytes 552968 | tf_op jit(solution)/shard_map/ppermute | solution.py:471
  43.8 3.9 %shard_map.77.begun = f32[16,8448]{1,0:T(8,128)S(1)} custom-call(bf16[236,16,128]{2,1,0:T(8,128)(2,1)S(1)} %collective-permute-done.2.mate, bf16[25,32,128]{2,1,0:T(8,128)(2,1)S(1)} %get-tuple-element.27.a_home, bf16[32,16,128]{2,1,0:T(8,128)(2,1)S(1)} %get-tuple-element.28.b_home, bf16[128,128]{1,0:T(8,128)(2,1)S(1)} %get-tuple-element.29.f_home, ...), custom_call_target="tpu_custom_call" | custom-call | flops 8000000 | bytes 24000000 | tf_op jit(solution)/shard_map/pallas_call | solution.py:570
  47.7 4.8 %collective-permute-done.5.cross = bf16[45,16,128]{2,1,0:T(8,128)(2,1)S(1)} collective-permute-done((bf16[45,16,128]{2,1,0:T(8,128)(2,1)}, bf16[45,16,128]{2,1,0:T(8,128)(2,1)S(1)}, u32[]{:S(2)}, u32[]{:S(2)}) %collective-permute-start.5) | collective-permute-done | bytes 184352 | tf_op jit(solution)/shard_map/ppermute | solution.py:471
  52.5 0.0 all-to-all-done.above
  52.5 0.0 collective-permute-done.3.plus
  52.5 0.0 collective-permute-done.4.minus
  52.5 5.3 %shard_map.78 = f32[4,4,8192]{2,1,0:T(4,128)} custom-call(s32[1]{0:T(128)} %bitcast.lev, f32[4]{0:T(128)} %geo_in.1, bf16[90,16,128]{2,1,0:T(8,128)(2,1)S(1)} %collective-permute-done.3.plus, bf16[90,16,128]{2,1,0:T(8,128)(2,1)S(1)} %collective-permute-done.4.minus, bf16[45,16,128]{2,1,0:T(8,128)(2,1)S(1)} %collective-permute-done.5.cross, ...), custom_call_target="tpu_custom_call" | custom-call | flops 4000000 | bytes 12000000 | tf_op jit(solution)/shard_map/pallas_call | solution.py:581
Async XLA Ops:
  1.0 8.7 %collective-permute-start.1 = (bf16[32,16,128]{2,1,0:T(8,128)(2,1)S(1)}, bf16[32,16,128]{2,1,0:T(8,128)(2,1)S(1)}, u32[]{:S(2)}, u32[]{:S(2)}) collective-permute-start(bf16[32,16,128]{2,1,0:T(8,128)(2,1)S(1)} %shard_map.74.own), channel_id=1, source_target_pairs={{16,0},{24,8},{32,16},{40,24},{48,32},{56,40},{64,48},{72,56},{80,... | collective-permute-start | bytes 393224 | tf_op jit(solution)/shard_map/ppermute | solution.py:461
  4.8 10.2 %collective-permute-start = (bf16[32,16,128]{2,1,0:T(8,128)(2,1)S(1)}, bf16[32,16,128]{2,1,0:T(8,128)(2,1)S(1)}, u32[]{:S(2)}, u32[]{:S(2)}) collective-permute-start(bf16[32,16,128]{2,1,0:T(8,128)(2,1)S(1)} %shard_map.74.own), channel_id=1, source_target_pairs={{0,16},{8,24},{16,32},{24,40},{32,48},{40,56},{48,64},{56,72},{64,... | collective-permute-start | bytes 393224 | tf_op jit(solution)/shard_map/ppermute | solution.py:461
  15.3 4.4 %collective-permute-start.2 = (bf16[236,16,128]{2,1,0:T(8,128)(2,1)S(1)}, bf16[236,16,128]{2,1,0:T(8,128)(2,1)S(1)}, u32[]{:S(2)}, u32[]{:S(2)}) collective-permute-start(bf16[236,16,128]{2,1,0:T(8,128)(2,1)S(1)} %shard_map.75), channel_id=1, source_target_pairs={{0,8},{8,0},{16,24},{24,16},{32,40},{40,32},{48,56},{56,48},{64,72... | collective-permute-start | bytes 2899976 | tf_op jit(solution)/shard_map/ppermute | solution.py:465
  25.1 27.4 %collective-permute-start.3 = (bf16[90,16,128]{2,1,0:T(8,128)(2,1)}, bf16[90,16,128]{2,1,0:T(8,128)(2,1)S(1)}, u32[]{:S(2)}, u32[]{:S(2)}) collective-permute-start(bf16[90,16,128]{2,1,0:T(8,128)(2,1)} %get-tuple-element.24), channel_id=1, source_target_pairs={{0,16},{8,24},{16,32},{24,40},{32,48},{40,56},{48,64},{56,72},{64,... | collective-permute-start | bytes 1105928 | tf_op jit(solution)/shard_map/ppermute | solution.py:461
  27.1 25.5 %collective-permute-start.4 = (bf16[90,16,128]{2,1,0:T(8,128)(2,1)S(1)}, bf16[90,16,128]{2,1,0:T(8,128)(2,1)S(1)}, u32[]{:S(2)}, u32[]{:S(2)}) collective-permute-start(bf16[90,16,128]{2,1,0:T(8,128)(2,1)S(1)} %get-tuple-element.25), channel_id=1, source_target_pairs={{16,0},{24,8},{32,16},{40,24},{48,32},{56,40},{64,48},{72,56},{80,... | collective-permute-start | bytes 1105928 | tf_op jit(solution)/shard_map/ppermute | solution.py:461
  34.3 18.2 %all-to-all-start = ((bf16[8,64,128]{2,1,0:T(8,128)(2,1)}), bf16[8,64,128]{2,1,0:T(8,128)(2,1)S(1)}, u32[]{:S(2)}, u32[]{:S(2)}) async-start(bf16[8,64,128]{2,1,0:T(8,128)(2,1)} %get-tuple-element.32), calls=%async_computation | async-start | bytes 262144 | tf_op jit(solution)/shard_map/all_to_all | solution.py:568
  41.9 10.7 %collective-permute-start.5 = (bf16[45,16,128]{2,1,0:T(8,128)(2,1)}, bf16[45,16,128]{2,1,0:T(8,128)(2,1)S(1)}, u32[]{:S(2)}, u32[]{:S(2)}) collective-permute-start(bf16[45,16,128]{2,1,0:T(8,128)(2,1)} %get-tuple-element.26), channel_id=1, source_target_pairs={{8,32},{24,48},{32,8},{40,64},{48,24},{56,80},{64,40},{72,96},{80,... | collective-permute-start | bytes 552968 | tf_op jit(solution)/shard_map/ppermute | solution.py:471

commit v8 on v7

--- a/solution.py
+++ b/solution.py
@@ -32,7 +32,7 @@
 RELAY_MINUS = RELAY_PLUS + HALO
 OWN = RELAY_MINUS + HALO
 NEAR = HOME + OFFCAP
-FAR = 5 * OFFCAP
+FAR = 4 * OFFCAP
 CROSS = LOAD + 4
 PAIR = 2 * LOAD + 8
 PACK = 8
@@ -411,35 +411,41 @@
     )
 
 
-def far_kernel(
-    lev, geo_in, plus, minus, cross, begun, local, above,
-    out, geo, total, a_in, cells, merged, meta, meta_s, entry_slot, entry_win, values, firsts, sems, meta_sem,
-):
-    parts = (
-        (plus, 0, 2 * LOAD),
-        (plus, LOAD, 2 * LOAD + 4),
-        (minus, 0, 2 * LOAD),
-        (minus, LOAD, 2 * LOAD + 4),
-        (cross, 0, LOAD),
-    )
+def spread_parcels(parts, begun, total, a_in, scratch, sems, meta_sem):
+    cells, merged, meta, meta_s, entry_slot, entry_win, values, firsts = scratch
     count = len(parts)
     routes = launch([(p.at[pl.ds(at, ROUTE)], a_in.at[i], sems.at[i]) for i, (p, at, _) in enumerate(parts)])
     pairs = [
         (p.at[pl.ds(at + ROUTE, OFFCAP)], values.at[pl.ds(OFFCAP * i, OFFCAP)]) for i, (p, at, _) in enumerate(parts)
     ]
-    pairs += [(geo_in, geo)]
     copies = launch([(a, b, sems.at[count + i]) for i, (a, b) in enumerate(pairs)])
     total[...] = begun[...]
     for i, (p, _, at) in enumerate(parts):
         for j in range(4):
             row = OFFCAP * 4 * i + 16 * j
             firsts[row : row + 16, :] = p[at + j].astype(F32)
-    firsts[FAR * 4 :, :] = jnp.zeros((8, BLK), F32)
+    firsts[OFFCAP * 4 * count :, :] = jnp.zeros((8, BLK), F32)
     spread(
         [arrival(copy, a_in.at[i]) for i, copy in enumerate(routes)],
-        FAR, cells, merged, meta, meta_s, entry_slot, entry_win, values, firsts, total, meta_sem,
+        OFFCAP * count, cells, merged, meta, meta_s, entry_slot, entry_win, values, firsts, total, meta_sem,
         lambda: finish(copies),
     )
+
+
+def far_kernel(plus, minus, begun, total, a_in, *rest):
+    parts = (
+        (plus, 0, 2 * LOAD),
+        (plus, LOAD, 2 * LOAD + 4),
+        (minus, 0, 2 * LOAD),
+        (minus, LOAD, 2 * LOAD + 4),
+    )
+    spread_parcels(parts, begun, total, a_in, rest[:-2], *rest[-2:])
+
+
+def last_kernel(lev, geo_in, cross, begun, local, above, out, geo, geo_sem, total, a_in, *rest):
+    geos = launch([(geo_in, geo, geo_sem)])
+    spread_parcels([(cross, 0, LOAD)], begun, total, a_in, rest[:-2], *rest[-2:])
+    finish(geos)
 
     sums = jnp.zeros((NBLK, BLK), F32)
     for peer in range(above.shape[0]):
@@ -578,20 +584,32 @@
         16,
     )(mate, a_home, b_home, f_home, f_mate)[0]
 
+    begun = call(
+        far_kernel,
+        [((16, CELLS + WIN), F32, vmem())],
+        [vmem()] * 3,
+        [pltpu.VMEM((4, ROUTE, 16, BLK), BF16)]
+        + spread_scratch(FAR)
+        + [pltpu.SemaphoreType.DMA((8,)), pltpu.SemaphoreType.DMA],
+        8,
+        16,
+    )(f_plus, f_minus, begun)[0]
+
     return call(
-        far_kernel,
+        last_kernel,
         [((4, 4, CELLS), F32, vmem())],
-        [smem(), hbm()] + [vmem()] * 6,
+        [smem(), hbm()] + [vmem()] * 4,
         [
             pltpu.SMEM((4,), F32),
+            pltpu.SemaphoreType.DMA,
             pltpu.VMEM((16, CELLS + WIN), F32),
-            pltpu.VMEM((5, ROUTE, 16, BLK), BF16),
+            pltpu.VMEM((1, ROUTE, 16, BLK), BF16),
         ]
-        + spread_scratch(FAR)
-        + [pltpu.SemaphoreType.DMA((11,)), pltpu.SemaphoreType.DMA],
+        + spread_scratch(OFFCAP)
+        + [pltpu.SemaphoreType.DMA((2,)), pltpu.SemaphoreType.DMA],
         4,
         16,
-    )(lev, kept(geo_coef), f_plus, f_minus, cross, begun, local, above)[0]
+    )(lev, kept(geo_coef), cross, begun, local, above)[0]
 
 
 def solution(mesh):

time: 58.8 us -> 60 us (1.020)
  the two profiles are of different devices: /device:TPU:264 before, /device:TPU:205 now
where the time goes in v8:
time: 60 us; the launch traced here: 59 us
  starting transfers between devices  35.8 us (60%)
  Pallas kernels  21 us (35%)
  waiting for transfers between devices  2.16 us (4%)
    ppermute x4, starting transfers between devices, moved(): lax.ppermute(parcel, 'tile', [(i, i + by) for i in range(peers) if 0 <= i...  12.8 us
    ppermute x1, starting transfers between devices, crossed(): lax.ppermute(parcel, 'tile', [(i, j) for i, j in pairs if 0 <= j < peers])  12.3 us
    all_to_all x1, starting transfers between devices, body(): above = lax.all_to_all(totals, 'lev', 0, 0)  7 us
    pallas_call x1, Pallas kernels, body(): call(solve_kernel, [((8, NLON), F32, vmem()), ((peers, NBLK, BLK), BF16,...  5.21 us
    pallas_call x1, Pallas kernels, body(): call(near_kernel, [((16, CELLS + WIN), F32, vmem())], [free()] + [vmem()]...  5.04 us
    pallas_call x1, Pallas kernels, body(): call(far_kernel, [((16, CELLS + WIN), F32, vmem())], [vmem()] * 3, [pltpu...  3.94 us
    ppermute x1, starting transfers between devices, swapped(): lax.ppermute(parcel, 'tile', [(i, i ^ 1) for i in range(lax.axis_size('ti...  3.72 us
    pallas_call x1, Pallas kernels, body(): call(pack_kernel, [((NBLK,), jnp.int32, smem()), ((ROUTE, HOME, BLK), BF1...  2.81 us
  transfers between devices with their start and end apart: 7, of which 1 were waited for; matrix products, arithmetic and copies ran while one was open for 0% of the time, Pallas kernels for 20%

profile of v8, /device:TPU:205, one launch (start us, length us, event | category | flops | bytes accessed | tf_op | source)
XLA Modules:
  0.0 59.0 jit_solution(2997796027172031899)
XLA Ops:
  0.0 1.0 %shard_map.74.own = bf16[32,16,128]{2,1,0:T(8,128)(2,1)S(1)} custom-call(bf16[4,4,8192]{2,1,0:T(4,128)(2,1)} %adj_in.3, f32[4,8192]{1,0:T(4,128)} %helm_in.5), custom_call_target="tpu_custom_call" | custom-call | flops 1000000 | bytes 3000000 | tf_op jit(solution)/shard_map/pallas_call | solution.py:491
  1.0 2.2 %collective-permute-start.1 = (bf16[32,16,128]{2,1,0:T(8,128)(2,1)S(1)}, bf16[32,16,128]{2,1,0:T(8,128)(2,1)S(1)}, u32[]{:S(2)}, u32[]{:S(2)}) collective-permute-start(bf16[32,16,128]{2,1,0:T(8,128)(2,1)S(1)} %shard_map.74.own), channel_id=1, source_target_pairs={{16,0},{24,8},{32,16},{40,24},{48,32},{56,40},{64,48},{72,56},{80,... | collective-permute-start | bytes 393224 | tf_op jit(solution)/shard_map/ppermute | solution.py:467
  3.2 3.1 %collective-permute-start = (bf16[32,16,128]{2,1,0:T(8,128)(2,1)S(1)}, bf16[32,16,128]{2,1,0:T(8,128)(2,1)S(1)}, u32[]{:S(2)}, u32[]{:S(2)}) collective-permute-start(bf16[32,16,128]{2,1,0:T(8,128)(2,1)S(1)} %shard_map.74.own), channel_id=1, source_target_pairs={{0,16},{8,24},{16,32},{24,40},{32,48},{40,56},{48,64},{56,72},{64,... | collective-permute-start | bytes 393224 | tf_op jit(solution)/shard_map/ppermute | solution.py:467
  6.3 2.8 %shard_map.73 = (s32[64]{0:T(128)S(1)}, bf16[25,32,128]{2,1,0:T(8,128)(2,1)S(1)}, bf16[32,16,128]{2,1,0:T(8,128)(2,1)S(1)}, bf16[236,16,128]{2,1,0:T(8,128)(2,1)...) custom-call(s32[1]{0:T(128)} %bitcast.1.me, ...), custom_call_target="tpu_custom_call" | custom-call | flops 20000000 | bytes 60000000 | tf_op jit(solution)/shard_map/pallas_call | solution.py:502
  9.1 0.0 collective-permute-done.1.minus
  9.1 0.0 collective-permute-done.plus
  9.1 0.4 shard_map.75
  9.5 3.7 %collective-permute-start.2 = (bf16[236,16,128]{2,1,0:T(8,128)(2,1)S(1)}, bf16[236,16,128]{2,1,0:T(8,128)(2,1)S(1)}, u32[]{:S(2)}, u32[]{:S(2)}) collective-permute-start(bf16[236,16,128]{2,1,0:T(8,128)(2,1)S(1)} %shard_map.75), channel_id=1, source_target_pairs={{0,8},{8,0},{16,24},{24,16},{32,40},{40,32},{48,56},{56,48},{64,72... | collective-permute-start | bytes 2899976 | tf_op jit(solution)/shard_map/ppermute | solution.py:471
  13.2 2.1 %collective-permute-done.2.mate = bf16[236,16,128]{2,1,0:T(8,128)(2,1)S(1)} collective-permute-done((bf16[236,16,128]{2,1,0:T(8,128)(2,1)S(1)}, bf16[236,16,128]{2,1,0:T(8,128)(2,1)S(1)}, u32[]{:S(2)}, u32[]{:S(2)}) %collective-permute-start.2) | collective-permute-done | bytes 966688 | tf_op jit(solution)/shard_map/ppermute | solution.py:471
  15.4 5.2 %shard_map.76 = (f32[8,4096]{1,0:T(8,128)S(1)}, bf16[8,64,128]{2,1,0:T(8,128)(2,1)}, bf16[128,128]{1,0:T(8,128)(2,1)S(1)}, bf16[64,128]{1,0:T(8,128)(2,1)S(1)}, ...) custom-call(s32[1]{0:T(128)} %bitcast.1.me, ...), custom_call_target="tpu_custom_call" | custom-call | flops 2000000 | bytes 6000000 | tf_op jit(solution)/shard_map/pallas_call | solution.py:541
  20.6 5.6 %collective-permute-start.4 = (bf16[90,16,128]{2,1,0:T(8,128)(2,1)S(1)}, bf16[90,16,128]{2,1,0:T(8,128)(2,1)S(1)}, u32[]{:S(2)}, u32[]{:S(2)}) collective-permute-start(bf16[90,16,128]{2,1,0:T(8,128)(2,1)S(1)} %get-tuple-element.25), channel_id=1, source_target_pairs={{0,16},{8,24},{16,32},{24,40},{32,48},{40,56},{48,64},{56,72},{64,... | collective-permute-start | bytes 1105928 | tf_op jit(solution)/shard_map/ppermute | solution.py:467
  26.2 1.9 %collective-permute-start.5 = (bf16[90,16,128]{2,1,0:T(8,128)(2,1)S(1)}, bf16[90,16,128]{2,1,0:T(8,128)(2,1)S(1)}, u32[]{:S(2)}, u32[]{:S(2)}) collective-permute-start(bf16[90,16,128]{2,1,0:T(8,128)(2,1)S(1)} %get-tuple-element.26), channel_id=1, source_target_pairs={{16,0},{24,8},{32,16},{40,24},{48,32},{56,40},{64,48},{72,56},{80,... | collective-permute-start | bytes 1105928 | tf_op jit(solution)/shard_map/ppermute | solution.py:467
  28.1 7.0 %all-to-all-start = ((bf16[8,64,128]{2,1,0:T(8,128)(2,1)}), bf16[8,64,128]{2,1,0:T(8,128)(2,1)S(1)}, u32[]{:S(2)}, u32[]{:S(2)}) async-start(bf16[8,64,128]{2,1,0:T(8,128)(2,1)} %get-tuple-element.32), calls=%async_computation | async-start | bytes 262144 | tf_op jit(solution)/shard_map/all_to_all | solution.py:574
  35.1 12.3 %collective-permute-start.3 = (bf16[45,16,128]{2,1,0:T(8,128)(2,1)S(1)}, bf16[45,16,128]{2,1,0:T(8,128)(2,1)S(1)}, u32[]{:S(2)}, u32[]{:S(2)}) collective-permute-start(bf16[45,16,128]{2,1,0:T(8,128)(2,1)S(1)} %get-tuple-element.24), channel_id=1, source_target_pairs={{8,32},{24,48},{32,8},{40,64},{48,24},{56,80},{64,40},{72,96},{80,... | collective-permute-start | bytes 552968 | tf_op jit(solution)/shard_map/ppermute | solution.py:477
  47.4 5.0 %shard_map.77.begun = f32[16,8448]{1,0:T(8,128)S(1)} custom-call(bf16[236,16,128]{2,1,0:T(8,128)(2,1)S(1)} %collective-permute-done.2.mate, bf16[25,32,128]{2,1,0:T(8,128)(2,1)S(1)} %get-tuple-element.27.a_home, bf16[32,16,128]{2,1,0:T(8,128)(2,1)S(1)} %get-tuple-element.28.b_home, bf16[128,128]{1,0:T(8,128)(2,1)S(1)} %get-tuple-element.29.f_home, ...), custom_call_target="tpu_custom_call" | custom-call | flops 8000000 | bytes 24000000 | tf_op jit(solution)/shard_map/pallas_call | solution.py:576
  52.4 0.0 collective-permute-done.4.plus
  52.4 0.0 collective-permute-done.5.minus
  52.5 3.9 %shard_map.78.begun = f32[16,8448]{1,0:T(8,128)S(1)} custom-call(bf16[90,16,128]{2,1,0:T(8,128)(2,1)S(1)} %collective-permute-done.4.plus, bf16[90,16,128]{2,1,0:T(8,128)(2,1)S(1)} %collective-permute-done.5.minus, f32[16,8448]{1,0:T(8,128)S(1)} %shard_map.77.begun), custom_call_target="tpu_custom_call" | custom-call | flops 8000000 | bytes 24000000 | tf_op jit(solution)/shard_map/pallas_call | solution.py:587
  56.4 0.0 collective-permute-done.3.cross
  56.4 0.0 all-to-all-done.above
  56.4 2.6 %shard_map.79 = f32[4,4,8192]{2,1,0:T(4,128)} custom-call(s32[1]{0:T(128)} %bitcast.lev, f32[4]{0:T(128)} %geo_in.1, bf16[45,16,128]{2,1,0:T(8,128)(2,1)S(1)} %collective-permute-done.3.cross, f32[16,8448]{1,0:T(8,128)S(1)} %shard_map.78.begun, f32[8,4096]{1,0:T(8,128)S(1)} %get-tuple-element.31.local, bf16[8,64,128]{2,1,0:T(8,128)(2,1)S(1)} %all-to-all-done.above), custom_call_target="tpu_custom_call" | custom-call | flops 4000000 | bytes 12000000 | tf_op jit(solution)/shard_map/pallas_call | solution.py:598
Async XLA Ops:
  1.0 8.1 %collective-permute-start.1 = (bf16[32,16,128]{2,1,0:T(8,128)(2,1)S(1)}, bf16[32,16,128]{2,1,0:T(8,128)(2,1)S(1)}, u32[]{:S(2)}, u32[]{:S(2)}) collective-permute-start(bf16[32,16,128]{2,1,0:T(8,128)(2,1)S(1)} %shard_map.74.own), channel_id=1, source_target_pairs={{16,0},{24,8},{32,16},{40,24},{48,32},{56,40},{64,48},{72,56},{80,... | collective-permute-start | bytes 393224 | tf_op jit(solution)/shard_map/ppermute | solution.py:467
  3.2 6.0 %collective-permute-start = (bf16[32,16,128]{2,1,0:T(8,128)(2,1)S(1)}, bf16[32,16,128]{2,1,0:T(8,128)(2,1)S(1)}, u32[]{:S(2)}, u32[]{:S(2)}) collective-permute-start(bf16[32,16,128]{2,1,0:T(8,128)(2,1)S(1)} %shard_map.74.own), channel_id=1, source_target_pairs={{0,16},{8,24},{16,32},{24,40},{32,48},{40,56},{48,64},{56,72},{64,... | collective-permute-start | bytes 393224 | tf_op jit(solution)/shard_map/ppermute | solution.py:467
  9.5 5.9 %collective-permute-start.2 = (bf16[236,16,128]{2,1,0:T(8,128)(2,1)S(1)}, bf16[236,16,128]{2,1,0:T(8,128)(2,1)S(1)}, u32[]{:S(2)}, u32[]{:S(2)}) collective-permute-start(bf16[236,16,128]{2,1,0:T(8,128)(2,1)S(1)} %shard_map.75), channel_id=1, source_target_pairs={{0,8},{8,0},{16,24},{24,16},{32,40},{40,32},{48,56},{56,48},{64,72... | collective-permute-start | bytes 2899976 | tf_op jit(solution)/shard_map/ppermute | solution.py:471
  20.6 31.8 %collective-permute-start.4 = (bf16[90,16,128]{2,1,0:T(8,128)(2,1)S(1)}, bf16[90,16,128]{2,1,0:T(8,128)(2,1)S(1)}, u32[]{:S(2)}, u32[]{:S(2)}) collective-permute-start(bf16[90,16,128]{2,1,0:T(8,128)(2,1)S(1)} %get-tuple-element.25), channel_id=1, source_target_pairs={{0,16},{8,24},{16,32},{24,40},{32,48},{40,56},{48,64},{56,72},{64,... | collective-permute-start | bytes 1105928 | tf_op jit(solution)/shard_map/ppermute | solution.py:467
  26.2 26.3 %collective-permute-start.5 = (bf16[90,16,128]{2,1,0:T(8,128)(2,1)S(1)}, bf16[90,16,128]{2,1,0:T(8,128)(2,1)S(1)}, u32[]{:S(2)}, u32[]{:S(2)}) collective-permute-start(bf16[90,16,128]{2,1,0:T(8,128)(2,1)S(1)} %get-tuple-element.26), channel_id=1, source_target_pairs={{16,0},{24,8},{32,16},{40,24},{48,32},{56,40},{64,48},{72,56},{80,... | collective-permute-start | bytes 1105928 | tf_op jit(solution)/shard_map/ppermute | solution.py:467
  28.1 28.3 %all-to-all-start = ((bf16[8,64,128]{2,1,0:T(8,128)(2,1)}), bf16[8,64,128]{2,1,0:T(8,128)(2,1)S(1)}, u32[]{:S(2)}, u32[]{:S(2)}) async-start(bf16[8,64,128]{2,1,0:T(8,128)(2,1)} %get-tuple-element.32), calls=%async_computation | async-start | bytes 262144 | tf_op jit(solution)/shard_map/all_to_all | solution.py:574
  35.1 21.3 %collective-permute-start.3 = (bf16[45,16,128]{2,1,0:T(8,128)(2,1)S(1)}, bf16[45,16,128]{2,1,0:T(8,128)(2,1)S(1)}, u32[]{:S(2)}, u32[]{:S(2)}) collective-permute-start(bf16[45,16,128]{2,1,0:T(8,128)(2,1)S(1)} %get-tuple-element.24), channel_id=1, source_target_pairs={{8,32},{24,48},{32,8},{40,64},{48,24},{56,80},{64,40},{72,96},{80,... | collective-permute-start | bytes 552968 | tf_op jit(solution)/shard_map/ppermute | solution.py:477
